TPU v7x, 128 devices: a whole 4x4x4 slice. The times are simulated.
128 devices in a mesh: author: 8 (over x, core), word: 16 (over y, z).
Axes of the slice: x: 4, y: 4, z: 4, core: 2. Of those that a mesh axis runs over, the one named last changes fastest.
Arguments:
- block_values: bfloat16 [8, 16, 128, 128, 128], P('author', 'word'), as said below
- block_rows: int32 [8, 16, 128], P('author', 'word'), may hold values from 0 to 31, as said below
- block_cols: int32 [8, 16, 128], P('author', 'word'), may hold values from 0 to 127
- block_count: int32 [8, 16], P('author', 'word'), may hold values from 32 to 128, as said below
- omega: bfloat16 [262144, 256], P('word'), may hold values from -6 to 6
Outputs:
- author_basis: bfloat16 [32768, 256], P(('author', 'word'))
- word_basis: bfloat16 [262144, 256], P(('word', 'author'))
Inputs may be any that keep to these rules, and one draw needn't show every extreme that they name: `block_values`: entries of slots at or past a device's count are finite and unused. `block_rows`: the 128 slots of one device name distinct (row block, column block) pairs. `block_count`: some device holds exactly 128 live blocks and some other device exactly a quarter of 128.
All inputs are finite; a program needn't handle non-finite values.
Results may differ from a plain program's by a relative error of at most 0.029.
Values may be sent and summed in bfloat16 or wider, within the bound.
No kernel may reach another device: no remote copies, remote signals or barrier semaphores. Data moves between devices by JAX's collectives and lax.ppermute only.
A program may use at most 192 MiB of HBM per device.

v0:
```python
import jax
import jax.numpy as jnp
from jax import lax
from jax.sharding import PartitionSpec as P

ABD = 2
ITERS = 2


def product(values, rows, cols, count, panel, out_blocks, transpose):
    cap = values.shape[0]
    size = values.shape[1]
    width = panel.shape[1]
    group = min(64, cap)
    blocks = panel.reshape(-1, size, width)

    def step(index, total):
        start = index * group
        part_values = lax.dynamic_slice_in_dim(values, start, group, 0)
        row_ids = lax.dynamic_slice_in_dim(rows, start, group, 0)
        col_ids = lax.dynamic_slice_in_dim(cols, start, group, 0)
        live = (start + jnp.arange(group, dtype=jnp.int32) < count).astype(jnp.float32)
        if transpose:
            source = jnp.take(blocks, row_ids, axis=0)
            target = col_ids
            prod = jnp.einsum(
                "kji,kjn->kin", part_values, source, preferred_element_type=jnp.float32
            )
        else:
            source = jnp.take(blocks, col_ids, axis=0)
            target = row_ids
            prod = jnp.einsum(
                "kij,kjn->kin", part_values, source, preferred_element_type=jnp.float32
            )
        return total.at[target].add(prod * live[:, None, None])

    limit = cap // group
    total = lax.fori_loop(0, limit, step, jnp.zeros((out_blocks, size, width), jnp.float32))
    return total.reshape(out_blocks * size, width)


def gram_of(field):
    return lax.dot_general(
        field,
        field,
        (((0,), (0,)), ((), ())),
        precision=lax.Precision.HIGHEST,
        preferred_element_type=jnp.float32,
    )


def orthonormal(field, gram, total):
    lower = jnp.linalg.cholesky(gram / total)
    inverse = jax.scipy.linalg.solve_triangular(
        lower, jnp.eye(gram.shape[0], dtype=jnp.float32), lower=True
    )
    return jnp.dot(
        field, inverse.T, precision=lax.Precision.HIGHEST, preferred_element_type=jnp.float32
    ).astype(jnp.bfloat16)


def word_panel_shares(word_terms, words):
    word_share = lax.psum_scatter(
        word_terms.astype(jnp.bfloat16), "author", scatter_dimension=0, tiled=True
    ).astype(jnp.float32)
    gram = lax.psum(gram_of(word_share), ("author", "word"))
    return orthonormal(word_share, gram, words)


def shards(block_values, block_rows, block_cols, block_count, omega):
    values = block_values[0, 0]
    rows = block_rows[0, 0]
    cols = block_cols[0, 0]
    count = block_count[0, 0]
    n_author = lax.axis_size("author")
    n_word = lax.axis_size("word")
    size = values.shape[1]
    author_blocks = ABD * n_word
    word_blocks = omega.shape[0] // size
    authors = author_blocks * size * n_author
    words = word_blocks * size * n_word
    panel = omega
    author_basis = None
    for turn in range(ITERS):
        if turn == 0:
            wide = panel
        else:
            wide = lax.all_gather(panel, "author", axis=0, tiled=True)
        author_terms = product(values, rows, cols, count, wide, author_blocks, False)
        author_share = lax.psum_scatter(
            author_terms.astype(jnp.bfloat16), "word", scatter_dimension=0, tiled=True
        ).astype(jnp.float32)
        gram = lax.psum(gram_of(author_share), ("author", "word"))
        author_basis = orthonormal(author_share, gram, authors)
        basis_rows = lax.all_gather(author_basis, "word", axis=0, tiled=True)
        word_terms = product(values, rows, cols, count, basis_rows, word_blocks, True)
        if turn + 1 == ITERS:
            panel = word_panel_shares(word_terms, words)
        else:
            panel = word_panel_shares(word_terms, words)
    return (author_basis, panel)


def solution(mesh):
    return jax.shard_map(
        shards,
        mesh=mesh,
        in_specs=(
            P("author", "word", None, None, None),
            P("author", "word", None),
            P("author", "word", None),
            P("author", "word"),
            P("word", None),
        ),
        out_specs=(P(("author", "word"), None), P(("word", "author"), None)),
        check_vma=False,
    )
```

profile of v0, /device:TPU:1, one launch (start us, length us, event | category | flops | bytes accessed | tf_op | source)
XLA Modules:
  0.0 1553.3 jit_solution(3369241538758465274)
XLA Ops:
  9.7 66.9 %while.60 = (s32[]{:T(128)}, f32[32,128,256]{2,1,0:T(8,128)}, s32[128]{0:T(128)S(1)}, bf16[128,128,128]{2,1,0:T(8,128)(2,1)}, s32[128]{0:T(128)S(1)}, /*index=5*...) while((s32[]{:T(128)}, f32[32,128,256]{2,1,0:T(8,128)}, ...), condition=%wide.region_2.0_spmd, body=%wide.region_0.3_spmd.sunk | while | flops 543164160 | bytes 48241200 | solution.py:38
  24.0 19.4 %scatter_fusion = f32[32,128,256]{2,1,0:T(8,128)} fusion(f32[32,128,256]{2,1,0:T(8,128)} %get-tuple-element.1008, s32[64]{0:T(128)S(1)} %compare_select_fusion.16, f32[64,128,256]{2,1,0:T(8,128)} %broadcast_multiply_fusion.12), kind=kCustom, calls=%fused_computation.4.clone.1 | custom fusion | flops 2097152 | bytes 25166080 | tf_op jit(solution)/shard_map/while/body/eval_jaxpr/scatter-add | solution.py:35
  57.8 18.8 %scatter_fusion = f32[32,128,256]{2,1,0:T(8,128)} fusion(f32[32,128,256]{2,1,0:T(8,128)} %get-tuple-element.1008, s32[64]{0:T(128)S(1)} %compare_select_fusion.16, f32[64,128,256]{2,1,0:T(8,128)} %broadcast_multiply_fusion.12), kind=kCustom, calls=%fused_computation.4.clone.1 | custom fusion | flops 2097152 | bytes 25166080 | tf_op jit(solution)/shard_map/while/body/eval_jaxpr/scatter-add | solution.py:35
  80.5 76.7 %reduce-scatter.5.cloned.1.call-done = bf16[256,256]{1,0:T(8,128)(2,1)} async-done(((bf16[4096,256]{1,0:T(8,128)(2,1)}), bf16[256,256]{1,0:T(8,128)(2,1)}) %reduce-scatter.5.cloned.1.call-update) | async-done | bytes 131088 | tf_op jit(solution)/shard_map/reduce_scatter | solution.py:90
  159.8 145.8 %all-reduce.6.cloned.1.call-done = f32[256,256]{0,1:T(8,128)} async-done(((f32[256,256]{0,1:T(8,128)}), f32[256,256]{0,1:T(8,128)}) %all-reduce.6.cloned.1.call-update) | async-done | bytes 262160 | tf_op jit(solution)/shard_map/psum | solution.py:93
  307.8 11.7 cholesky.214
  329.8 11.7 cholesky.231
  348.1 19.7 %custom-call.18 = f32[2,128,128]{1,2,0:T(8,128)S(1)} custom-call(f32[2,128,128]{2,1,0:T(8,128)S(1)} %get-tuple-element.532), custom_call_target="InvertDiagBlocksLowerTriangular" | custom-call | tf_op jit(solution)/shard_map/jit(_solve_triangular)/triangular_solve | solution.py:54
  376.1 35.4 %all-gather.4.cloned.1.call-done = bf16[4096,256]{1,0:T(8,128)(2,1)} async-done(((bf16[256,256]{1,0:T(8,128)(2,1)}), bf16[4096,256]{1,0:T(8,128)(2,1)}) %all-gather.4.cloned.1.call-update) | async-done | bytes 2097168 | tf_op jit(solution)/shard_map/all_gather | solution.py:95
  419.3 61.2 %while.61 = (s32[]{:T(128)}, f32[128,128,256]{2,1,0:T(8,128)}, s32[128]{0:T(128)S(1)}, bf16[128,128,128]{1,2,0:T(8,128)(2,1)}, s32[128]{0:T(128)S(1)}, /*index=5...) while((s32[]{:T(128)}, f32[128,128,256]{2,1,0:T(8,128)}, ...), condition=%wide.region_11.16_spmd, body=%wide.region_9.0_spmd.sunk | while | flops 543164160 | bytes 48241200 | solution.py:38
  430.2 19.5 %scatter_fusion.1 = f32[128,128,256]{2,1,0:T(8,128)} fusion(f32[128,128,256]{2,1,0:T(8,128)} %get-tuple-element.1056, s32[64]{0:T(128)S(1)} %compare_select_fusion.17, f32[64,128,256]{2,1,0:T(8,128)} %broadcast_multiply_fusion.13), kind=kCustom, calls=%fused_computation.5.clone.1 | custom fusion | flops 2097152 | bytes 25166080 | tf_op jit(solution)/shard_map/while/body/eval_jaxpr/scatter-add | solution.py:35
  460.7 19.8 %scatter_fusion.1 = f32[128,128,256]{2,1,0:T(8,128)} fusion(f32[128,128,256]{2,1,0:T(8,128)} %get-tuple-element.1056, s32[64]{0:T(128)S(1)} %compare_select_fusion.17, f32[64,128,256]{2,1,0:T(8,128)} %broadcast_multiply_fusion.13), kind=kCustom, calls=%fused_computation.5.clone.1 | custom fusion | flops 2097152 | bytes 25166080 | tf_op jit(solution)/shard_map/while/body/eval_jaxpr/scatter-add | solution.py:35
  489.6 52.3 %reduce-scatter.7.cloned.1.call-done = bf16[2048,256]{1,0:T(8,128)(2,1)} async-done(((bf16[16384,256]{1,0:T(8,128)(2,1)}), bf16[2048,256]{1,0:T(8,128)(2,1)}) %reduce-scatter.7.cloned.1.call-update) | async-done | bytes 1048592 | tf_op jit(solution)/shard_map/reduce_scatter | solution.py:63
  545.0 144.5 %all-reduce.8.cloned.1.call-done = f32[256,256]{0,1:T(8,128)} async-done(((f32[256,256]{0,1:T(8,128)}), f32[256,256]{0,1:T(8,128)}) %all-reduce.8.cloned.1.call-update) | async-done | bytes 262160 | tf_op jit(solution)/shard_map/psum | solution.py:66
  713.7 11.7 cholesky.265
  732.6 19.7 %custom-call.20 = f32[2,128,128]{1,2,0:T(8,128)S(1)} custom-call(f32[2,128,128]{2,1,0:T(8,128)S(1)} %get-tuple-element.533), custom_call_target="InvertDiagBlocksLowerTriangular" | custom-call | tf_op jit(solution)/shard_map/jit(_solve_triangular)/triangular_solve | solution.py:54
  755.3 47.6 %all-gather.6.cloned.1.call-done = bf16[16384,256]{1,0:T(8,128)(2,1)} async-done(((bf16[2048,256]{1,0:T(8,128)(2,1)}), bf16[16384,256]{1,0:T(8,128)(2,1)}) %all-gather.6.cloned.1.call-update) | async-done | bytes 8388624 | tf_op jit(solution)/shard_map/all_gather | solution.py:88
  805.4 66.7 %while.62 = (s32[]{:T(128)}, f32[32,128,256]{2,1,0:T(8,128)}, s32[128]{0:T(128)S(1)}, bf16[128,128,128]{2,1,0:T(8,128)(2,1)}, s32[128]{0:T(128)S(1)}, /*index=5*...) while((s32[]{:T(128)}, f32[32,128,256]{2,1,0:T(8,128)}, ...), condition=%wide.region_16.21_spmd, body=%wide.region_14.0_spmd.sunk | while | flops 543164160 | bytes 48241200 | solution.py:38
  819.6 19.3 %scatter_fusion.2 = f32[32,128,256]{2,1,0:T(8,128)} fusion(f32[32,128,256]{2,1,0:T(8,128)} %get-tuple-element.1104, s32[64]{0:T(128)S(1)} %compare_select_fusion.18, f32[64,128,256]{2,1,0:T(8,128)} %broadcast_multiply_fusion.14), kind=kCustom, calls=%fused_computation.6.clone.1 | custom fusion | flops 2097152 | bytes 25166080 | tf_op jit(solution)/shard_map/while/body/eval_jaxpr/scatter-add | solution.py:35
  853.2 18.8 %scatter_fusion.2 = f32[32,128,256]{2,1,0:T(8,128)} fusion(f32[32,128,256]{2,1,0:T(8,128)} %get-tuple-element.1104, s32[64]{0:T(128)S(1)} %compare_select_fusion.18, f32[64,128,256]{2,1,0:T(8,128)} %broadcast_multiply_fusion.14), kind=kCustom, calls=%fused_computation.6.clone.1 | custom fusion | flops 2097152 | bytes 25166080 | tf_op jit(solution)/shard_map/while/body/eval_jaxpr/scatter-add | solution.py:35
  875.9 73.0 %reduce-scatter.9.cloned.1.call-done = bf16[256,256]{1,0:T(8,128)(2,1)} async-done(((bf16[4096,256]{1,0:T(8,128)(2,1)}), bf16[256,256]{1,0:T(8,128)(2,1)}) %reduce-scatter.9.cloned.1.call-update) | async-done | bytes 131088 | tf_op jit(solution)/shard_map/reduce_scatter | solution.py:90
  951.2 145.4 %all-reduce.10.cloned.1.call-done = f32[256,256]{0,1:T(8,128)} async-done(((f32[256,256]{0,1:T(8,128)}), f32[256,256]{0,1:T(8,128)}) %all-reduce.10.cloned.1.call-update) | async-done | bytes 262160 | tf_op jit(solution)/shard_map/psum | solution.py:93
  1120.8 11.7 cholesky.299
  1139.6 19.7 %custom-call.22 = f32[2,128,128]{1,2,0:T(8,128)S(1)} custom-call(f32[2,128,128]{2,1,0:T(8,128)S(1)} %get-tuple-element.534), custom_call_target="InvertDiagBlocksLowerTriangular" | custom-call | tf_op jit(solution)/shard_map/jit(_solve_triangular)/triangular_solve | solution.py:54
  1161.3 41.8 %all-gather.8.cloned.1.call-done = bf16[4096,256]{1,0:T(8,128)(2,1)} async-done(((bf16[256,256]{1,0:T(8,128)(2,1)}), bf16[4096,256]{1,0:T(8,128)(2,1)}) %all-gather.8.cloned.1.call-update) | async-done | bytes 2097168 | tf_op jit(solution)/shard_map/all_gather | solution.py:95
  1210.9 61.2 %while.63 = (s32[]{:T(128)}, f32[128,128,256]{2,1,0:T(8,128)}, s32[128]{0:T(128)S(1)}, bf16[128,128,128]{1,2,0:T(8,128)(2,1)}, s32[128]{0:T(128)S(1)}, /*index=5...) while((s32[]{:T(128)}, f32[128,128,256]{2,1,0:T(8,128)}, ...), condition=%wide.region_21.26_spmd, body=%wide.region_19.0_spmd.sunk | while | flops 543164160 | bytes 48241200 | solution.py:38
  1221.8 19.5 %scatter_fusion.3 = f32[128,128,256]{2,1,0:T(8,128)} fusion(f32[128,128,256]{2,1,0:T(8,128)} %get-tuple-element.1152, s32[64]{0:T(128)S(1)} %compare_select_fusion.19, f32[64,128,256]{2,1,0:T(8,128)} %broadcast_multiply_fusion.15), kind=kCustom, calls=%fused_computation.7.clone.1 | custom fusion | flops 2097152 | bytes 25166080 | tf_op jit(solution)/shard_map/while/body/eval_jaxpr/scatter-add | solution.py:35
  1252.3 19.8 %scatter_fusion.3 = f32[128,128,256]{2,1,0:T(8,128)} fusion(f32[128,128,256]{2,1,0:T(8,128)} %get-tuple-element.1152, s32[64]{0:T(128)S(1)} %compare_select_fusion.19, f32[64,128,256]{2,1,0:T(8,128)} %broadcast_multiply_fusion.15), kind=kCustom, calls=%fused_computation.7.clone.1 | custom fusion | flops 2097152 | bytes 25166080 | tf_op jit(solution)/shard_map/while/body/eval_jaxpr/scatter-add | solution.py:35
  1281.4 52.0 %reduce-scatter.11.cloned.1.call-done = bf16[2048,256]{1,0:T(8,128)(2,1)} async-done(((bf16[16384,256]{1,0:T(8,128)(2,1)}), bf16[2048,256]{1,0:T(8,128)(2,1)}) %reduce-scatter.11.cloned.1.call-update) | async-done | bytes 1048592 | tf_op jit(solution)/shard_map/reduce_scatter | solution.py:63
  1336.3 144.2 %all-reduce.12.cloned.1.call-done = f32[256,256]{0,1:T(8,128)} async-done(((f32[256,256]{0,1:T(8,128)}), f32[256,256]{0,1:T(8,128)}) %all-reduce.12.cloned.1.call-update) | async-done | bytes 262160 | tf_op jit(solution)/shard_map/psum | solution.py:66
  1504.7 11.7 cholesky.333
  1523.6 19.7 %custom-call.24 = f32[2,128,128]{1,2,0:T(8,128)S(1)} custom-call(f32[2,128,128]{2,1,0:T(8,128)S(1)} %get-tuple-element.535), custom_call_target="InvertDiagBlocksLowerTriangular" | custom-call | tf_op jit(solution)/shard_map/jit(_solve_triangular)/triangular_solve | solution.py:54
  (196 shorter events, 298.2 us)
Async XLA Ops:
  7.2 2.5 copy-start.6
  7.2 2.5 copy-start.7
  7.2 150.0 %reduce-scatter.5.cloned.1.call-start = ((), (), s32[]{:S(2)}) async-start(), calls=%async_computation.4 | async-start | bytes 2228224 | tf_op jit(solution)/shard_map/reduce_scatter | solution.py:90
  80.5 225.2 %all-reduce.6.cloned.1.call-start = ((), (), s32[]{:S(2)}) async-start(), calls=%async_computation.5 | async-start | bytes 524288 | tf_op jit(solution)/shard_map/psum | solution.py:93
  157.2 211.4 %copy-start.2 = (bf16[256,256]{1,0:T(8,128)(2,1)S(1)}, bf16[256,256]{1,0:T(8,128)(2,1)}, u32[]{:S(2)}) copy-start(bf16[256,256]{1,0:T(8,128)(2,1)} %reduce-scatter.5.cloned.1.call-done) | copy-start | bytes 393220
  159.2 252.2 %all-gather.4.cloned.1.call-start = ((), (), s32[]{:S(2)}) async-start(), calls=%async_computation.6 | async-start | bytes 2228224 | tf_op jit(solution)/shard_map/all_gather | solution.py:95
  369.7 172.2 %reduce-scatter.7.cloned.1.call-start = ((), (), s32[]{:S(2)}) async-start(), calls=%async_computation.7 | async-start | bytes 9437184 | tf_op jit(solution)/shard_map/reduce_scatter | solution.py:63
  411.5 7.8 copy-start.1
  489.5 200.0 %all-reduce.8.cloned.1.call-start = ((), (), s32[]{:S(2)}) async-start(), calls=%async_computation.8 | async-start | bytes 524288 | tf_op jit(solution)/shard_map/psum | solution.py:66
  541.8 211.4 %copy-start.5 = (bf16[2048,256]{1,0:T(8,128)(2,1)S(1)}, bf16[2048,256]{1,0:T(8,128)(2,1)}, u32[]{:S(2)}) copy-start(bf16[2048,256]{1,0:T(8,128)(2,1)} %reduce-scatter.7.cloned.1.call-done) | copy-start | bytes 3145732
  544.7 258.2 %all-gather.6.cloned.1.call-start = ((), (), s32[]{:S(2)}) async-start(), calls=%async_computation.9 | async-start | bytes 9437184 | tf_op jit(solution)/shard_map/all_gather | solution.py:88
  755.2 193.7 %reduce-scatter.9.cloned.1.call-start = ((), (), s32[]{:S(2)}) async-start(), calls=%async_computation.10 | async-start | bytes 2228224 | tf_op jit(solution)/shard_map/reduce_scatter | solution.py:90
  875.9 220.8 %all-reduce.10.cloned.1.call-start = ((), (), s32[]{:S(2)}) async-start(), calls=%async_computation.11 | async-start | bytes 524288 | tf_op jit(solution)/shard_map/psum | solution.py:93
  949.0 211.3 %copy-start.3 = (bf16[256,256]{1,0:T(8,128)(2,1)S(1)}, bf16[256,256]{1,0:T(8,128)(2,1)}, u32[]{:S(2)}) copy-start(bf16[256,256]{1,0:T(8,128)(2,1)} %reduce-scatter.9.cloned.1.call-done) | copy-start | bytes 393220
  951.0 252.1 %all-gather.8.cloned.1.call-start = ((), (), s32[]{:S(2)}) async-start(), calls=%async_computation.12 | async-start | bytes 2228224 | tf_op jit(solution)/shard_map/all_gather | solution.py:95
  1161.3 172.2 %reduce-scatter.11.cloned.1.call-start = ((), (), s32[]{:S(2)}) async-start(), calls=%async_computation.13 | async-start | bytes 9437184 | tf_op jit(solution)/shard_map/reduce_scatter | solution.py:63
  1203.1 7.8 copy-start
  1281.1 199.5 %all-reduce.12.cloned.1.call-start = ((), (), s32[]{:S(2)}) async-start(), calls=%async_computation.14 | async-start | bytes 524288 | tf_op jit(solution)/shard_map/psum | solution.py:66
  1333.4 210.8 %copy-start.4 = (bf16[2048,256]{1,0:T(8,128)(2,1)S(1)}, bf16[2048,256]{1,0:T(8,128)(2,1)}, u32[]{:S(2)}) copy-start(bf16[2048,256]{1,0:T(8,128)(2,1)} %reduce-scatter.11.cloned.1.call-done) | copy-start | bytes 3145732
Sparse Core Ops, SparseCore 0:
  80.6 76.5 reduce-scatter.4
  163.3 142.3 all-reduce.5
  369.8 41.6 all-gather.3
  489.6 52.1 reduce-scatter.6
  547.7 141.7 all-reduce.7
  755.4 47.5 all-gather.5
  876.0 72.9 reduce-scatter.8
  954.3 142.3 all-reduce.9
  1161.4 41.6 all-gather.7
  1281.2 52.1 reduce-scatter.10
  1338.8 141.7 all-reduce.11
where the time goes:
time: 1560 us; the launch traced here: 1550 us
  waiting for transfers between devices  959 us (61%)
  other arithmetic  412 us (26%)
  matrix products  80 us (5%)
  local copies, waits for them, and re-layouts  79.5 us (5%)
  between operations  20.2 us (1%)
    psum x2, waiting for transfers between devices, shards(): gram = lax.psum(gram_of(author_share), ('author', 'word'))  291 us
    psum x2, waiting for transfers between devices, word_panel_shares(): gram = lax.psum(gram_of(word_share), ('author', 'word'))  289 us
    scatter-add x8, other arithmetic, step(): return total.at[target].add(prod * live[:, None, None])  155 us
    reduce_scatter x2, waiting for transfers between devices, shards(): lax.psum_scatter(author_terms.astype(jnp.bfloat16), 'word', scatter_dimen...  150 us
    another operation x27, other arithmetic, orthonormal(): lower = jnp.linalg.cholesky(gram / total)  138 us
    reduce_scatter x2, waiting for transfers between devices, word_panel_shares(): lax.psum_scatter(word_terms.astype(jnp.bfloat16), 'author', scatter_dimen...  104 us
    another operation x9, other arithmetic, orthonormal(): jax.scipy.linalg.solve_triangular(lower, jnp.eye(gram.shape[0], dtype=jnp...  78.8 us
    all_gather x2, waiting for transfers between devices, shards(): basis_rows = lax.all_gather(author_basis, 'word', axis=0, tiled=True)  77.2 us
  transfers between devices with their start and end apart: 11, of which 11 were waited for; matrix products, arithmetic and copies ran while one was open for 0% of the time, Pallas kernels for 0%

commit v1 on v0

v1 whole, which is shorter than its diff:
```python
import functools
import jax
import jax.numpy as jnp
from jax import lax
from jax.experimental import pallas as pl
from jax.experimental.pallas import tpu as pltpu
from jax.sharding import PartitionSpec as P

ITERS = 2
GROUP = 4
SLOTS = 16
HIGH = lax.Precision.HIGHEST


def product_kernel(src_ids, dst_ids, count, values, panel, out, total, *, transpose):
    step = pl.program_id(0)
    size = values.shape[1]
    blocks = out.shape[0] // size

    @pl.when(step == 0)
    def _():
        def clear(index, carry):
            total[index] = jnp.zeros_like(total[index])
            return carry

        lax.fori_loop(0, blocks, clear, 0)

    def group(index, carry):
        base = step * SLOTS + index * GROUP
        prods = []
        for offset in range(GROUP):
            part = values[index * GROUP + offset]
            source = panel[pl.ds(pl.multiple_of(src_ids[base + offset] * size, size), size), :]
            dims = (((0,), (0,)), ((), ())) if transpose else (((1,), (0,)), ((), ()))
            prods.append(lax.dot_general(part, source, dims, preferred_element_type=jnp.float32))
        for offset in range(GROUP):
            total[dst_ids[base + offset]] += prods[offset]
        return carry

    live = jnp.clip(count[0] - step * SLOTS, 0, SLOTS)
    lax.fori_loop(0, (live + GROUP - 1) // GROUP, group, 0)

    @pl.when(step == pl.num_programs(0) - 1)
    def _():
        def emit(index, carry):
            out[pl.ds(pl.multiple_of(index * size, size), size), :] = total[index].astype(out.dtype)
            return carry

        lax.fori_loop(0, blocks, emit, 0)


def product(values, src_ids, dst_ids, count, panel, out_blocks, transpose):
    cap, size, _ = values.shape
    width = panel.shape[1]
    dst_ids = jnp.where(jnp.arange(cap, dtype=jnp.int32) < count, dst_ids, out_blocks)
    return pl.pallas_call(
        functools.partial(product_kernel, transpose=transpose),
        out_shape=jax.ShapeDtypeStruct((out_blocks * size, width), jnp.bfloat16),
        grid_spec=pltpu.PrefetchScalarGridSpec(
            num_scalar_prefetch=3,
            grid=(cap // SLOTS,),
            in_specs=[
                pl.BlockSpec((SLOTS, size, size), lambda i, *_: (i, 0, 0)),
                pl.BlockSpec(panel.shape, lambda i, *_: (0, 0), pipeline_mode=pl.Buffered(1)),
            ],
            out_specs=pl.BlockSpec((out_blocks * size, width), lambda i, *_: (0, 0), pipeline_mode=pl.Buffered(1)),
            scratch_shapes=[pltpu.VMEM((out_blocks + 1, size, width), jnp.float32)],
        ),
        compiler_params=pltpu.CompilerParams(vmem_limit_bytes=52 * 1024 * 1024),
        cost_estimate=pl.CostEstimate(
            flops=2 * cap * size * size * width,
            bytes_accessed=2 * (cap * size * size + panel.size + out_blocks * size * width),
            transcendentals=0,
        ),
        name="product_t" if transpose else "product",
    )(src_ids, dst_ids, count.reshape(1), values, panel)


def gram_of(field):
    return lax.dot_general(
        field, field, (((0,), (0,)), ((), ())), precision=HIGH, preferred_element_type=jnp.float32
    )


def hop_core(array):
    return lax.ppermute(array, "author", [(i, i ^ 1) for i in range(8)])


def hop_x(array, k):
    return lax.ppermute(array, "author", [(i, (i + 2 * k) % 8) for i in range(8)])


def hop_y(array, k):
    return lax.ppermute(array, "word", [(i, (i + 4 * k) % 16) for i in range(16)])


def hop_z(array, k):
    return lax.ppermute(array, "word", [(i, (i // 4) * 4 + (i + k) % 4) for i in range(16)])


def pick(array, index):
    return lax.dynamic_index_in_dim(array, index, 0, keepdims=False)


def split_core(gram, core):
    halves = gram.reshape(2, gram.shape[0] // 2, gram.shape[1])
    return pick(halves, core) + hop_core(pick(halves, 1 - core))


def join_core(half, core):
    other = hop_core(half)
    return jnp.where(core == 0, jnp.concatenate([half, other]), jnp.concatenate([other, half]))


def sum_author(gram):
    core = lax.axis_index("author") % 2
    half = split_core(gram, core)
    parts = [hop_x(half, k) for k in (1, 3, 2)]
    half = (half + parts[2]) + (parts[0] + parts[1])
    return join_core(half, core)


def sum_all(gram):
    place = lax.axis_index("author")
    core, x = place % 2, place // 2
    half = split_core(gram, core)
    chunks = half.reshape(4, half.shape[0] // 4, half.shape[1])
    got = [hop_x(pick(chunks, (x + k) % 4), k) for k in (1, 3, 2)]
    part = (pick(chunks, x) + got[2]) + (got[0] + got[1])
    for hop in (hop_y, hop_z):
        got = [hop(part, k) for k in (1, 3, 2)]
        part = (part + got[2]) + (got[0] + got[1])
    ring = jnp.stack([part] + [hop_x(part, k) for k in (1, 2, 3)])
    half = jnp.take(ring, (x - jnp.arange(4)) % 4, axis=0).reshape(half.shape)
    return join_core(half, core)


def whitener(gram):
    lower = jnp.linalg.cholesky(gram)
    inverse = jax.scipy.linalg.solve_triangular(
        lower, jnp.eye(gram.shape[0], dtype=jnp.float32), lower=True
    )
    return inverse.T


def apply(field, factor):
    return jnp.dot(field, factor, precision=HIGH, preferred_element_type=jnp.float32)


def scatter_word(terms):
    parts = lax.all_to_all(terms.reshape(16, -1, terms.shape[1]), "word", 0, 0)
    return jnp.sum(parts.astype(jnp.float32), axis=0)


def gather_word(share):
    copies = jnp.broadcast_to(share[None], (16,) + share.shape)
    return lax.all_to_all(copies, "word", 0, 0).reshape(-1, share.shape[1])


def shards(block_values, block_rows, block_cols, block_count, omega):
    values = block_values[0, 0]
    rows = block_rows[0, 0]
    cols = block_cols[0, 0]
    count = block_count[0, 0]
    size = values.shape[1]
    word_blocks = omega.shape[0] // size
    author_blocks = 32
    authors = author_blocks * size * lax.axis_size("author")
    words = word_blocks * size * lax.axis_size("word")
    wide = omega
    word_factor = None
    for turn in range(ITERS):
        terms = product(values, cols, rows, count, wide, author_blocks, False)
        y = scatter_word(terms)
        if word_factor is not None:
            y = apply(y, word_factor)
        y_rows = gather_word(y.astype(jnp.bfloat16))
        author_factor = whitener(
            sum_author(lax.dot_general(y_rows, y_rows, (((0,), (0,)), ((), ())), preferred_element_type=jnp.float32))
            / authors
        )
        terms = product(values, rows, cols, count, y_rows, word_blocks, True)
        z = lax.psum_scatter(terms, "author", scatter_dimension=0, tiled=True).astype(jnp.float32)
        z = apply(z, author_factor)
        word_factor = whitener(sum_all(gram_of(z)) / words)
        if turn + 1 < ITERS:
            wide = lax.all_gather(z.astype(jnp.bfloat16), "author", axis=0, tiled=True)
    author_basis = apply(y, author_factor).astype(jnp.bfloat16)
    word_basis = apply(z, word_factor).astype(jnp.bfloat16)
    return (author_basis, word_basis)


def solution(mesh):
    return jax.shard_map(
        shards,
        mesh=mesh,
        in_specs=(
            P("author", "word", None, None, None),
            P("author", "word", None),
            P("author", "word", None),
            P("author", "word"),
            P("word", None),
        ),
        out_specs=(P(("author", "word"), None), P(("word", "author"), None)),
        check_vma=False,
    )
```

time: 1560 us -> 564 us (0.36)
  waiting for transfers between devices: 959 us -> 73.2 us
  other arithmetic: 412 us -> 219 us
  blocking collectives: 0 us -> 70.1 us
  starting transfers between devices: 1.61 us -> 71.3 us
  matrix products: 80 us -> 26.9 us
  Pallas kernels: 0 us -> 49 us
  local copies, waits for them, and re-layouts: 79.5 us -> 30.8 us
    psum x4 -> x0, waiting for transfers between devices: 580 us -> none  [the longest x2 291 us: shards(): gram = lax.psum(gram_of(author_share), ('author', 'word'))]
    reduce_scatter x4 -> x2, waiting for transfers between devices: 254 us -> 0.04 us  [shards(): lax.psum_scatter(terms, 'author', scatter_dimension=0, tiled=True)]
    scatter-add x8 -> x0, other arithmetic: 155 us -> none  [step(): return total.at[target].add(prod * live[:, None, None])]
    all_gather x3 -> x1, waiting for transfers between devices: 125 us -> 0.02 us  [shards(): wide = lax.all_gather(z.astype(jnp.bfloat16), 'author', axis=0, tiled=True)]
    all_to_all x0 -> x2, blocking collectives: none -> 70.1 us  [the longest x1 38.6 us: scatter_word(): parts = lax.all_to_all(terms.reshape(16, -1, terms.shape[1]), 'word', 0, 0)]
    ppermute x0 -> x38, starting transfers between devices: none -> 61.3 us  [the longest x8 24.7 us: hop_core(): return lax.ppermute(array, 'author', [(i, i ^ 1) for i in range(8)])]
    dot_general x16 -> x9, matrix products: 74.6 us -> 21.5 us  [the longest x5 9.81 us: apply(): jnp.dot(field, factor, precision=HIGH, preferred_element_type=jnp.float32)]
    pallas_call x0 -> x4, Pallas kernels: none -> 49 us  [product(): pl.pallas_call(functools.partial(product_kernel, transpose=transpose), ou...]
  transfers between devices with their start and end apart: 11 -> 43, of which waited for: 11 -> 30; matrix products, arithmetic and copies ran while one was open for 0% -> 35% of each run, Pallas kernels for 0% -> 0%
where the time goes in v1:
time: 564 us; the launch traced here: 561 us
  other arithmetic  219 us (39%)
  waiting for transfers between devices  73.2 us (13%)
  starting transfers between devices  71.3 us (13%)
  blocking collectives  70.1 us (12%)
  Pallas kernels  49 us (9%)
  local copies, waits for them, and re-layouts  30.8 us (5%)
  matrix products  26.9 us (5%)
  between operations  20.4 us (4%)
    another operation x27, other arithmetic, whitener(): lower = jnp.linalg.cholesky(gram)  138 us
    another operation x9, other arithmetic, whitener(): jax.scipy.linalg.solve_triangular(lower, jnp.eye(gram.shape[0], dtype=jnp...  78.8 us
    pallas_call x4, Pallas kernels, product(): pl.pallas_call(functools.partial(product_kernel, transpose=transpose), ou...  49 us
    all_to_all x1, blocking collectives, scatter_word(): parts = lax.all_to_all(terms.reshape(16, -1, terms.shape[1]), 'word', 0, 0)  38.6 us
    all_to_all x1, blocking collectives, gather_word(): return lax.all_to_all(copies, 'word', 0, 0).reshape(-1, share.shape[1])  31.5 us
    all_to_all x1, waiting for transfers between devices, gather_word(): return lax.all_to_all(copies, 'word', 0, 0).reshape(-1, share.shape[1])  29.2 us
    ppermute x18, waiting for transfers between devices, hop_x(): lax.ppermute(array, 'author', [(i, (i + 2 * k) % 8) for i in range(8)])  25.7 us
    ppermute x8, starting transfers between devices, hop_core(): return lax.ppermute(array, 'author', [(i, i ^ 1) for i in range(8)])  24.7 us
  transfers between devices with their start and end apart: 43, of which 30 were waited for; matrix products, arithmetic and copies ran while one was open for 35% of the time, Pallas kernels for 0%

profile of v1, /device:TPU:1, one launch (start us, length us, event | category | flops | bytes accessed | tf_op | source)
XLA Modules:
  0.0 561.0 jit_solution(9839964708015373013)
XLA Ops:
  9.1 11.2 %product.2 = bf16[4096,256]{1,0:T(8,128)(2,1)} custom-call(s32[128]{0:T(128)S(1)} %bitcast.212, s32[128]{0:T(128)S(1)} %compare_select_fusion.4.dst_ids, s32[1]{0:T(128)} %bitcast.208.count, bf16[128,128,128]{2,1,0:T(8,128)(2,1)} %bitcast.216, bf16[16384,256]{1,0:T(8,128)(2,1)} %panel.1), custom_call_target="tpu_custom_call" | custom-call | flops 1073741824 | bytes 14680064 | tf_op jit(solution)/shard_map/product/pallas_call | solution.py:56
  20.3 38.6 %all_to_all.20 = bf16[16,256,256]{2,1,0:T(8,128)(2,1)S(1)} all-to-all(bf16[16,256,256]{2,1,0:T(8,128)(2,1)} %bitcast.229), channel_id=1, replica_groups=mesh['author'=8,'word'=16] {'word'}, dimensions={0} | all-to-all | bytes 4194304 | tf_op jit(solution)/shard_map/all_to_all | solution.py:151
  64.7 29.2 %all-to-all-done.1 = bf16[16,256,256]{2,1,0:T(8,128)(2,1)S(1)} async-done(((bf16[16,256,256]{2,1,0:T(8,128)(2,1)}), bf16[16,256,256]{2,1,0:T(8,128)(2,1)S(1)}, u32[]{:S(2)}, u32[]{:S(2)}) %all-to-all-start.1) | async-done | bytes 2097184 | tf_op jit(solution)/shard_map/all_to_all | solution.py:157
  95.3 13.3 %product_t.2 = bf16[16384,256]{1,0:T(8,128)(2,1)} custom-call(s32[128]{0:T(128)S(1)} %bitcast.214, s32[128]{0:T(128)S(1)} %compare_select_fusion.3.dst_ids, s32[1]{0:T(128)} %bitcast.209.count, bf16[128,128,128]{2,1,0:T(8,128)(2,1)} %bitcast.217, bf16[4096,256]{1,0:T(8,128)(2,1)} %bitcast.220), custom_call_target="tpu_custom_call" | custom-call | flops 1073741824 | bytes 14680064 | tf_op jit(solution)/shard_map/product_t/pallas_call | solution.py:56
  123.0 4.5 collective-permute-done.1
  133.4 11.7 %cholesky.214 = f32[128,128]{1,0:T(8,128)S(1)} custom-call(f32[128,128]{1,0:T(8,128)S(1)} %cholesky.346), custom_call_target="Cholesky" | custom-call | tf_op jit(solution)/shard_map/jit(cholesky)/cholesky | solution.py:139
  145.2 9.8 %custom-call.17 = f32[1,128,128]{1,2,0:T(8,128)S(1)} custom-call(f32[1,128,128]{2,1,0:T(8,128)S(1)} %get-tuple-element.100), custom_call_target="InvertDiagBlocksLowerTriangular" | custom-call | tf_op jit(solution)/shard_map/jit(cholesky)/cholesky | solution.py:139
  155.5 11.7 %cholesky.231 = f32[128,128]{1,0:T(8,128)S(1)} custom-call(f32[128,128]{1,0:T(8,128)S(1)} %convolution_subtract_fusion.7), custom_call_target="Cholesky" | custom-call | tf_op jit(solution)/shard_map/jit(cholesky)/cholesky | solution.py:139
  173.2 19.7 %custom-call.18 = f32[2,128,128]{1,2,0:T(8,128)S(1)} custom-call(f32[2,128,128]{2,1,0:T(8,128)S(1)} %get-tuple-element.31), custom_call_target="InvertDiagBlocksLowerTriangular" | custom-call | tf_op jit(solution)/shard_map/jit(_solve_triangular)/triangular_solve | solution.py:140
  229.3 6.2 %collective-permute-start.18 = (f32[128,256]{0,1:T(8,128)S(1)}, f32[128,256]{0,1:T(8,128)S(1)}, u32[]{:S(2)}, u32[]{:S(2)}) collective-permute-start(f32[128,256]{0,1:T(8,128)S(1)} %copy.22), channel_id=1, source_target_pairs={{0,16},{16,0},{32,48},{48,32},{64,80},{80,64},{96,112},{112,96},{1... | collective-permute-start | bytes 393224 | tf_op jit(solution)/shard_map/ppermute | solution.py:86
  236.7 11.7 %cholesky.248 = f32[128,128]{1,0:T(8,128)S(1)} custom-call(f32[128,128]{1,0:T(8,128)S(1)} %cholesky.349), custom_call_target="Cholesky" | custom-call | tf_op jit(solution)/shard_map/jit(cholesky)/cholesky | solution.py:139
  248.5 9.8 %custom-call.19 = f32[1,128,128]{1,2,0:T(8,128)S(1)} custom-call(f32[1,128,128]{2,1,0:T(8,128)S(1)} %get-tuple-element.96), custom_call_target="InvertDiagBlocksLowerTriangular" | custom-call | tf_op jit(solution)/shard_map/jit(cholesky)/cholesky | solution.py:139
  258.8 11.7 %cholesky.265 = f32[128,128]{1,0:T(8,128)S(1)} custom-call(f32[128,128]{1,0:T(8,128)S(1)} %convolution_subtract_fusion.6), custom_call_target="Cholesky" | custom-call | tf_op jit(solution)/shard_map/jit(cholesky)/cholesky | solution.py:139
  270.5 11.2 %product.3 = bf16[4096,256]{1,0:T(8,128)(2,1)} custom-call(s32[128]{0:T(128)S(1)} %bitcast.213, s32[128]{0:T(128)S(1)} %compare_select_fusion.4.dst_ids, s32[1]{0:T(128)} %bitcast.210.count, bf16[128,128,128]{2,1,0:T(8,128)(2,1)} %bitcast.218, bf16[16384,256]{1,0:T(8,128)(2,1)} %all-gather.2.cloned.1.call-done.panel), custom_call_target="tpu_custom_call" | custom-call | flops 1073741824 | bytes 14680064 | tf_op jit(solution)/shard_map/product/pallas_call | solution.py:56
  281.8 5.7 %all-to-all-start.2 = ((bf16[16,256,256]{2,1,0:T(8,128)(2,1)}), bf16[16,256,256]{2,1,0:T(8,128)(2,1)S(1)}, u32[]{:S(2)}, u32[]{:S(2)}) async-start(bf16[16,256,256]{2,1,0:T(8,128)(2,1)} %bitcast.228), calls=%async_computation.3 | async-start | bytes 4194304 | tf_op jit(solution)/shard_map/all_to_all | solution.py:151
  290.7 4.1 while.9
  294.8 19.7 %custom-call.20 = f32[2,128,128]{1,2,0:T(8,128)S(1)} custom-call(f32[2,128,128]{2,1,0:T(8,128)S(1)} %get-tuple-element.32), custom_call_target="InvertDiagBlocksLowerTriangular" | custom-call | tf_op jit(solution)/shard_map/jit(_solve_triangular)/triangular_solve | solution.py:140
  317.6 31.5 %all_to_all.21 = bf16[16,256,256]{2,1,0:T(8,128)(2,1)} all-to-all(bf16[16,256,256]{2,1,0:T(8,128)(2,1)S(1)} %broadcast_in_dim.34), channel_id=1, replica_groups=mesh['author'=8,'word'=16] {'word'}, dimensions={0} | all-to-all | bytes 4194304 | tf_op jit(solution)/shard_map/all_to_all | solution.py:157
  349.1 13.3 %product_t.3 = bf16[16384,256]{1,0:T(8,128)(2,1)} custom-call(s32[128]{0:T(128)S(1)} %bitcast.215, s32[128]{0:T(128)S(1)} %compare_select_fusion.3.dst_ids, s32[1]{0:T(128)} %bitcast.211.count, bf16[128,128,128]{2,1,0:T(8,128)(2,1)} %bitcast.219, bf16[4096,256]{1,0:T(8,128)(2,1)} %bitcast.223), custom_call_target="tpu_custom_call" | custom-call | flops 1073741824 | bytes 14680064 | tf_op jit(solution)/shard_map/product_t/pallas_call | solution.py:56
  369.5 5.2 collective-permute-start.19
  378.6 5.3 collective-permute-done.20
  388.9 11.7 %cholesky.282 = f32[128,128]{1,0:T(8,128)S(1)} custom-call(f32[128,128]{1,0:T(8,128)S(1)} %cholesky.352), custom_call_target="Cholesky" | custom-call | tf_op jit(solution)/shard_map/jit(cholesky)/cholesky | solution.py:139
  400.7 9.8 %custom-call.21 = f32[1,128,128]{1,2,0:T(8,128)S(1)} custom-call(f32[1,128,128]{2,1,0:T(8,128)S(1)} %get-tuple-element.92), custom_call_target="InvertDiagBlocksLowerTriangular" | custom-call | tf_op jit(solution)/shard_map/jit(cholesky)/cholesky | solution.py:139
  411.0 11.7 %cholesky.299 = f32[128,128]{1,0:T(8,128)S(1)} custom-call(f32[128,128]{1,0:T(8,128)S(1)} %convolution_subtract_fusion.5), custom_call_target="Cholesky" | custom-call | tf_op jit(solution)/shard_map/jit(cholesky)/cholesky | solution.py:139
  425.3 4.0 while.10
  429.3 19.7 %custom-call.22 = f32[2,128,128]{1,2,0:T(8,128)S(1)} custom-call(f32[2,128,128]{2,1,0:T(8,128)S(1)} %get-tuple-element.33), custom_call_target="InvertDiagBlocksLowerTriangular" | custom-call | tf_op jit(solution)/shard_map/jit(_solve_triangular)/triangular_solve | solution.py:140
  481.8 7.3 %collective-permute-start.37 = (f32[128,256]{0,1:T(8,128)S(1)}, f32[128,256]{0,1:T(8,128)S(1)}, u32[]{:S(2)}, u32[]{:S(2)}) collective-permute-start(f32[128,256]{0,1:T(8,128)S(1)} %copy.30), channel_id=1, source_target_pairs={{0,16},{16,0},{32,48},{48,32},{64,80},{80,64},{96,112},{112,96},{1... | collective-permute-start | bytes 393224 | tf_op jit(solution)/shard_map/ppermute | solution.py:86
  490.4 11.7 %cholesky.316 = f32[128,128]{1,0:T(8,128)S(1)} custom-call(f32[128,128]{1,0:T(8,128)S(1)} %cholesky.355), custom_call_target="Cholesky" | custom-call | tf_op jit(solution)/shard_map/jit(cholesky)/cholesky | solution.py:139
  502.1 9.8 %custom-call.23 = f32[1,128,128]{1,2,0:T(8,128)S(1)} custom-call(f32[1,128,128]{2,1,0:T(8,128)S(1)} %get-tuple-element.88), custom_call_target="InvertDiagBlocksLowerTriangular" | custom-call | tf_op jit(solution)/shard_map/jit(cholesky)/cholesky | solution.py:139
  512.4 11.7 %cholesky.333 = f32[128,128]{1,0:T(8,128)S(1)} custom-call(f32[128,128]{1,0:T(8,128)S(1)} %convolution_subtract_fusion.4), custom_call_target="Cholesky" | custom-call | tf_op jit(solution)/shard_map/jit(cholesky)/cholesky | solution.py:139
  526.8 4.1 while.11
  530.9 19.7 %custom-call.24 = f32[2,128,128]{1,2,0:T(8,128)S(1)} custom-call(f32[2,128,128]{2,1,0:T(8,128)S(1)} %get-tuple-element.34), custom_call_target="InvertDiagBlocksLowerTriangular" | custom-call | tf_op jit(solution)/shard_map/jit(_solve_triangular)/triangular_solve | solution.py:140
  (235 shorter events, 149.7 us)
Async XLA Ops:
  60.8 33.1 %all-to-all-start.1 = ((bf16[16,256,256]{2,1,0:T(8,128)(2,1)}), bf16[16,256,256]{2,1,0:T(8,128)(2,1)S(1)}, u32[]{:S(2)}, u32[]{:S(2)}) async-start(bf16[16,256,256]{2,1,0:T(8,128)(2,1)} %broadcast_in_dim.33), calls=%async_computation.1 | async-start | bytes 4194304 | tf_op jit(solution)/shard_map/all_to_all | solution.py:157
  64.6 129.2 %reduce-scatter.3.cloned.1.call-start = ((), (), s32[]{:S(2)}) async-start(), calls=%async_computation.6 | async-start | bytes 9437184 | tf_op jit(solution)/shard_map/reduce_scatter | solution.py:183
  108.6 161.9 %all-gather.2.cloned.1.call-start = ((), (), s32[]{:S(2)}) async-start(), calls=%async_computation.7 | async-start | bytes 9437184 | tf_op jit(solution)/shard_map/all_gather | solution.py:187
  119.4 8.1 %collective-permute-start.1 = (f32[128,256]{0,1:T(8,128)S(1)}, f32[128,256]{0,1:T(8,128)S(1)}, u32[]{:S(2)}, u32[]{:S(2)}) collective-permute-start(f32[128,256]{0,1:T(8,128)S(1)} %bitcast_add_fusion.7), channel_id=1, source_target_pairs={{0,64},{16,80},{32,96},{48,112},{64,0},{80,16},{96,32},{112,48},{1... | collective-permute-start | bytes 393224 | tf_op jit(solution)/shard_map/ppermute | solution.py:90
  120.3 10.6 %collective-permute-start.2 = (f32[128,256]{0,1:T(8,128)S(1)}, f32[128,256]{0,1:T(8,128)S(1)}, u32[]{:S(2)}, u32[]{:S(2)}) collective-permute-start(f32[128,256]{0,1:T(8,128)S(1)} %bitcast_add_fusion.7), channel_id=1, source_target_pairs={{0,32},{16,48},{32,64},{48,80},{64,96},{80,112},{96,0},{112,16},{1... | collective-permute-start | bytes 393224 | tf_op jit(solution)/shard_map/ppermute | solution.py:90
  120.3 10.6 %collective-permute-start.3 = (f32[128,256]{0,1:T(8,128)S(1)}, f32[128,256]{0,1:T(8,128)S(1)}, u32[]{:S(2)}, u32[]{:S(2)}) collective-permute-start(f32[128,256]{0,1:T(8,128)S(1)} %bitcast_add_fusion.7), channel_id=1, source_target_pairs={{0,96},{16,112},{32,0},{48,16},{64,32},{80,48},{96,64},{112,80},{1... | collective-permute-start | bytes 393224 | tf_op jit(solution)/shard_map/ppermute | solution.py:90
  202.0 4.9 collective-permute-start.6
  204.2 4.0 collective-permute-start.7
  208.2 4.4 collective-permute-start.10
  208.3 4.4 collective-permute-start.11
  211.0 4.3 collective-permute-start.9
  215.3 4.4 collective-permute-start.12
  216.9 4.4 collective-permute-start.13
  221.3 5.1 collective-permute-start.15
  221.4 6.3 %collective-permute-start.16 = (f32[32,256]{1,0:T(8,128)S(1)}, f32[32,256]{1,0:T(8,128)S(1)}, u32[]{:S(2)}, u32[]{:S(2)}) collective-permute-start(f32[32,256]{1,0:T(8,128)S(1)} %add_add_fusion.4), channel_id=1, source_target_pairs={{0,64},{16,80},{32,96},{48,112},{64,0},{80,16},{96,32},{112,48},{1... | collective-permute-start | bytes 98312 | tf_op jit(solution)/shard_map/ppermute | solution.py:90
  224.6 4.0 collective-permute-start.17
  229.3 7.2 %collective-permute-start.18 = (f32[128,256]{0,1:T(8,128)S(1)}, f32[128,256]{0,1:T(8,128)S(1)}, u32[]{:S(2)}, u32[]{:S(2)}) collective-permute-start(f32[128,256]{0,1:T(8,128)S(1)} %copy.22), channel_id=1, source_target_pairs={{0,16},{16,0},{32,48},{48,32},{64,80},{80,64},{96,112},{112,96},{1... | collective-permute-start | bytes 393224 | tf_op jit(solution)/shard_map/ppermute | solution.py:86
  281.8 35.0 %all-to-all-start.2 = ((bf16[16,256,256]{2,1,0:T(8,128)(2,1)}), bf16[16,256,256]{2,1,0:T(8,128)(2,1)S(1)}, u32[]{:S(2)}, u32[]{:S(2)}) async-start(bf16[16,256,256]{2,1,0:T(8,128)(2,1)} %bitcast.228), calls=%async_computation.3 | async-start | bytes 4194304 | tf_op jit(solution)/shard_map/all_to_all | solution.py:151
  287.4 162.5 %reduce-scatter.5.cloned.1.call-start = ((), (), s32[]{:S(2)}) async-start(), calls=%async_computation.8 | async-start | bytes 9437184 | tf_op jit(solution)/shard_map/reduce_scatter | solution.py:183
  369.5 6.2 %collective-permute-start.19 = (f32[128,256]{0,1:T(8,128)S(1)}, f32[128,256]{0,1:T(8,128)S(1)}, u32[]{:S(2)}, u32[]{:S(2)}) collective-permute-start(f32[128,256]{0,1:T(8,128)S(1)} %bitcast.241), channel_id=1, source_target_pairs={{0,16},{16,0},{32,48},{48,32},{64,80},{80,64},{96,112},{112,96},{1... | collective-permute-start | bytes 393224 | tf_op jit(solution)/shard_map/ppermute | solution.py:86
  375.7 8.1 %collective-permute-start.20 = (f32[128,256]{0,1:T(8,128)S(1)}, f32[128,256]{0,1:T(8,128)S(1)}, u32[]{:S(2)}, u32[]{:S(2)}) collective-permute-start(f32[128,256]{0,1:T(8,128)S(1)} %bitcast_add_fusion.5), channel_id=1, source_target_pairs={{0,64},{16,80},{32,96},{48,112},{64,0},{80,16},{96,32},{112,48},{1... | collective-permute-start | bytes 393224 | tf_op jit(solution)/shard_map/ppermute | solution.py:90
  375.8 10.9 %collective-permute-start.21 = (f32[128,256]{0,1:T(8,128)S(1)}, f32[128,256]{0,1:T(8,128)S(1)}, u32[]{:S(2)}, u32[]{:S(2)}) collective-permute-start(f32[128,256]{0,1:T(8,128)S(1)} %bitcast_add_fusion.5), channel_id=1, source_target_pairs={{0,32},{16,48},{32,64},{48,80},{64,96},{80,112},{96,0},{112,16},{1... | collective-permute-start | bytes 393224 | tf_op jit(solution)/shard_map/ppermute | solution.py:90
  375.9 10.8 %collective-permute-start.22 = (f32[128,256]{0,1:T(8,128)S(1)}, f32[128,256]{0,1:T(8,128)S(1)}, u32[]{:S(2)}, u32[]{:S(2)}) collective-permute-start(f32[128,256]{0,1:T(8,128)S(1)} %bitcast_add_fusion.5), channel_id=1, source_target_pairs={{0,96},{16,112},{32,0},{48,16},{64,32},{80,48},{96,64},{112,80},{1... | collective-permute-start | bytes 393224 | tf_op jit(solution)/shard_map/ppermute | solution.py:90
  457.4 4.3 collective-permute-start.25
  458.6 4.5 collective-permute-start.26
  463.1 4.4 collective-permute-start.28
  463.6 4.2 collective-permute-start.29
  467.9 4.3 collective-permute-start.31
  468.6 4.0 collective-permute-start.32
  473.9 4.3 collective-permute-start.34
  474.0 5.5 collective-permute-start.35
  481.8 8.4 %collective-permute-start.37 = (f32[128,256]{0,1:T(8,128)S(1)}, f32[128,256]{0,1:T(8,128)S(1)}, u32[]{:S(2)}, u32[]{:S(2)}) collective-permute-start(f32[128,256]{0,1:T(8,128)S(1)} %copy.30), channel_id=1, source_target_pairs={{0,16},{16,0},{32,48},{48,32},{64,80},{80,64},{96,112},{112,96},{1... | collective-permute-start | bytes 393224 | tf_op jit(solution)/shard_map/ppermute | solution.py:86
  (17 other events, 75.1 us)
Sparse Core Ops, SparseCore 0:
  108.8 57.0 reduce-scatter.2
  197.2 50.3 all-gather.1
  362.6 58.0 reduce-scatter.4

commit v2 on v1

v2 whole, which is shorter than its diff:
```python
import jax
import jax.numpy as jnp
from jax import lax
from jax.experimental import pallas as pl
from jax.experimental.pallas import tpu as pltpu
from jax.sharding import PartitionSpec as P

ITERS = 2
GROUP = 4
AHEAD = 8
BLOCK = 64
HIGH = lax.Precision.HIGHEST


def product_kernel(src_ids, dst_ids, count, values, panel, out, total, part, source, part_sem, source_sem):
    size = part.shape[1]
    groups = (count[0] + GROUP - 1) // GROUP

    def copies(group):
        first = group * GROUP
        yield pltpu.make_async_copy(
            values.at[pl.ds(first, GROUP)], part.at[pl.ds(first, GROUP)], part_sem.at[group]
        )
        for offset in range(GROUP):
            slot = first + offset
            rows = pl.ds(pl.multiple_of(src_ids[slot] * size, size), size)
            yield pltpu.make_async_copy(panel.at[rows], source.at[slot], source_sem.at[slot])

    def start(group, carry):
        for copy in copies(group):
            copy.start()
        return carry

    def clear(index, carry):
        total[index] = jnp.zeros_like(total[index])
        return carry

    def work(group, carry):
        @pl.when(group + AHEAD < groups)
        def _():
            start(group + AHEAD, 0)

        for copy in copies(group):
            copy.wait()
        first = group * GROUP
        prods = [
            jnp.dot(part[first + offset], source[first + offset], preferred_element_type=jnp.float32)
            for offset in range(GROUP)
        ]
        for offset in range(GROUP):
            total[dst_ids[first + offset]] += prods[offset]
        return carry

    def emit(index, carry):
        out[pl.ds(pl.multiple_of(index * size, size), size), :] = total[index].astype(out.dtype)
        return carry

    lax.fori_loop(0, jnp.minimum(AHEAD, groups), start, 0)
    lax.fori_loop(0, total.shape[0], clear, 0)
    lax.fori_loop(0, groups, work, 0)
    lax.fori_loop(0, out.shape[0] // size, emit, 0)


def product_t_kernel(src_ids, dst_ids, count, values, panel, out, total, part, staged, part_sem, out_sem):
    size = part.shape[1]
    groups = (count[0] + GROUP - 1) // GROUP

    def fetch(group):
        span = pl.ds(group * GROUP, GROUP)
        return pltpu.make_async_copy(values.at[span], part.at[span], part_sem.at[group])

    def start(group, carry):
        fetch(group).start()
        return carry

    def clear(index, carry):
        total[index] = jnp.zeros_like(total[index])
        return carry

    def work(group, carry):
        fetch(group).wait()
        first = group * GROUP
        prods = []
        for offset in range(GROUP):
            rows = pl.ds(pl.multiple_of(src_ids[first + offset] * size, size), size)
            prods.append(
                lax.dot_general(
                    part[first + offset],
                    panel[rows, :],
                    (((0,), (0,)), ((), ())),
                    preferred_element_type=jnp.float32,
                )
            )
        for offset in range(GROUP):
            total[dst_ids[first + offset]] += prods[offset]
        return carry

    def emit(index, carry):
        staged[pl.ds(pl.multiple_of(index * size, size), size), :] = total[index].astype(staged.dtype)
        return carry

    lax.fori_loop(0, groups, start, 0)
    lax.fori_loop(0, total.shape[0], clear, 0)
    lax.fori_loop(0, groups, work, 0)
    blocks = out.shape[0] // size
    pieces = out_sem.shape[0]
    sends = []
    for piece in range(pieces):
        lax.fori_loop(piece * blocks // pieces, (piece + 1) * blocks // pieces, emit, 0)
        rows = pl.ds(piece * out.shape[0] // pieces, out.shape[0] // pieces)
        sends.append(pltpu.make_async_copy(staged.at[rows], out.at[rows], out_sem.at[piece]))
        sends[-1].start()
    for send in sends:
        send.wait()


def product(values, src_ids, dst_ids, count, panel, out_blocks, transpose):
    cap, size, _ = values.shape
    width = panel.shape[1]
    dst_ids = jnp.where(jnp.arange(cap, dtype=jnp.int32) < count, dst_ids, out_blocks)
    smem = pl.BlockSpec(memory_space=pltpu.SMEM)
    vmem = pl.BlockSpec(memory_space=pltpu.VMEM)
    whole = pl.BlockSpec(memory_space=pl.ANY)
    values = pltpu.with_memory_space_constraint(values, pltpu.HBM)
    rows = out_blocks * size
    scratch = [
        pltpu.VMEM((out_blocks + 1, size, width), jnp.float32),
        pltpu.VMEM((cap, size, size), values.dtype),
    ]
    if transpose:
        kernel, panel_spec, out_spec = product_t_kernel, vmem, whole
        out_shape = jax.ShapeDtypeStruct((rows, width), jnp.bfloat16)
        scratch += [pltpu.VMEM((rows, width), jnp.bfloat16)]
        scratch += [pltpu.SemaphoreType.DMA((cap // GROUP,)), pltpu.SemaphoreType.DMA((8,))]
    else:
        kernel, panel_spec, out_spec = product_kernel, whole, vmem
        panel = pltpu.with_memory_space_constraint(panel, pltpu.HBM)
        out_shape = pltpu.VMEM((rows, width), jnp.bfloat16)
        scratch += [pltpu.VMEM((cap, size, width), panel.dtype)]
        scratch += [pltpu.SemaphoreType.DMA((cap // GROUP,)), pltpu.SemaphoreType.DMA((cap,))]
    return pl.pallas_call(
        kernel,
        out_shape=out_shape,
        in_specs=[smem, smem, smem, whole, panel_spec],
        out_specs=out_spec,
        scratch_shapes=scratch,
        compiler_params=pltpu.CompilerParams(vmem_limit_bytes=36 * 1024 * 1024),
        cost_estimate=pl.CostEstimate(
            flops=2 * cap * size * size * width,
            bytes_accessed=2 * (cap * size * size + panel.size + rows * width),
            transcendentals=0,
        ),
        name="product_t" if transpose else "product",
    )(src_ids, dst_ids, count.reshape(1), values, panel)


def fold_kernel(parts, factor, field, copies):
    total = parts[0].astype(jnp.float32)
    for index in range(1, parts.shape[0]):
        total += parts[index].astype(jnp.float32)
    if factor is not None:
        total = apply_t(total, factor[...])
    field[...] = total
    short = total.astype(copies.dtype)
    for index in range(copies.shape[0]):
        copies[index] = short


def fold(parts, factor):
    vmem = pl.BlockSpec(memory_space=pltpu.VMEM)
    operands = (parts,) if factor is None else (parts, factor)
    kernel = fold_kernel if factor is not None else lambda p, f, c: fold_kernel(p, None, f, c)
    return pl.pallas_call(
        kernel,
        out_shape=(
            pltpu.VMEM(parts.shape[1:], jnp.float32),
            pltpu.VMEM(parts.shape, jnp.bfloat16),
        ),
        in_specs=[vmem] * len(operands),
        out_specs=(vmem, vmem),
        name="fold",
    )(*operands)


def gram_of(field):
    return lax.dot_general(
        field, field, (((0,), (0,)), ((), ())), precision=HIGH, preferred_element_type=jnp.float32
    )


def hop_core(array):
    return lax.ppermute(array, "author", [(i, i ^ 1) for i in range(8)])


def hop_x(array, k):
    return lax.ppermute(array, "author", [(i, (i + 2 * k) % 8) for i in range(8)])


def hop_y(array, k):
    return lax.ppermute(array, "word", [(i, (i + 4 * k) % 16) for i in range(16)])


def hop_z(array, k):
    return lax.ppermute(array, "word", [(i, (i // 4) * 4 + (i + k) % 4) for i in range(16)])


def pick(array, index):
    return lax.dynamic_index_in_dim(array, index, 0, keepdims=False)


def split_core(gram, core):
    halves = gram.reshape(2, gram.shape[0] // 2, gram.shape[1])
    return pick(halves, core) + hop_core(pick(halves, 1 - core))


def join_core(half, core):
    other = hop_core(half)
    return jnp.where(core == 0, jnp.concatenate([half, other]), jnp.concatenate([other, half]))


def sum_author(gram):
    core = lax.axis_index("author") % 2
    half = split_core(gram, core)
    parts = [hop_x(half, k) for k in (1, 3, 2)]
    half = (half + parts[2]) + (parts[0] + parts[1])
    return join_core(half, core)


def sum_all(gram):
    place = lax.axis_index("author")
    core, x = place % 2, place // 2
    half = split_core(gram, core)
    chunks = half.reshape(4, half.shape[0] // 4, half.shape[1])
    got = [hop_x(pick(chunks, (x + k) % 4), k) for k in (1, 3, 2)]
    part = (pick(chunks, x) + got[2]) + (got[0] + got[1])
    for hop in (hop_y, hop_z):
        got = [hop(part, k) for k in (1, 3, 2)]
        part = (part + got[2]) + (got[0] + got[1])
    ring = jnp.stack([part] + [hop_x(part, k) for k in (1, 2, 3)])
    half = jnp.take(ring, (x - jnp.arange(4)) % 4, axis=0).reshape(half.shape)
    return join_core(half, core)


def eliminate(strips):
    shape = strips[0].shape
    sub = lax.broadcasted_iota(jnp.int32, shape, 0)
    half = shape[1] // 2

    def column(strip, lane):
        return jnp.broadcast_to(strip[:, lane : lane + 1], shape)

    def row(strip, j):
        return jnp.broadcast_to(strip[j : j + 1, :], shape)

    for p in range(len(strips)):
        lead = strips[p]
        lanes = [half + 8 * p + j for j in range(8)]
        cols = [column(lead, lane) for lane in lanes]
        below = {i: [column(strips[i], lane) for lane in lanes] for i in range(p + 1, len(strips))}
        scale = jnp.zeros(shape, jnp.float32)
        for j in range(0, 8, 2):
            a, b, c = row(cols[j], j), row(cols[j + 1], j), row(cols[j + 1], j + 1)
            inv0 = 1.0 / a
            inv1 = a / (a * c - b * b)
            m0 = jnp.where(sub > j, cols[j] * inv0, 0.0)
            m1 = jnp.where(sub > j + 1, (cols[j + 1] - m0 * b) * inv1, 0.0)
            top0 = row(lead, j)
            top1 = row(lead, j + 1) - (b * inv0) * top0
            lead = (lead - m0 * top0) - m1 * top1
            scale = jnp.where(sub == j, lax.rsqrt(a), scale)
            scale = jnp.where(sub == j + 1, jnp.sqrt(inv1), scale)
            tops = []
            for k in range(j + 2, 8):
                u0 = row(cols[k], j)
                u1 = row(cols[k], j + 1) - (b * inv0) * u0
                cols[k] = (cols[k] - m0 * u0) - m1 * u1
                tops.append((u0, u1))
            for i, col in below.items():
                n0 = col[j] * inv0
                n1 = (col[j + 1] - n0 * b) * inv1
                for k, (u0, u1) in zip(range(j + 2, 8), tops):
                    col[k] = (col[k] - n0 * u0) - n1 * u1
                strips[i] = (strips[i] - n0 * top0) - n1 * top1
        strips[p] = lead * scale
    return strips


def whiten_kernel(g_ref, out_ref, s_ref, y_ref):
    n = g_ref.shape[0]
    g = g_ref[...]
    eye = lax.broadcasted_iota(jnp.int32, (n, n), 0) == lax.broadcasted_iota(jnp.int32, (n, n), 1)
    diag = jnp.where(eye, g, 0.0)
    across = lax.rsqrt(jnp.sum(diag, axis=0, keepdims=True))
    down = lax.rsqrt(jnp.sum(diag, axis=1, keepdims=True))
    s_ref[...] = g * across * down
    y_ref[...] = jnp.where(eye, 1.0, 0.0)
    lane = lax.broadcasted_iota(jnp.int32, (BLOCK, n), 1)
    def stage(at, carry):
        rows = pl.ds(pl.multiple_of(at * BLOCK, BLOCK), BLOCK)
        left, right = s_ref[rows, :], y_ref[rows, :]
        turned = pltpu.roll(left, lax.rem(n + BLOCK - at * BLOCK, n), 1)[:, : 2 * BLOCK]
        i0 = lax.broadcasted_iota(jnp.int32, turned.shape, 0)
        i1 = lax.broadcasted_iota(jnp.int32, turned.shape, 1)
        start = jnp.where(i1 < BLOCK, jnp.where(i0 == i1, 1.0, 0.0), turned)
        strips = eliminate([start[8 * i : 8 * i + 8] for i in range(BLOCK // 8)])
        inverse = jnp.concatenate(strips, axis=0)[:, :BLOCK]
        dot = lambda u, v, d: lax.dot_general(u, v, (((d,), (0,)), ((), ())), precision=HIGH, preferred_element_type=jnp.float32)
        left = dot(inverse, left, 1)
        right = dot(inverse, right, 1)
        rest = jnp.where(lane >= (at + 1) * BLOCK, left, 0.0)
        s_ref[...] -= dot(rest, left, 0)
        y_ref[...] -= dot(rest, right, 0)
        y_ref[rows, :] = right
        return carry
    lax.fori_loop(0, n // BLOCK, stage, 0)
    out_ref[...] = y_ref[...] * across


def whitener(gram):
    return pl.pallas_call(
        whiten_kernel,
        out_shape=jax.ShapeDtypeStruct(gram.shape, jnp.float32),
        scratch_shapes=[pltpu.VMEM(gram.shape, jnp.float32)] * 2,
        cost_estimate=pl.CostEstimate(flops=10**9, bytes_accessed=40 * 10**6, transcendentals=0),
        name="whitener",
    )(gram)


def apply_t(field, inverse):
    return lax.dot_general(
        field, inverse, (((1,), (1,)), ((), ())), precision=HIGH, preferred_element_type=jnp.float32
    )


def swap_word(parts):
    return lax.all_to_all(parts, "word", 0, 0)


def shards(block_values, block_rows, block_cols, block_count, omega):
    values = block_values[0, 0]
    rows = block_rows[0, 0]
    cols = block_cols[0, 0]
    count = block_count[0, 0]
    size = values.shape[1]
    word_blocks = omega.shape[0] // size
    author_blocks = 32
    authors = author_blocks * size * lax.axis_size("author")
    words = word_blocks * size * lax.axis_size("word")
    wide = omega
    word_factor = None
    for turn in range(ITERS):
        terms = product(values, cols, rows, count, wide, author_blocks, False)
        y, copies = fold(swap_word(terms.reshape(16, -1, terms.shape[1])), word_factor)
        y_rows = swap_word(copies).reshape(terms.shape)
        author_factor = whitener(
            sum_author(lax.dot_general(y_rows, y_rows, (((0,), (0,)), ((), ())), preferred_element_type=jnp.float32))
            / authors
        )
        terms = product(values, rows, cols, count, y_rows, word_blocks, True)
        z = lax.psum_scatter(terms, "author", scatter_dimension=0, tiled=True).astype(jnp.float32)
        z = apply_t(z, author_factor)
        word_factor = whitener(sum_all(gram_of(z)) / words)
        if turn + 1 < ITERS:
            wide = lax.all_gather(z.astype(jnp.bfloat16), "author", axis=0, tiled=True)
    author_basis = apply_t(y, author_factor).astype(jnp.bfloat16)
    word_basis = apply_t(z, word_factor).astype(jnp.bfloat16)
    return (author_basis, word_basis)


def solution(mesh):
    return jax.shard_map(
        shards,
        mesh=mesh,
        in_specs=(
            P("author", "word", None, None, None),
            P("author", "word", None),
            P("author", "word", None),
            P("author", "word"),
            P("word", None),
        ),
        out_specs=(P(("author", "word"), None), P(("word", "author"), None)),
        check_vma=False,
    )
```

time: 564 us -> 470 us (0.83)
  other arithmetic: 219 us -> 3.97 us
  waiting for transfers between devices: 73.2 us -> 170 us
  Pallas kernels: 49 us -> 88.3 us
  local copies, waits for them, and re-layouts: 30.8 us -> 17.1 us
    another operation x36 -> x0, other arithmetic: 217 us -> none  [the longest x27 138 us: whitener(): lower = jnp.linalg.cholesky(gram)]
    all_gather x1, waiting for transfers between devices: 0.02 us -> 45.2 us  [shards(): wide = lax.all_gather(z.astype(jnp.bfloat16), 'author', axis=0, tiled=True)]
    reduce_scatter x2, waiting for transfers between devices: 0.04 us -> 42.4 us  [shards(): lax.psum_scatter(terms, 'author', scatter_dimension=0, tiled=True)]
    pallas_call x4 -> x10, Pallas kernels: 49 us -> 88.3 us  [the longest x4 49.2 us: whitener(): pl.pallas_call(whiten_kernel, out_shape=jax.ShapeDtypeStruct(gram.shape,...]
    another operation x37 -> x0, local copies, waits for them, and re-layouts: 15.6 us -> none  [the longest x29 15.5 us: whitener(): jax.scipy.linalg.solve_triangular(lower, jnp.eye(gram.shape[0], dtype=jnp...]
    ppermute x6, waiting for transfers between devices: 5.78 us -> 19.3 us  [hop_y(): lax.ppermute(array, 'word', [(i, (i + 4 * k) % 16) for i in range(16)])]
    ppermute x8, starting transfers between devices: 24.7 us -> 12.9 us  [hop_core(): return lax.ppermute(array, 'author', [(i, i ^ 1) for i in range(8)])]
  transfers between devices with their start and end apart: 43 -> 43, of which waited for: 30 -> 31; matrix products, arithmetic and copies ran while one was open for 35% -> 4% of each run, Pallas kernels for 0% -> 10%
where the time goes in v2:
time: 470 us; the launch traced here: 463 us
  waiting for transfers between devices  170 us (36%)
  Pallas kernels  88.3 us (19%)
  blocking collectives  74.1 us (16%)
  starting transfers between devices  71.6 us (15%)
  matrix products  22 us (5%)
  local copies, waits for them, and re-layouts  17.1 us (4%)
  between operations  15.2 us (3%)
    all_to_all x2, blocking collectives, swap_word(): return lax.all_to_all(parts, 'word', 0, 0)  74.1 us
    pallas_call x4, Pallas kernels, whitener(): pl.pallas_call(whiten_kernel, out_shape=jax.ShapeDtypeStruct(gram.shape,...  49.2 us
    all_gather x1, waiting for transfers between devices, shards(): wide = lax.all_gather(z.astype(jnp.bfloat16), 'author', axis=0, tiled=True)  45.2 us
    reduce_scatter x2, waiting for transfers between devices, shards(): lax.psum_scatter(terms, 'author', scatter_dimension=0, tiled=True)  42.4 us
    pallas_call x4, Pallas kernels, product(): pl.pallas_call(kernel, out_shape=out_shape, in_specs=[smem, smem, smem, w...  34.1 us
    all_to_all x2, waiting for transfers between devices, swap_word(): return lax.all_to_all(parts, 'word', 0, 0)  29.5 us
    ppermute x18, starting transfers between devices, hop_x(): lax.ppermute(array, 'author', [(i, (i + 2 * k) % 8) for i in range(8)])  26 us
    ppermute x18, waiting for transfers between devices, hop_x(): lax.ppermute(array, 'author', [(i, (i + 2 * k) % 8) for i in range(8)])  24.1 us
  transfers between devices with their start and end apart: 43, of which 31 were waited for; matrix products, arithmetic and copies ran while one was open for 4% of the time, Pallas kernels for 10%

profile of v2, /device:TPU:1, one launch (start us, length us, event | category | flops | bytes accessed | tf_op | source)
XLA Modules:
  0.0 462.6 jit_solution(16420566643332369267)
XLA Ops:
  9.1 7.6 %product.2 = bf16[4096,256]{1,0:T(8,128)(2,1)S(1)} custom-call(s32[128]{0:T(128)S(1)} %bitcast.100, s32[128]{0:T(128)S(1)} %compare_select_fusion.4.dst_ids, s32[1]{0:T(128)} %bitcast.89.count, bf16[128,128,128]{2,1,0:T(8,128)(2,1)} %bitcast.104, bf16[16384,256]{1,0:T(8,128)(2,1)} %panel.1), custom_call_target="tpu_custom_call" | custom-call | flops 1073741824 | bytes 14680064 | tf_op jit(solution)/shard_map/product/pallas_call | solution.py:141
  16.7 39.9 %all_to_all.20.p = bf16[16,256,256]{2,1,0:T(8,128)(2,1)} all-to-all(bf16[16,256,256]{2,1,0:T(8,128)(2,1)S(1)} %bitcast.99), channel_id=1, replica_groups=mesh['author'=8,'word'=16] {'word'}, dimensions={0} | all-to-all | bytes 4194304 | tf_op jit(solution)/shard_map/all_to_all | solution.py:336
  60.6 3.8 all-to-all-start.1
  64.6 29.5 %all-to-all-done.1 = bf16[16,256,256]{2,1,0:T(8,128)(2,1)S(1)} async-done(((bf16[16,256,256]{2,1,0:T(8,128)(2,1)}), bf16[16,256,256]{2,1,0:T(8,128)(2,1)S(1)}, u32[]{:S(2)}, u32[]{:S(2)}) %all-to-all-start.1) | async-done | bytes 2097184 | tf_op jit(solution)/shard_map/all_to_all | solution.py:336
  94.1 8.7 %product_t.2 = bf16[16384,256]{1,0:T(8,128)(2,1)S(1)} custom-call(s32[128]{0:T(128)S(1)} %bitcast.102, s32[128]{0:T(128)S(1)} %compare_select_fusion.3.dst_ids, s32[1]{0:T(128)} %bitcast.90.count, bf16[128,128,128]{2,1,0:T(8,128)(2,1)} %bitcast.105, bf16[4096,256]{1,0:T(8,128)(2,1)S(1)} %bitcast.93), custom_call_target="tpu_custom_call" | custom-call | flops 1073741824 | bytes 14680064 | tf_op jit(solution)/shard_map/product_t/pallas_call | solution.py:141
  102.8 3.3 copy-done
  106.2 3.0 copy.9
  117.5 2.8 collective-permute-done.1
  120.3 4.1 collective-permute-done.2
  126.9 12.3 %whitener.4 = f32[256,256]{1,0:T(8,128)} custom-call(f32[256,256]{1,0:T(8,128)} %fusion.g_ref), custom_call_target="tpu_custom_call" | custom-call | flops 1000000000 | bytes 40000000 | tf_op jit(solution)/shard_map/whitener/pallas_call | solution.py:320
  139.2 23.2 %reduce-scatter.3.cloned.1.call-done = bf16[2048,256]{1,0:T(8,128)(2,1)} async-done(((bf16[16384,256]{1,0:T(8,128)(2,1)}), bf16[2048,256]{1,0:T(8,128)(2,1)}) %reduce-scatter.3.cloned.1.call-update) | async-done | bytes 1048592 | tf_op jit(solution)/shard_map/reduce_scatter | solution.py:360
  162.3 3.3 fusion.7
  165.6 3.5 fusion.9
  170.8 45.2 %all-gather.2.cloned.1.call-done.panel = bf16[16384,256]{1,0:T(8,128)(2,1)} async-done(((bf16[2048,256]{1,0:T(8,128)(2,1)}), bf16[16384,256]{1,0:T(8,128)(2,1)}) %all-gather.2.cloned.1.call-update) | async-done | bytes 8388624 | tf_op jit(solution)/shard_map/all_gather | solution.py:364
  216.0 9.1 %product.3 = bf16[4096,256]{1,0:T(8,128)(2,1)} custom-call(s32[128]{0:T(128)S(1)} %bitcast.101, s32[128]{0:T(128)S(1)} %compare_select_fusion.4.dst_ids, s32[1]{0:T(128)} %bitcast.91.count, bf16[128,128,128]{2,1,0:T(8,128)(2,1)} %bitcast.106, bf16[16384,256]{1,0:T(8,128)(2,1)} %all-gather.2.cloned.1.call-done.panel), custom_call_target="tpu_custom_call" | custom-call | flops 1073741824 | bytes 14680064 | tf_op jit(solution)/shard_map/product/pallas_call | solution.py:141
  225.2 10.1 %all-to-all-start.2 = ((bf16[16,256,256]{2,1,0:T(8,128)(2,1)}), bf16[16,256,256]{2,1,0:T(8,128)(2,1)}, u32[]{:S(2)}, u32[]{:S(2)}) async-start(bf16[16,256,256]{2,1,0:T(8,128)(2,1)} %bitcast.12), calls=%async_computation.3 | async-start | bytes 4194304 | tf_op jit(solution)/shard_map/all_to_all | solution.py:336
  244.7 15.6 %collective-permute-done.10 = f32[32,256]{1,0:T(8,128)S(1)} collective-permute-done((f32[32,256]{1,0:T(8,128)S(1)}, f32[32,256]{1,0:T(8,128)S(1)}, u32[]{:S(2)}, u32[]{:S(2)}) %collective-permute-start.10) | collective-permute-done | bytes 32800 | tf_op jit(solution)/shard_map/ppermute | solution.py:200
  278.9 12.3 %whitener.5.factor = f32[256,256]{1,0:T(8,128)} custom-call(f32[256,256]{1,0:T(8,128)} %fusion.1.g_ref), custom_call_target="tpu_custom_call" | custom-call | flops 1000000000 | bytes 40000000 | tf_op jit(solution)/shard_map/whitener/pallas_call | solution.py:320
  294.9 34.3 %all_to_all.21 = bf16[16,256,256]{2,1,0:T(8,128)(2,1)S(1)} all-to-all(bf16[16,256,256]{2,1,0:T(8,128)(2,1)} %copy-done.3), channel_id=1, replica_groups=mesh['author'=8,'word'=16] {'word'}, dimensions={0} | all-to-all | bytes 4194304 | tf_op jit(solution)/shard_map/all_to_all | solution.py:336
  329.2 8.7 %product_t.3 = bf16[16384,256]{1,0:T(8,128)(2,1)S(1)} custom-call(s32[128]{0:T(128)S(1)} %bitcast.103, s32[128]{0:T(128)S(1)} %compare_select_fusion.3.dst_ids, s32[1]{0:T(128)} %bitcast.92.count, bf16[128,128,128]{2,1,0:T(8,128)(2,1)} %bitcast.107, bf16[4096,256]{1,0:T(8,128)(2,1)S(1)} %bitcast.96), custom_call_target="tpu_custom_call" | custom-call | flops 1073741824 | bytes 14680064 | tf_op jit(solution)/shard_map/product_t/pallas_call | solution.py:141
  337.9 3.3 copy-done.1
  341.2 3.0 copy.10
  350.5 4.1 collective-permute-start.21
  354.8 5.0 %collective-permute-done.21 = f32[128,256]{1,0:T(8,128)S(1)} collective-permute-done((f32[128,256]{1,0:T(8,128)S(1)}, f32[128,256]{1,0:T(8,128)S(1)}, u32[]{:S(2)}, u32[]{:S(2)}) %collective-permute-start.21) | collective-permute-done | bytes 131104 | tf_op jit(solution)/shard_map/ppermute | solution.py:196
  359.8 4.1 collective-permute-done.22
  367.0 12.3 %whitener.6 = f32[256,256]{1,0:T(8,128)} custom-call(f32[256,256]{1,0:T(8,128)} %fusion.2.g_ref), custom_call_target="tpu_custom_call" | custom-call | flops 1000000000 | bytes 40000000 | tf_op jit(solution)/shard_map/whitener/pallas_call | solution.py:320
  379.3 19.3 %reduce-scatter.5.cloned.1.call-done = bf16[2048,256]{1,0:T(8,128)(2,1)} async-done(((bf16[16384,256]{1,0:T(8,128)(2,1)}), bf16[2048,256]{1,0:T(8,128)(2,1)}) %reduce-scatter.5.cloned.1.call-update) | async-done | bytes 1048592 | tf_op jit(solution)/shard_map/reduce_scatter | solution.py:360
  400.9 3.5 fusion.12
  424.5 3.2 collective-permute-start.35
  431.1 6.6 %collective-permute-start.37 = (f32[128,256]{1,0:T(8,128)S(1)}, f32[128,256]{1,0:T(8,128)S(1)}, u32[]{:S(2)}, u32[]{:S(2)}) collective-permute-start(f32[128,256]{1,0:T(8,128)S(1)} %bitcast.114), channel_id=1, source_target_pairs={{0,16},{16,0},{32,48},{48,32},{64,80},{80,64},{96,112},{112,96},{1... | collective-permute-start | bytes 393224 | tf_op jit(solution)/shard_map/ppermute | solution.py:192
  439.6 12.3 %whitener.7 = f32[256,256]{1,0:T(8,128)} custom-call(f32[256,256]{1,0:T(8,128)} %fusion.3.g_ref), custom_call_target="tpu_custom_call" | custom-call | flops 1000000000 | bytes 40000000 | tf_op jit(solution)/shard_map/whitener/pallas_call | solution.py:320
  451.8 3.8 convolution_convert_fusion
  (128 shorter events, 86.9 us)
Async XLA Ops:
  60.6 33.5 %all-to-all-start.1 = ((bf16[16,256,256]{2,1,0:T(8,128)(2,1)}), bf16[16,256,256]{2,1,0:T(8,128)(2,1)S(1)}, u32[]{:S(2)}, u32[]{:S(2)}) async-start(bf16[16,256,256]{2,1,0:T(8,128)(2,1)} %copy-done.2), calls=%async_computation.1 | async-start | bytes 4194304 | tf_op jit(solution)/shard_map/all_to_all | solution.py:336
  64.5 97.8 %reduce-scatter.3.cloned.1.call-start = ((), (), s32[]{:S(2)}) async-start(), calls=%async_computation.6 | async-start | bytes 9437184 | tf_op jit(solution)/shard_map/reduce_scatter | solution.py:360
  106.1 109.9 %all-gather.2.cloned.1.call-start = ((), (), s32[]{:S(2)}) async-start(), calls=%async_computation.7 | async-start | bytes 9437184 | tf_op jit(solution)/shard_map/all_gather | solution.py:364
  112.9 7.3 %collective-permute-start.1 = (f32[128,256]{1,0:T(8,128)S(1)}, f32[128,256]{1,0:T(8,128)S(1)}, u32[]{:S(2)}, u32[]{:S(2)}) collective-permute-start(f32[128,256]{1,0:T(8,128)S(1)} %bitcast_add_fusion.3), channel_id=1, source_target_pairs={{0,64},{16,80},{32,96},{48,112},{64,0},{80,16},{96,32},{112,48},{1... | collective-permute-start | bytes 393224 | tf_op jit(solution)/shard_map/ppermute | solution.py:196
  114.8 9.5 %collective-permute-start.2 = (f32[128,256]{1,0:T(8,128)S(1)}, f32[128,256]{1,0:T(8,128)S(1)}, u32[]{:S(2)}, u32[]{:S(2)}) collective-permute-start(f32[128,256]{1,0:T(8,128)S(1)} %bitcast_add_fusion.3), channel_id=1, source_target_pairs={{0,32},{16,48},{32,64},{48,80},{64,96},{80,112},{96,0},{112,16},{1... | collective-permute-start | bytes 393224 | tf_op jit(solution)/shard_map/ppermute | solution.py:196
  114.8 9.5 %collective-permute-start.3 = (f32[128,256]{1,0:T(8,128)S(1)}, f32[128,256]{1,0:T(8,128)S(1)}, u32[]{:S(2)}, u32[]{:S(2)}) collective-permute-start(f32[128,256]{1,0:T(8,128)S(1)} %bitcast_add_fusion.3), channel_id=1, source_target_pairs={{0,96},{16,112},{32,0},{48,16},{64,32},{80,48},{96,64},{112,80},{1... | collective-permute-start | bytes 393224 | tf_op jit(solution)/shard_map/ppermute | solution.py:196
  169.2 66.2 %collective-permute-start.5 = (f32[128,256]{1,0:T(8,128)S(1)}, f32[128,256]{1,0:T(8,128)S(1)}, u32[]{:S(2)}, u32[]{:S(2)}) collective-permute-start(f32[128,256]{1,0:T(8,128)S(1)} %dynamic-slice_bitcast_fusion.2), channel_id=1, source_target_pairs={{0,16},{16,0},{32,48},{48,32},{64,80},{80,64},{96,112},{112,96},{1... | collective-permute-start | bytes 393224 | tf_op jit(solution)/shard_map/ppermute | solution.py:192
  225.2 66.0 %all-to-all-start.2 = ((bf16[16,256,256]{2,1,0:T(8,128)(2,1)}), bf16[16,256,256]{2,1,0:T(8,128)(2,1)}, u32[]{:S(2)}, u32[]{:S(2)}) async-start(bf16[16,256,256]{2,1,0:T(8,128)(2,1)} %bitcast.12), calls=%async_computation.3 | async-start | bytes 4194304 | tf_op jit(solution)/shard_map/all_to_all | solution.py:336
  235.3 163.3 %reduce-scatter.5.cloned.1.call-start = ((), (), s32[]{:S(2)}) async-start(), calls=%async_computation.8 | async-start | bytes 9437184 | tf_op jit(solution)/shard_map/reduce_scatter | solution.py:360
  235.4 4.5 collective-permute-start.6
  235.5 4.8 %collective-permute-start.7 = (f32[32,256]{1,0:T(8,128)S(1)}, f32[32,256]{1,0:T(8,128)S(1)}, u32[]{:S(2)}, u32[]{:S(2)}) collective-permute-start(f32[32,256]{1,0:T(8,128)S(1)} %get-tuple-element.13), channel_id=1, source_target_pairs={{0,32},{16,48},{32,64},{48,80},{64,96},{80,112},{96,0},{112,16},{1... | collective-permute-start | bytes 98312 | tf_op jit(solution)/shard_map/ppermute | solution.py:196
  235.6 4.7 %collective-permute-start.8 = (f32[32,256]{1,0:T(8,128)S(1)}, f32[32,256]{1,0:T(8,128)S(1)}, u32[]{:S(2)}, u32[]{:S(2)}) collective-permute-start(f32[32,256]{1,0:T(8,128)S(1)} %get-tuple-element.12), channel_id=1, source_target_pairs={{0,96},{16,112},{32,0},{48,16},{64,32},{80,48},{96,64},{112,80},{1... | collective-permute-start | bytes 98312 | tf_op jit(solution)/shard_map/ppermute | solution.py:196
  240.3 19.9 %collective-permute-start.10 = (f32[32,256]{1,0:T(8,128)S(1)}, f32[32,256]{1,0:T(8,128)S(1)}, u32[]{:S(2)}, u32[]{:S(2)}) collective-permute-start(f32[32,256]{1,0:T(8,128)S(1)} %fusion.5), channel_id=1, source_target_pairs={{0,4},{1,5},{2,6},{3,7},{4,8},{5,9},{6,10},{7,11},{8,12},{9,13},{1... | collective-permute-start | bytes 98312 | tf_op jit(solution)/shard_map/ppermute | solution.py:200
  241.7 18.8 %collective-permute-start.11 = (f32[32,256]{1,0:T(8,128)S(1)}, f32[32,256]{1,0:T(8,128)S(1)}, u32[]{:S(2)}, u32[]{:S(2)}) collective-permute-start(f32[32,256]{1,0:T(8,128)S(1)} %fusion.5), channel_id=1, source_target_pairs={{0,12},{1,13},{2,14},{3,15},{4,0},{5,1},{6,2},{7,3},{8,4},{9,5},{1... | collective-permute-start | bytes 98312 | tf_op jit(solution)/shard_map/ppermute | solution.py:200
  243.1 19.3 %collective-permute-start.9 = (f32[32,256]{1,0:T(8,128)S(1)}, f32[32,256]{1,0:T(8,128)S(1)}, u32[]{:S(2)}, u32[]{:S(2)}) collective-permute-start(f32[32,256]{1,0:T(8,128)S(1)} %fusion.5), channel_id=1, source_target_pairs={{0,8},{1,9},{2,10},{3,11},{4,12},{5,13},{6,14},{7,15},{8,0},{9,1},... | collective-permute-start | bytes 98312 | tf_op jit(solution)/shard_map/ppermute | solution.py:200
  262.4 5.2 %collective-permute-start.12 = (f32[32,256]{1,0:T(8,128)S(1)}, f32[32,256]{1,0:T(8,128)S(1)}, u32[]{:S(2)}, u32[]{:S(2)}) collective-permute-start(f32[32,256]{1,0:T(8,128)S(1)} %add_add_fusion.5), channel_id=1, source_target_pairs={{0,2},{1,3},{2,0},{3,1},{4,6},{5,7},{6,4},{7,5},{8,10},{9,11},{10,... | collective-permute-start | bytes 98312 | tf_op jit(solution)/shard_map/ppermute | solution.py:204
  265.0 4.3 collective-permute-start.13
  265.2 4.1 collective-permute-start.14
  269.3 4.0 collective-permute-start.15
  269.9 4.4 collective-permute-start.16
  347.9 6.9 %collective-permute-start.20 = (f32[128,256]{1,0:T(8,128)S(1)}, f32[128,256]{1,0:T(8,128)S(1)}, u32[]{:S(2)}, u32[]{:S(2)}) collective-permute-start(f32[128,256]{1,0:T(8,128)S(1)} %bitcast_add_fusion.1), channel_id=1, source_target_pairs={{0,64},{16,80},{32,96},{48,112},{64,0},{80,16},{96,32},{112,48},{1... | collective-permute-start | bytes 393224 | tf_op jit(solution)/shard_map/ppermute | solution.py:196
  350.5 9.3 %collective-permute-start.21 = (f32[128,256]{1,0:T(8,128)S(1)}, f32[128,256]{1,0:T(8,128)S(1)}, u32[]{:S(2)}, u32[]{:S(2)}) collective-permute-start(f32[128,256]{1,0:T(8,128)S(1)} %bitcast_add_fusion.1), channel_id=1, source_target_pairs={{0,32},{16,48},{32,64},{48,80},{64,96},{80,112},{96,0},{112,16},{1... | collective-permute-start | bytes 393224 | tf_op jit(solution)/shard_map/ppermute | solution.py:196
  354.5 9.4 %collective-permute-start.22 = (f32[128,256]{1,0:T(8,128)S(1)}, f32[128,256]{1,0:T(8,128)S(1)}, u32[]{:S(2)}, u32[]{:S(2)}) collective-permute-start(f32[128,256]{1,0:T(8,128)S(1)} %bitcast_add_fusion.1), channel_id=1, source_target_pairs={{0,96},{16,112},{32,0},{48,16},{64,32},{80,48},{96,64},{112,80},{1... | collective-permute-start | bytes 393224 | tf_op jit(solution)/shard_map/ppermute | solution.py:196
  405.9 5.2 %collective-permute-start.25 = (f32[32,256]{1,0:T(8,128)S(1)}, f32[32,256]{1,0:T(8,128)S(1)}, u32[]{:S(2)}, u32[]{:S(2)}) collective-permute-start(f32[32,256]{1,0:T(8,128)S(1)} %get-tuple-element.11), channel_id=1, source_target_pairs={{0,64},{16,80},{32,96},{48,112},{64,0},{80,16},{96,32},{112,48},{1... | collective-permute-start | bytes 98312 | tf_op jit(solution)/shard_map/ppermute | solution.py:196
  408.4 4.0 collective-permute-start.26
  408.4 4.0 collective-permute-start.27
  412.4 4.8 %collective-permute-start.28 = (f32[32,256]{1,0:T(8,128)S(1)}, f32[32,256]{1,0:T(8,128)S(1)}, u32[]{:S(2)}, u32[]{:S(2)}) collective-permute-start(f32[32,256]{1,0:T(8,128)S(1)} %fusion.4), channel_id=1, source_target_pairs={{0,8},{1,9},{2,10},{3,11},{4,12},{5,13},{6,14},{7,15},{8,0},{9,1},... | collective-permute-start | bytes 98312 | tf_op jit(solution)/shard_map/ppermute | solution.py:200
  414.5 4.3 collective-permute-start.29
  418.8 4.3 collective-permute-start.31
  424.4 4.0 collective-permute-start.34
  424.5 4.9 %collective-permute-start.35 = (f32[32,256]{1,0:T(8,128)S(1)}, f32[32,256]{1,0:T(8,128)S(1)}, u32[]{:S(2)}, u32[]{:S(2)}) collective-permute-start(f32[32,256]{1,0:T(8,128)S(1)} %add_add_fusion.2), channel_id=1, source_target_pairs={{0,64},{16,80},{32,96},{48,112},{64,0},{80,16},{96,32},{112,48},{1... | collective-permute-start | bytes 98312 | tf_op jit(solution)/shard_map/ppermute | solution.py:196
  431.1 7.7 %collective-permute-start.37 = (f32[128,256]{1,0:T(8,128)S(1)}, f32[128,256]{1,0:T(8,128)S(1)}, u32[]{:S(2)}, u32[]{:S(2)}) collective-permute-start(f32[128,256]{1,0:T(8,128)S(1)} %bitcast.114), channel_id=1, source_target_pairs={{0,16},{16,0},{32,48},{48,32},{64,80},{80,64},{96,112},{112,96},{1... | collective-permute-start | bytes 393224 | tf_op jit(solution)/shard_map/ppermute | solution.py:192
  (19 other events, 110.0 us)
Sparse Core Ops, SparseCore 0:
  106.2 56.0 reduce-scatter.2
  165.8 50.2 all-gather.1
  341.3 57.2 reduce-scatter.4

commit v3 on v2

--- a/solution.py
+++ b/solution.py
@@ -362,6 +362,7 @@
         word_factor = whitener(sum_all(gram_of(z)) / words)
         if turn + 1 < ITERS:
             wide = lax.all_gather(z.astype(jnp.bfloat16), "author", axis=0, tiled=True)
+            wide, word_factor = lax.optimization_barrier((wide, word_factor))
     author_basis = apply_t(y, author_factor).astype(jnp.bfloat16)
     word_basis = apply_t(z, word_factor).astype(jnp.bfloat16)
     return (author_basis, word_basis)

time: 470 us -> 439 us (0.934)
  waiting for transfers between devices: 170 us -> 114 us
  blocking collectives: 74.1 us -> 91.5 us
  starting transfers between devices: 71.6 us -> 88.2 us
  Pallas kernels: 88.3 us -> 79.5 us
    all_gather x1, waiting for transfers between devices: 45.2 us -> 0.01 us  [shards(): wide = lax.all_gather(z.astype(jnp.bfloat16), 'author', axis=0, tiled=True)]
    all_to_all x2 -> x3, blocking collectives: 74.1 us -> 91.5 us  [swap_word(): return lax.all_to_all(parts, 'word', 0, 0)]
    ppermute x8, starting transfers between devices: 12.9 us -> 28.9 us  [hop_core(): return lax.ppermute(array, 'author', [(i, i ^ 1) for i in range(8)])]
    ppermute x18, starting transfers between devices: 26 us -> 39.7 us  [hop_x(): lax.ppermute(array, 'author', [(i, (i + 2 * k) % 8) for i in range(8)])]
    ppermute x6, waiting for transfers between devices: 19.3 us -> 7.87 us  [hop_y(): lax.ppermute(array, 'word', [(i, (i + 4 * k) % 16) for i in range(16)])]
    all_to_all x2 -> x1, starting transfers between devices: 14 us -> 3.85 us  [swap_word(): return lax.all_to_all(parts, 'word', 0, 0)]
    pallas_call x4, Pallas kernels: 34.1 us -> 25.2 us  [product(): pl.pallas_call(kernel, out_shape=out_shape, in_specs=[smem, smem, smem, w...]
    all_to_all x2 -> x1, waiting for transfers between devices: 29.5 us -> 22.8 us  [swap_word(): return lax.all_to_all(parts, 'word', 0, 0)]
  transfers between devices with their start and end apart: 43 -> 42, of which waited for: 31 -> 30; matrix products, arithmetic and copies ran while one was open for 4% -> 4% of each run, Pallas kernels for 10% -> 9%
where the time goes in v3:
time: 439 us; the launch traced here: 432 us
  waiting for transfers between devices  114 us (26%)
  blocking collectives  91.5 us (21%)
  starting transfers between devices  88.2 us (20%)
  Pallas kernels  79.5 us (18%)
  matrix products  21.9 us (5%)
  local copies, waits for them, and re-layouts  17.1 us (4%)
  between operations  15.3 us (3%)
    all_to_all x3, blocking collectives, swap_word(): return lax.all_to_all(parts, 'word', 0, 0)  91.5 us
    pallas_call x4, Pallas kernels, whitener(): pl.pallas_call(whiten_kernel, out_shape=jax.ShapeDtypeStruct(gram.shape,...  49.2 us
    reduce_scatter x2, waiting for transfers between devices, shards(): lax.psum_scatter(terms, 'author', scatter_dimension=0, tiled=True)  46.5 us
    ppermute x18, starting transfers between devices, hop_x(): lax.ppermute(array, 'author', [(i, (i + 2 * k) % 8) for i in range(8)])  39.7 us
    ppermute x8, starting transfers between devices, hop_core(): return lax.ppermute(array, 'author', [(i, i ^ 1) for i in range(8)])  28.9 us
    pallas_call x4, Pallas kernels, product(): pl.pallas_call(kernel, out_shape=out_shape, in_specs=[smem, smem, smem, w...  25.2 us
    ppermute x18, waiting for transfers between devices, hop_x(): lax.ppermute(array, 'author', [(i, (i + 2 * k) % 8) for i in range(8)])  24.6 us
    all_to_all x1, waiting for transfers between devices, swap_word(): return lax.all_to_all(parts, 'word', 0, 0)  22.8 us
  transfers between devices with their start and end apart: 42, of which 30 were waited for; matrix products, arithmetic and copies ran while one was open for 4% of the time, Pallas kernels for 9%

profile of v3, /device:TPU:1, one launch (start us, length us, event | category | flops | bytes accessed | tf_op | source)
XLA Modules:
  0.0 431.7 jit_solution(17180983483574396340)
XLA Ops:
  9.1 5.8 %product.2 = bf16[4096,256]{1,0:T(8,128)(2,1)S(1)} custom-call(s32[128]{0:T(128)S(1)} %bitcast.101, s32[128]{0:T(128)S(1)} %compare_select_fusion.4.dst_ids, s32[1]{0:T(128)} %bitcast.89.count, bf16[128,128,128]{2,1,0:T(8,128)(2,1)} %bitcast.105, bf16[16384,256]{1,0:T(8,128)(2,1)} %panel.1), custom_call_target="tpu_custom_call" | custom-call | flops 1073741824 | bytes 14680064 | tf_op jit(solution)/shard_map/product/pallas_call | solution.py:141
  15.0 33.6 %all_to_all.20.p = bf16[16,256,256]{2,1,0:T(8,128)(2,1)} all-to-all(bf16[16,256,256]{2,1,0:T(8,128)(2,1)S(1)} %bitcast.100), channel_id=1, replica_groups=mesh['author'=8,'word'=16] {'word'}, dimensions={0} | all-to-all | bytes 4194304 | tf_op jit(solution)/shard_map/all_to_all | solution.py:336
  52.6 3.8 all-to-all-start.1
  56.6 22.8 %all-to-all-done.1 = bf16[16,256,256]{2,1,0:T(8,128)(2,1)S(1)} async-done(((bf16[16,256,256]{2,1,0:T(8,128)(2,1)}), bf16[16,256,256]{2,1,0:T(8,128)(2,1)S(1)}, u32[]{:S(2)}, u32[]{:S(2)}) %all-to-all-start.1) | async-done | bytes 2097184 | tf_op jit(solution)/shard_map/all_to_all | solution.py:336
  79.4 6.8 %product_t.2 = bf16[16384,256]{1,0:T(8,128)(2,1)S(1)} custom-call(s32[128]{0:T(128)S(1)} %bitcast.103, s32[128]{0:T(128)S(1)} %compare_select_fusion.3.dst_ids, s32[1]{0:T(128)} %bitcast.90.count, bf16[128,128,128]{2,1,0:T(8,128)(2,1)} %bitcast.106, bf16[4096,256]{1,0:T(8,128)(2,1)S(1)} %bitcast.93), custom_call_target="tpu_custom_call" | custom-call | flops 1073741824 | bytes 14680064 | tf_op jit(solution)/shard_map/product_t/pallas_call | solution.py:141
  86.2 3.3 copy-done
  89.6 3.0 copy.9
  94.9 6.8 %collective-permute-start = (f32[128,256]{1,0:T(8,128)S(1)}, f32[128,256]{1,0:T(8,128)S(1)}, u32[]{:S(2)}, u32[]{:S(2)}) collective-permute-start(f32[128,256]{1,0:T(8,128)S(1)} %dynamic-slice_bitcast_fusion.3), channel_id=1, source_target_pairs={{0,16},{16,0},{32,48},{48,32},{64,80},{80,64},{96,112},{112,96},{1... | collective-permute-start | bytes 393224 | tf_op jit(solution)/shard_map/ppermute | solution.py:192
  102.7 12.9 %collective-permute-start.2 = (f32[128,256]{1,0:T(8,128)S(1)}, f32[128,256]{1,0:T(8,128)S(1)}, u32[]{:S(2)}, u32[]{:S(2)}) collective-permute-start(f32[128,256]{1,0:T(8,128)S(1)} %bitcast_add_fusion.3), channel_id=1, source_target_pairs={{0,32},{16,48},{32,64},{48,80},{64,96},{80,112},{96,0},{112,16},{1... | collective-permute-start | bytes 393224 | tf_op jit(solution)/shard_map/ppermute | solution.py:196
  126.9 12.3 %whitener.4 = f32[256,256]{1,0:T(8,128)} custom-call(f32[256,256]{1,0:T(8,128)} %fusion.g_ref), custom_call_target="tpu_custom_call" | custom-call | flops 1000000000 | bytes 40000000 | tf_op jit(solution)/shard_map/whitener/pallas_call | solution.py:320
  139.2 25.0 %reduce-scatter.3.cloned.1.call-done = bf16[2048,256]{1,0:T(8,128)(2,1)} async-done(((bf16[16384,256]{1,0:T(8,128)(2,1)}), bf16[2048,256]{1,0:T(8,128)(2,1)}) %reduce-scatter.3.cloned.1.call-update) | async-done | bytes 1048592 | tf_op jit(solution)/shard_map/reduce_scatter | solution.py:360
  164.2 3.3 fusion.7
  167.5 3.5 fusion.9
  195.9 3.5 collective-permute-done.16
  200.5 6.5 %collective-permute-start.18 = (f32[128,256]{1,0:T(8,128)S(1)}, f32[128,256]{1,0:T(8,128)S(1)}, u32[]{:S(2)}, u32[]{:S(2)}) collective-permute-start(f32[128,256]{1,0:T(8,128)S(1)} %bitcast.117), channel_id=1, source_target_pairs={{0,16},{16,0},{32,48},{48,32},{64,80},{80,64},{96,112},{112,96},{1... | collective-permute-start | bytes 393224 | tf_op jit(solution)/shard_map/ppermute | solution.py:192
  208.7 12.3 %whitener.5.factor = f32[256,256]{1,0:T(8,128)} custom-call(f32[256,256]{1,0:T(8,128)} %fusion.1.g_ref), custom_call_target="tpu_custom_call" | custom-call | flops 1000000000 | bytes 40000000 | tf_op jit(solution)/shard_map/whitener/pallas_call | solution.py:320
  221.0 5.8 %product.3 = bf16[4096,256]{1,0:T(8,128)(2,1)S(1)} custom-call(s32[128]{0:T(128)S(1)} %bitcast.102, s32[128]{0:T(128)S(1)} %compare_select_fusion.4.dst_ids, s32[1]{0:T(128)} %bitcast.91.count, bf16[128,128,128]{2,1,0:T(8,128)(2,1)} %bitcast.107, bf16[16384,256]{1,0:T(8,128)(2,1)} %all-gather.2.cloned.1.call-done.panel), custom_call_target="tpu_custom_call" | custom-call | flops 1073741824 | bytes 14680064 | tf_op jit(solution)/shard_map/product/pallas_call | solution.py:141
  226.8 30.7 %all_to_all.21.parts = bf16[16,256,256]{2,1,0:T(8,128)(2,1)} all-to-all(bf16[16,256,256]{2,1,0:T(8,128)(2,1)S(1)} %bitcast.99), channel_id=1, replica_groups=mesh['author'=8,'word'=16] {'word'}, dimensions={0} | all-to-all | bytes 4194304 | tf_op jit(solution)/shard_map/all_to_all | solution.py:336
  261.3 27.2 %all_to_all.22 = bf16[16,256,256]{2,1,0:T(8,128)(2,1)S(1)} all-to-all(bf16[16,256,256]{2,1,0:T(8,128)(2,1)} %copy-done.3), channel_id=1, replica_groups=mesh['author'=8,'word'=16] {'word'}, dimensions={0} | all-to-all | bytes 4194304 | tf_op jit(solution)/shard_map/all_to_all | solution.py:336
  288.5 6.8 %product_t.3 = bf16[16384,256]{1,0:T(8,128)(2,1)S(1)} custom-call(s32[128]{0:T(128)S(1)} %bitcast.104, s32[128]{0:T(128)S(1)} %compare_select_fusion.3.dst_ids, s32[1]{0:T(128)} %bitcast.92.count, bf16[128,128,128]{2,1,0:T(8,128)(2,1)} %bitcast.108, bf16[4096,256]{1,0:T(8,128)(2,1)S(1)} %bitcast.96), custom_call_target="tpu_custom_call" | custom-call | flops 1073741824 | bytes 14680064 | tf_op jit(solution)/shard_map/product_t/pallas_call | solution.py:141
  295.3 3.3 copy-done.1
  298.6 3.0 copy.10
  303.9 6.0 %collective-permute-start.19 = (f32[128,256]{1,0:T(8,128)S(1)}, f32[128,256]{1,0:T(8,128)S(1)}, u32[]{:S(2)}, u32[]{:S(2)}) collective-permute-start(f32[128,256]{1,0:T(8,128)S(1)} %dynamic-slice_bitcast_fusion.1), channel_id=1, source_target_pairs={{0,16},{16,0},{32,48},{48,32},{64,80},{80,64},{96,112},{112,96},{1... | collective-permute-start | bytes 393224 | tf_op jit(solution)/shard_map/ppermute | solution.py:192
  310.9 8.4 %collective-permute-start.21 = (f32[128,256]{1,0:T(8,128)S(1)}, f32[128,256]{1,0:T(8,128)S(1)}, u32[]{:S(2)}, u32[]{:S(2)}) collective-permute-start(f32[128,256]{1,0:T(8,128)S(1)} %bitcast_add_fusion.1), channel_id=1, source_target_pairs={{0,32},{16,48},{32,64},{48,80},{64,96},{80,112},{96,0},{112,16},{1... | collective-permute-start | bytes 393224 | tf_op jit(solution)/shard_map/ppermute | solution.py:196
  331.0 12.3 %whitener.6 = f32[256,256]{1,0:T(8,128)} custom-call(f32[256,256]{1,0:T(8,128)} %fusion.2.g_ref), custom_call_target="tpu_custom_call" | custom-call | flops 1000000000 | bytes 40000000 | tf_op jit(solution)/shard_map/whitener/pallas_call | solution.py:320
  343.3 21.5 %reduce-scatter.5.cloned.1.call-done = bf16[2048,256]{1,0:T(8,128)(2,1)} async-done(((bf16[16384,256]{1,0:T(8,128)(2,1)}), bf16[2048,256]{1,0:T(8,128)(2,1)}) %reduce-scatter.5.cloned.1.call-update) | async-done | bytes 1048592 | tf_op jit(solution)/shard_map/reduce_scatter | solution.py:360
  367.0 3.5 fusion.12
  381.9 3.1 collective-permute-done.28
  395.9 3.3 collective-permute-done.35
  399.9 7.0 %collective-permute-start.37 = (f32[128,256]{1,0:T(8,128)S(1)}, f32[128,256]{1,0:T(8,128)S(1)}, u32[]{:S(2)}, u32[]{:S(2)}) collective-permute-start(f32[128,256]{1,0:T(8,128)S(1)} %bitcast.115), channel_id=1, source_target_pairs={{0,16},{16,0},{32,48},{48,32},{64,80},{80,64},{96,112},{112,96},{1... | collective-permute-start | bytes 393224 | tf_op jit(solution)/shard_map/ppermute | solution.py:192
  408.7 12.3 %whitener.7 = f32[256,256]{1,0:T(8,128)} custom-call(f32[256,256]{1,0:T(8,128)} %fusion.3.g_ref), custom_call_target="tpu_custom_call" | custom-call | flops 1000000000 | bytes 40000000 | tf_op jit(solution)/shard_map/whitener/pallas_call | solution.py:320
  421.0 3.8 convolution_convert_fusion
  (127 shorter events, 93.3 us)
Async XLA Ops:
  52.6 26.8 %all-to-all-start.1 = ((bf16[16,256,256]{2,1,0:T(8,128)(2,1)}), bf16[16,256,256]{2,1,0:T(8,128)(2,1)S(1)}, u32[]{:S(2)}, u32[]{:S(2)}) async-start(bf16[16,256,256]{2,1,0:T(8,128)(2,1)} %copy-done.2), calls=%async_computation.1 | async-start | bytes 4194304 | tf_op jit(solution)/shard_map/all_to_all | solution.py:336
  56.5 107.7 %reduce-scatter.3.cloned.1.call-start = ((), (), s32[]{:S(2)}) async-start(), calls=%async_computation.6 | async-start | bytes 9437184 | tf_op jit(solution)/shard_map/reduce_scatter | solution.py:360
  89.5 131.5 %all-gather.2.cloned.1.call-start = ((), (), s32[]{:S(2)}) async-start(), calls=%async_computation.7 | async-start | bytes 9437184 | tf_op jit(solution)/shard_map/all_gather | solution.py:364
  94.9 7.8 %collective-permute-start = (f32[128,256]{1,0:T(8,128)S(1)}, f32[128,256]{1,0:T(8,128)S(1)}, u32[]{:S(2)}, u32[]{:S(2)}) collective-permute-start(f32[128,256]{1,0:T(8,128)S(1)} %dynamic-slice_bitcast_fusion.3), channel_id=1, source_target_pairs={{0,16},{16,0},{32,48},{48,32},{64,80},{80,64},{96,112},{112,96},{1... | collective-permute-start | bytes 393224 | tf_op jit(solution)/shard_map/ppermute | solution.py:192
  102.7 17.1 %collective-permute-start.2 = (f32[128,256]{1,0:T(8,128)S(1)}, f32[128,256]{1,0:T(8,128)S(1)}, u32[]{:S(2)}, u32[]{:S(2)}) collective-permute-start(f32[128,256]{1,0:T(8,128)S(1)} %bitcast_add_fusion.3), channel_id=1, source_target_pairs={{0,32},{16,48},{32,64},{48,80},{64,96},{80,112},{96,0},{112,16},{1... | collective-permute-start | bytes 393224 | tf_op jit(solution)/shard_map/ppermute | solution.py:196
  115.6 6.5 %collective-permute-start.3 = (f32[128,256]{1,0:T(8,128)S(1)}, f32[128,256]{1,0:T(8,128)S(1)}, u32[]{:S(2)}, u32[]{:S(2)}) collective-permute-start(f32[128,256]{1,0:T(8,128)S(1)} %bitcast_add_fusion.3), channel_id=1, source_target_pairs={{0,96},{16,112},{32,0},{48,16},{64,32},{80,48},{96,64},{112,80},{1... | collective-permute-start | bytes 393224 | tf_op jit(solution)/shard_map/ppermute | solution.py:196
  115.6 8.4 %collective-permute-start.1 = (f32[128,256]{1,0:T(8,128)S(1)}, f32[128,256]{1,0:T(8,128)S(1)}, u32[]{:S(2)}, u32[]{:S(2)}) collective-permute-start(f32[128,256]{1,0:T(8,128)S(1)} %bitcast_add_fusion.3), channel_id=1, source_target_pairs={{0,64},{16,80},{32,96},{48,112},{64,0},{80,16},{96,32},{112,48},{1... | collective-permute-start | bytes 393224 | tf_op jit(solution)/shard_map/ppermute | solution.py:196
  167.5 197.2 %reduce-scatter.5.cloned.1.call-start = ((), (), s32[]{:S(2)}) async-start(), calls=%async_computation.8 | async-start | bytes 9437184 | tf_op jit(solution)/shard_map/reduce_scatter | solution.py:360
  172.5 4.3 %collective-permute-start.6 = (f32[32,256]{1,0:T(8,128)S(1)}, f32[32,256]{1,0:T(8,128)S(1)}, u32[]{:S(2)}, u32[]{:S(2)}) collective-permute-start(f32[32,256]{1,0:T(8,128)S(1)} %get-tuple-element.18), channel_id=1, source_target_pairs={{0,64},{16,80},{32,96},{48,112},{64,0},{80,16},{96,32},{112,48},{1... | collective-permute-start | bytes 98312 | tf_op jit(solution)/shard_map/ppermute | solution.py:196
  173.4 4.5 %collective-permute-start.7 = (f32[32,256]{1,0:T(8,128)S(1)}, f32[32,256]{1,0:T(8,128)S(1)}, u32[]{:S(2)}, u32[]{:S(2)}) collective-permute-start(f32[32,256]{1,0:T(8,128)S(1)} %get-tuple-element.17), channel_id=1, source_target_pairs={{0,32},{16,48},{32,64},{48,80},{64,96},{80,112},{96,0},{112,16},{1... | collective-permute-start | bytes 98312 | tf_op jit(solution)/shard_map/ppermute | solution.py:196
  177.9 4.4 %collective-permute-start.10 = (f32[32,256]{1,0:T(8,128)S(1)}, f32[32,256]{1,0:T(8,128)S(1)}, u32[]{:S(2)}, u32[]{:S(2)}) collective-permute-start(f32[32,256]{1,0:T(8,128)S(1)} %fusion.5), channel_id=1, source_target_pairs={{0,4},{1,5},{2,6},{3,7},{4,8},{5,9},{6,10},{7,11},{8,12},{9,13},{1... | collective-permute-start | bytes 98312 | tf_op jit(solution)/shard_map/ppermute | solution.py:200
  177.9 4.4 %collective-permute-start.11 = (f32[32,256]{1,0:T(8,128)S(1)}, f32[32,256]{1,0:T(8,128)S(1)}, u32[]{:S(2)}, u32[]{:S(2)}) collective-permute-start(f32[32,256]{1,0:T(8,128)S(1)} %fusion.5), channel_id=1, source_target_pairs={{0,12},{1,13},{2,14},{3,15},{4,0},{5,1},{6,2},{7,3},{8,4},{9,5},{1... | collective-permute-start | bytes 98312 | tf_op jit(solution)/shard_map/ppermute | solution.py:200
  180.6 4.3 collective-permute-start.9
  184.9 5.0 %collective-permute-start.13 = (f32[32,256]{1,0:T(8,128)S(1)}, f32[32,256]{1,0:T(8,128)S(1)}, u32[]{:S(2)}, u32[]{:S(2)}) collective-permute-start(f32[32,256]{1,0:T(8,128)S(1)} %add_add_fusion.5), channel_id=1, source_target_pairs={{0,1},{1,2},{2,3},{3,0},{4,5},{5,6},{6,7},{7,4},{8,9},{9,10},{10,1... | collective-permute-start | bytes 98312 | tf_op jit(solution)/shard_map/ppermute | solution.py:204
  185.0 4.9 %collective-permute-start.14 = (f32[32,256]{1,0:T(8,128)S(1)}, f32[32,256]{1,0:T(8,128)S(1)}, u32[]{:S(2)}, u32[]{:S(2)}) collective-permute-start(f32[32,256]{1,0:T(8,128)S(1)} %add_add_fusion.5), channel_id=1, source_target_pairs={{0,3},{1,0},{2,1},{3,2},{4,7},{5,4},{6,5},{7,6},{8,11},{9,8},{10,9... | collective-permute-start | bytes 98312 | tf_op jit(solution)/shard_map/ppermute | solution.py:204
  187.7 4.3 collective-permute-start.12
  194.4 5.0 %collective-permute-start.16 = (f32[32,256]{1,0:T(8,128)S(1)}, f32[32,256]{1,0:T(8,128)S(1)}, u32[]{:S(2)}, u32[]{:S(2)}) collective-permute-start(f32[32,256]{1,0:T(8,128)S(1)} %add_add_fusion.4), channel_id=1, source_target_pairs={{0,64},{16,80},{32,96},{48,112},{64,0},{80,16},{96,32},{112,48},{1... | collective-permute-start | bytes 98312 | tf_op jit(solution)/shard_map/ppermute | solution.py:196
  194.4 5.4 %collective-permute-start.15 = (f32[32,256]{1,0:T(8,128)S(1)}, f32[32,256]{1,0:T(8,128)S(1)}, u32[]{:S(2)}, u32[]{:S(2)}) collective-permute-start(f32[32,256]{1,0:T(8,128)S(1)} %add_add_fusion.4), channel_id=1, source_target_pairs={{0,32},{16,48},{32,64},{48,80},{64,96},{80,112},{96,0},{112,16},{1... | collective-permute-start | bytes 98312 | tf_op jit(solution)/shard_map/ppermute | solution.py:196
  200.5 7.5 %collective-permute-start.18 = (f32[128,256]{1,0:T(8,128)S(1)}, f32[128,256]{1,0:T(8,128)S(1)}, u32[]{:S(2)}, u32[]{:S(2)}) collective-permute-start(f32[128,256]{1,0:T(8,128)S(1)} %bitcast.117), channel_id=1, source_target_pairs={{0,16},{16,0},{32,48},{48,32},{64,80},{80,64},{96,112},{112,96},{1... | collective-permute-start | bytes 393224 | tf_op jit(solution)/shard_map/ppermute | solution.py:192
  303.9 7.0 %collective-permute-start.19 = (f32[128,256]{1,0:T(8,128)S(1)}, f32[128,256]{1,0:T(8,128)S(1)}, u32[]{:S(2)}, u32[]{:S(2)}) collective-permute-start(f32[128,256]{1,0:T(8,128)S(1)} %dynamic-slice_bitcast_fusion.1), channel_id=1, source_target_pairs={{0,16},{16,0},{32,48},{48,32},{64,80},{80,64},{96,112},{112,96},{1... | collective-permute-start | bytes 393224 | tf_op jit(solution)/shard_map/ppermute | solution.py:192
  310.9 12.8 %collective-permute-start.21 = (f32[128,256]{1,0:T(8,128)S(1)}, f32[128,256]{1,0:T(8,128)S(1)}, u32[]{:S(2)}, u32[]{:S(2)}) collective-permute-start(f32[128,256]{1,0:T(8,128)S(1)} %bitcast_add_fusion.1), channel_id=1, source_target_pairs={{0,32},{16,48},{32,64},{48,80},{64,96},{80,112},{96,0},{112,16},{1... | collective-permute-start | bytes 393224 | tf_op jit(solution)/shard_map/ppermute | solution.py:196
  319.3 6.6 %collective-permute-start.22 = (f32[128,256]{1,0:T(8,128)S(1)}, f32[128,256]{1,0:T(8,128)S(1)}, u32[]{:S(2)}, u32[]{:S(2)}) collective-permute-start(f32[128,256]{1,0:T(8,128)S(1)} %bitcast_add_fusion.1), channel_id=1, source_target_pairs={{0,96},{16,112},{32,0},{48,16},{64,32},{80,48},{96,64},{112,80},{1... | collective-permute-start | bytes 393224 | tf_op jit(solution)/shard_map/ppermute | solution.py:196
  319.3 8.6 %collective-permute-start.20 = (f32[128,256]{1,0:T(8,128)S(1)}, f32[128,256]{1,0:T(8,128)S(1)}, u32[]{:S(2)}, u32[]{:S(2)}) collective-permute-start(f32[128,256]{1,0:T(8,128)S(1)} %bitcast_add_fusion.1), channel_id=1, source_target_pairs={{0,64},{16,80},{32,96},{48,112},{64,0},{80,16},{96,32},{112,48},{1... | collective-permute-start | bytes 393224 | tf_op jit(solution)/shard_map/ppermute | solution.py:196
  372.0 4.5 %collective-permute-start.25 = (f32[32,256]{1,0:T(8,128)S(1)}, f32[32,256]{1,0:T(8,128)S(1)}, u32[]{:S(2)}, u32[]{:S(2)}) collective-permute-start(f32[32,256]{1,0:T(8,128)S(1)} %get-tuple-element.15), channel_id=1, source_target_pairs={{0,64},{16,80},{32,96},{48,112},{64,0},{80,16},{96,32},{112,48},{1... | collective-permute-start | bytes 98312 | tf_op jit(solution)/shard_map/ppermute | solution.py:196
  373.8 4.0 collective-permute-start.26
  377.8 4.0 collective-permute-start.29
  380.6 4.4 %collective-permute-start.28 = (f32[32,256]{1,0:T(8,128)S(1)}, f32[32,256]{1,0:T(8,128)S(1)}, u32[]{:S(2)}, u32[]{:S(2)}) collective-permute-start(f32[32,256]{1,0:T(8,128)S(1)} %fusion.4), channel_id=1, source_target_pairs={{0,8},{1,9},{2,10},{3,11},{4,12},{5,13},{6,14},{7,15},{8,0},{9,1},... | collective-permute-start | bytes 98312 | tf_op jit(solution)/shard_map/ppermute | solution.py:200
  385.0 4.2 collective-permute-start.32
  387.8 4.3 collective-permute-start.31
  394.9 4.3 %collective-permute-start.35 = (f32[32,256]{1,0:T(8,128)S(1)}, f32[32,256]{1,0:T(8,128)S(1)}, u32[]{:S(2)}, u32[]{:S(2)}) collective-permute-start(f32[32,256]{1,0:T(8,128)S(1)} %add_add_fusion.2), channel_id=1, source_target_pairs={{0,64},{16,80},{32,96},{48,112},{64,0},{80,16},{96,32},{112,48},{1... | collective-permute-start | bytes 98312 | tf_op jit(solution)/shard_map/ppermute | solution.py:196
  394.9 4.3 %collective-permute-start.34 = (f32[32,256]{1,0:T(8,128)S(1)}, f32[32,256]{1,0:T(8,128)S(1)}, u32[]{:S(2)}, u32[]{:S(2)}) collective-permute-start(f32[32,256]{1,0:T(8,128)S(1)} %add_add_fusion.2), channel_id=1, source_target_pairs={{0,32},{16,48},{32,64},{48,80},{64,96},{80,112},{96,0},{112,16},{1... | collective-permute-start | bytes 98312 | tf_op jit(solution)/shard_map/ppermute | solution.py:196
  399.9 8.1 %collective-permute-start.37 = (f32[128,256]{1,0:T(8,128)S(1)}, f32[128,256]{1,0:T(8,128)S(1)}, u32[]{:S(2)}, u32[]{:S(2)}) collective-permute-start(f32[128,256]{1,0:T(8,128)S(1)} %bitcast.115), channel_id=1, source_target_pairs={{0,16},{16,0},{32,48},{48,32},{64,80},{80,64},{96,112},{112,96},{1... | collective-permute-start | bytes 393224 | tf_op jit(solution)/shard_map/ppermute | solution.py:192
  (18 other events, 105.4 us)
Sparse Core Ops, SparseCore 0:
  89.6 74.5 reduce-scatter.2
  167.6 51.0 all-gather.1
  298.7 65.9 reduce-scatter.4

commit v4 on v2

--- a/solution.py
+++ b/solution.py
@@ -6,29 +6,23 @@
 from jax.sharding import PartitionSpec as P
 
 ITERS = 2
-GROUP = 4
-AHEAD = 8
+GROUP = 16
+CUT = 2048
 BLOCK = 64
 HIGH = lax.Precision.HIGHEST
-
-
-def product_kernel(src_ids, dst_ids, count, values, panel, out, total, part, source, part_sem, source_sem):
+MIDDLE = lax.Precision.HIGH
+
+
+def product_kernel(src_ids, dst_ids, count, values, given, out, total, part, panel, part_sem, panel_sem):
     size = part.shape[1]
     groups = (count[0] + GROUP - 1) // GROUP
 
-    def copies(group):
-        first = group * GROUP
-        yield pltpu.make_async_copy(
-            values.at[pl.ds(first, GROUP)], part.at[pl.ds(first, GROUP)], part_sem.at[group]
-        )
-        for offset in range(GROUP):
-            slot = first + offset
-            rows = pl.ds(pl.multiple_of(src_ids[slot] * size, size), size)
-            yield pltpu.make_async_copy(panel.at[rows], source.at[slot], source_sem.at[slot])
+    def fetch(group):
+        span = pl.ds(group * GROUP, GROUP)
+        return pltpu.make_async_copy(values.at[span], part.at[span], part_sem.at[group])
 
     def start(group, carry):
-        for copy in copies(group):
-            copy.start()
+        fetch(group).start()
         return carry
 
     def clear(index, carry):
@@ -36,17 +30,12 @@
         return carry
 
     def work(group, carry):
-        @pl.when(group + AHEAD < groups)
-        def _():
-            start(group + AHEAD, 0)
-
-        for copy in copies(group):
-            copy.wait()
+        fetch(group).wait()
         first = group * GROUP
-        prods = [
-            jnp.dot(part[first + offset], source[first + offset], preferred_element_type=jnp.float32)
-            for offset in range(GROUP)
-        ]
+        prods = []
+        for offset in range(GROUP):
+            rows = pl.ds(pl.multiple_of(src_ids[first + offset] * size, size), size)
+            prods.append(jnp.dot(part[first + offset], panel[rows, :], preferred_element_type=jnp.float32))
         for offset in range(GROUP):
             total[dst_ids[first + offset]] += prods[offset]
         return carry
@@ -55,8 +44,17 @@
         out[pl.ds(pl.multiple_of(index * size, size), size), :] = total[index].astype(out.dtype)
         return carry
 
-    lax.fori_loop(0, jnp.minimum(AHEAD, groups), start, 0)
+    moves = []
+    for index in range(panel_sem.shape[0]):
+        rows = pl.ds(index * CUT, CUT)
+        moves.append(pltpu.make_async_copy(given.at[rows], panel.at[rows], panel_sem.at[index]))
+    fetch(0).start()
+    for move in moves:
+        move.start()
+    lax.fori_loop(1, groups, start, 0)
     lax.fori_loop(0, total.shape[0], clear, 0)
+    for move in moves:
+        move.wait()
     lax.fori_loop(0, groups, work, 0)
     lax.fori_loop(0, out.shape[0] // size, emit, 0)
 
@@ -114,44 +112,61 @@
         send.wait()
 
 
-def product(values, src_ids, dst_ids, count, panel, out_blocks, transpose):
+def kernel_call(kernel, name, operands, specs, out, cap, size, scratch):
+    rows, width = out.shape
+    return pl.pallas_call(
+        kernel,
+        out_shape=out,
+        in_specs=specs,
+        out_specs=pl.BlockSpec(memory_space=pltpu.VMEM if name == "product" else pl.ANY),
+        scratch_shapes=[
+            pltpu.VMEM((rows // size + 1, size, width), jnp.float32),
+            pltpu.VMEM((cap, size, size), jnp.bfloat16),
+            *scratch,
+        ],
+        compiler_params=pltpu.CompilerParams(vmem_limit_bytes=36 * 1024 * 1024),
+        cost_estimate=pl.CostEstimate(
+            flops=4 * cap * size * size * width, bytes_accessed=20 * 1024 * 1024, transcendentals=0
+        ),
+        name=name,
+    )(*operands)
+
+
+def product(values, cols, rows, count, panel, out_blocks):
     cap, size, _ = values.shape
     width = panel.shape[1]
-    dst_ids = jnp.where(jnp.arange(cap, dtype=jnp.int32) < count, dst_ids, out_blocks)
+    rows = jnp.where(jnp.arange(cap, dtype=jnp.int32) < count, rows, out_blocks)
     smem = pl.BlockSpec(memory_space=pltpu.SMEM)
-    vmem = pl.BlockSpec(memory_space=pltpu.VMEM)
     whole = pl.BlockSpec(memory_space=pl.ANY)
     values = pltpu.with_memory_space_constraint(values, pltpu.HBM)
-    rows = out_blocks * size
+    panel = pltpu.with_memory_space_constraint(panel, pltpu.HBM)
     scratch = [
-        pltpu.VMEM((out_blocks + 1, size, width), jnp.float32),
-        pltpu.VMEM((cap, size, size), values.dtype),
+        pltpu.VMEM(panel.shape, jnp.bfloat16),
+        pltpu.SemaphoreType.DMA((cap // GROUP,)),
+        pltpu.SemaphoreType.DMA((panel.shape[0] // CUT,)),
     ]
-    if transpose:
-        kernel, panel_spec, out_spec = product_t_kernel, vmem, whole
-        out_shape = jax.ShapeDtypeStruct((rows, width), jnp.bfloat16)
-        scratch += [pltpu.VMEM((rows, width), jnp.bfloat16)]
-        scratch += [pltpu.SemaphoreType.DMA((cap // GROUP,)), pltpu.SemaphoreType.DMA((8,))]
-    else:
-        kernel, panel_spec, out_spec = product_kernel, whole, vmem
-        panel = pltpu.with_memory_space_constraint(panel, pltpu.HBM)
-        out_shape = pltpu.VMEM((rows, width), jnp.bfloat16)
-        scratch += [pltpu.VMEM((cap, size, width), panel.dtype)]
-        scratch += [pltpu.SemaphoreType.DMA((cap // GROUP,)), pltpu.SemaphoreType.DMA((cap,))]
-    return pl.pallas_call(
-        kernel,
-        out_shape=out_shape,
-        in_specs=[smem, smem, smem, whole, panel_spec],
-        out_specs=out_spec,
-        scratch_shapes=scratch,
-        compiler_params=pltpu.CompilerParams(vmem_limit_bytes=36 * 1024 * 1024),
-        cost_estimate=pl.CostEstimate(
-            flops=2 * cap * size * size * width,
-            bytes_accessed=2 * (cap * size * size + panel.size + rows * width),
-            transcendentals=0,
-        ),
-        name="product_t" if transpose else "product",
-    )(src_ids, dst_ids, count.reshape(1), values, panel)
+    operands = (cols, rows, count.reshape(1), values, panel)
+    specs = [smem] * 3 + [whole] * 2
+    out = pltpu.VMEM((out_blocks * size, width), jnp.bfloat16)
+    return kernel_call(product_kernel, "product", operands, specs, out, cap, size, scratch)
+
+
+def product_t(values, rows, cols, count, panel, out_blocks):
+    cap, size, _ = values.shape
+    cols = jnp.where(jnp.arange(cap, dtype=jnp.int32) < count, cols, out_blocks)
+    smem = pl.BlockSpec(memory_space=pltpu.SMEM)
+    whole = pl.BlockSpec(memory_space=pl.ANY)
+    vmem = pl.BlockSpec(memory_space=pltpu.VMEM)
+    values = pltpu.with_memory_space_constraint(values, pltpu.HBM)
+    out = pltpu.HBM((out_blocks * size, panel.shape[1]), jnp.bfloat16)
+    scratch = [
+        pltpu.VMEM(out.shape, jnp.bfloat16),
+        pltpu.SemaphoreType.DMA((cap // GROUP,)),
+        pltpu.SemaphoreType.DMA((8,)),
+    ]
+    operands = (rows, cols, count.reshape(1), values, panel)
+    specs = [smem] * 3 + [whole, vmem]
+    return kernel_call(product_t_kernel, "product_t", operands, specs, out, cap, size, scratch)
 
 
 def fold_kernel(parts, factor, field, copies):
@@ -159,7 +174,7 @@
     for index in range(1, parts.shape[0]):
         total += parts[index].astype(jnp.float32)
     if factor is not None:
-        total = apply_t(total, factor[...])
+        total = apply_t(total, factor[...], HIGH)
     field[...] = total
     short = total.astype(copies.dtype)
     for index in range(copies.shape[0]):
@@ -182,9 +197,29 @@
     )(*operands)
 
 
+def gram_kernel(field, out):
+    total = jnp.zeros(out.shape, jnp.float32)
+    step = 512
+    for start in range(0, field.shape[0], step):
+        part = field[pl.ds(start, step), :]
+        total += lax.dot_general(part, part, (((0,), (0,)), ((), ())), preferred_element_type=jnp.float32)
+    out[...] = total
+
+
+def gram_short(field):
+    vmem = pl.BlockSpec(memory_space=pltpu.VMEM)
+    return pl.pallas_call(
+        gram_kernel,
+        out_shape=jax.ShapeDtypeStruct((field.shape[1],) * 2, jnp.float32),
+        in_specs=[vmem],
+        out_specs=vmem,
+        name="gram_short",
+    )(field)
+
+
 def gram_of(field):
     return lax.dot_general(
-        field, field, (((0,), (0,)), ((), ())), precision=HIGH, preferred_element_type=jnp.float32
+        field, field, (((0,), (0,)), ((), ())), precision=MIDDLE, preferred_element_type=jnp.float32
     )
 
 
@@ -326,14 +361,22 @@
     )(gram)
 
 
-def apply_t(field, inverse):
+def apply_t(field, inverse, precision=MIDDLE):
     return lax.dot_general(
-        field, inverse, (((1,), (1,)), ((), ())), precision=HIGH, preferred_element_type=jnp.float32
+        field, inverse, (((1,), (1,)), ((), ())), precision=precision, preferred_element_type=jnp.float32
     )
 
 
 def swap_word(parts):
     return lax.all_to_all(parts, "word", 0, 0)
+
+
+def short(array):
+    return array.astype(jnp.bfloat16)
+
+
+def long(array):
+    return array.astype(jnp.float32)
 
 
 def shards(block_values, block_rows, block_cols, block_count, omega):
@@ -349,21 +392,20 @@
     wide = omega
     word_factor = None
     for turn in range(ITERS):
-        terms = product(values, cols, rows, count, wide, author_blocks, False)
+        terms = product(values, cols, rows, count, wide, author_blocks)
         y, copies = fold(swap_word(terms.reshape(16, -1, terms.shape[1])), word_factor)
         y_rows = swap_word(copies).reshape(terms.shape)
-        author_factor = whitener(
-            sum_author(lax.dot_general(y_rows, y_rows, (((0,), (0,)), ((), ())), preferred_element_type=jnp.float32))
-            / authors
-        )
-        terms = product(values, rows, cols, count, y_rows, word_blocks, True)
-        z = lax.psum_scatter(terms, "author", scatter_dimension=0, tiled=True).astype(jnp.float32)
+        terms = product_t(values, rows, cols, count, y_rows, word_blocks)
+        z = long(lax.psum_scatter(terms, "author", scatter_dimension=0, tiled=True))
+        author_factor = whitener(sum_author(gram_short(y_rows)) / authors)
         z = apply_t(z, author_factor)
-        word_factor = whitener(sum_all(gram_of(z)) / words)
+        gram = sum_all(gram_of(z)) / words
         if turn + 1 < ITERS:
-            wide = lax.all_gather(z.astype(jnp.bfloat16), "author", axis=0, tiled=True)
-    author_basis = apply_t(y, author_factor).astype(jnp.bfloat16)
-    word_basis = apply_t(z, word_factor).astype(jnp.bfloat16)
+            wide = lax.all_gather(short(z), "author", axis=0, tiled=True)
+            wide, gram = lax.optimization_barrier((wide, gram))
+        word_factor = whitener(gram)
+    author_basis = short(apply_t(y, author_factor))
+    word_basis = short(apply_t(z, word_factor))
     return (author_basis, word_basis)
 
 

time: 470 us -> 416 us (0.89)
  waiting for transfers between devices: 170 us -> 142 us
  local copies, waits for them, and re-layouts: 17.1 us -> 6.36 us
  matrix products: 22 us -> 12.6 us
  blocking collectives: 74.1 us -> 64.8 us
  starting transfers between devices: 71.6 us -> 79.9 us
    all_gather x1, waiting for transfers between devices: 45.2 us -> 9.84 us  [shards(): wide = lax.all_gather(short(z), 'author', axis=0, tiled=True)]
    ppermute x8, starting transfers between devices: 12.9 us -> 27.8 us  [hop_core(): return lax.ppermute(array, 'author', [(i, i ^ 1) for i in range(8)])]
    ppermute x6, waiting for transfers between devices: 19.3 us -> 7.53 us  [hop_y(): lax.ppermute(array, 'word', [(i, (i + 4 * k) % 16) for i in range(16)])]
    all_to_all x2, waiting for transfers between devices: 29.5 us -> 39.1 us  [swap_word(): return lax.all_to_all(parts, 'word', 0, 0)]
    dot_general x8 -> x6, matrix products: 22 us -> 12.6 us  [the longest x4 8.94 us: apply_t(): lax.dot_general(field, inverse, (((1,), (1,)), ((), ())), precision=preci...]
    all_to_all x2, blocking collectives: 74.1 us -> 64.8 us  [swap_word(): return lax.all_to_all(parts, 'word', 0, 0)]
    unnamed x16, local copies, waits for them, and re-layouts: 9.93 us -> 3.35 us
    dot_general x2 -> x0, local copies, waits for them, and re-layouts: 5.91 us -> none  [shards(): lax.dot_general(y_rows, y_rows, (((0,), (0,)), ((), ())), preferred_eleme...]
  transfers between devices with their start and end apart: 43 -> 43, of which waited for: 31 -> 33; matrix products, arithmetic and copies ran while one was open for 4% -> 2% of each run, Pallas kernels for 10% -> 10%
where the time goes in v4:
time: 416 us; the launch traced here: 413 us
  waiting for transfers between devices  142 us (34%)
  Pallas kernels  87.1 us (21%)
  starting transfers between devices  79.9 us (19%)
  blocking collectives  64.8 us (16%)
  between operations  14.7 us (4%)
  matrix products  12.6 us (3%)
  local copies, waits for them, and re-layouts  6.36 us (2%)
  other arithmetic  5.76 us (1%)
    all_to_all x2, blocking collectives, swap_word(): return lax.all_to_all(parts, 'word', 0, 0)  64.8 us
    pallas_call x4, Pallas kernels, whitener(): pl.pallas_call(whiten_kernel, out_shape=jax.ShapeDtypeStruct(gram.shape,...  49.2 us
    reduce_scatter x2, waiting for transfers between devices, shards(): z = long(lax.psum_scatter(terms, 'author', scatter_dimension=0, tiled=True))  42.2 us
    all_to_all x2, waiting for transfers between devices, swap_word(): return lax.all_to_all(parts, 'word', 0, 0)  39.1 us
    ppermute x18, waiting for transfers between devices, hop_x(): lax.ppermute(array, 'author', [(i, (i + 2 * k) % 8) for i in range(8)])  28 us
    ppermute x8, starting transfers between devices, hop_core(): return lax.ppermute(array, 'author', [(i, i ^ 1) for i in range(8)])  27.8 us
    ppermute x18, starting transfers between devices, hop_x(): lax.ppermute(array, 'author', [(i, (i + 2 * k) % 8) for i in range(8)])  27.4 us
    pallas_call x4, Pallas kernels, kernel_call(): pl.pallas_call(kernel, out_shape=out, in_specs=specs, out_specs=pl.BlockS...  26.7 us
  transfers between devices with their start and end apart: 43, of which 33 were waited for; matrix products, arithmetic and copies ran while one was open for 2% of the time, Pallas kernels for 10%

profile of v4, /device:TPU:1, one launch (start us, length us, event | category | flops | bytes accessed | tf_op | source)
XLA Modules:
  0.0 412.8 jit_solution(18087751875838782554)
XLA Ops:
  9.1 5.9 %product.2 = bf16[4096,256]{1,0:T(8,128)(2,1)S(1)} custom-call(s32[128]{0:T(128)S(1)} %bitcast.86, s32[128]{0:T(128)S(1)} %compare_select_fusion.4.dst_ids, s32[1]{0:T(128)} %bitcast.77.count, bf16[128,128,128]{2,1,0:T(8,128)(2,1)} %bitcast.90, bf16[16384,256]{1,0:T(8,128)(2,1)} %given.1), custom_call_target="tpu_custom_call" | custom-call | flops 2147483648 | bytes 20971520 | tf_op jit(solution)/shard_map/product/pallas_call | solution.py:117
  15.0 35.0 %all_to_all.20.p = bf16[16,256,256]{2,1,0:T(8,128)(2,1)} all-to-all(bf16[16,256,256]{2,1,0:T(8,128)(2,1)S(1)} %bitcast.85), channel_id=1, replica_groups=mesh['author'=8,'word'=16] {'word'}, dimensions={0} | all-to-all | bytes 4194304 | tf_op jit(solution)/shard_map/all_to_all | solution.py:371
  54.0 3.8 all-to-all-start.1
  57.9 25.2 %all-to-all-done.1 = bf16[16,256,256]{2,1,0:T(8,128)(2,1)S(1)} async-done(((bf16[16,256,256]{2,1,0:T(8,128)(2,1)}), bf16[16,256,256]{2,1,0:T(8,128)(2,1)S(1)}, u32[]{:S(2)}, u32[]{:S(2)}) %all-to-all-start.1) | async-done | bytes 2097184 | tf_op jit(solution)/shard_map/all_to_all | solution.py:371
  83.1 6.8 %product_t.2 = bf16[16384,256]{1,0:T(8,128)(2,1)} custom-call(s32[128]{0:T(128)S(1)} %bitcast.88, s32[128]{0:T(128)S(1)} %compare_select_fusion.3.dst_ids, s32[1]{0:T(128)} %bitcast.78.count, bf16[128,128,128]{2,1,0:T(8,128)(2,1)} %bitcast.91, bf16[4096,256]{1,0:T(8,128)(2,1)S(1)} %bitcast.81), custom_call_target="tpu_custom_call" | custom-call | flops 2147483648 | bytes 20971520 | tf_op jit(solution)/shard_map/product_t/pallas_call | solution.py:117
  90.0 3.0 gram_short.2
  94.0 5.8 %collective-permute-start = (f32[128,256]{1,0:T(8,128)S(1)}, f32[128,256]{1,0:T(8,128)S(1)}, u32[]{:S(2)}, u32[]{:S(2)}) collective-permute-start(f32[128,256]{1,0:T(8,128)S(1)} %dynamic-slice_bitcast_fusion.3), channel_id=1, source_target_pairs={{0,16},{16,0},{32,48},{48,32},{64,80},{80,64},{96,112},{112,96},{1... | collective-permute-start | bytes 393224 | tf_op jit(solution)/shard_map/ppermute | solution.py:227
  107.1 4.1 collective-permute-done.2
  111.1 4.9 %collective-permute-done.1 = f32[128,256]{1,0:T(8,128)S(1)} collective-permute-done((f32[128,256]{1,0:T(8,128)S(1)}, f32[128,256]{1,0:T(8,128)S(1)}, u32[]{:S(2)}, u32[]{:S(2)}) %collective-permute-start.1) | collective-permute-done | bytes 131104 | tf_op jit(solution)/shard_map/ppermute | solution.py:231
  119.1 12.3 %whitener.4 = f32[256,256]{1,0:T(8,128)} custom-call(f32[256,256]{1,0:T(8,128)} %fusion.g_ref), custom_call_target="tpu_custom_call" | custom-call | flops 1000000000 | bytes 40000000 | tf_op jit(solution)/shard_map/whitener/pallas_call | solution.py:355
  131.4 21.0 %reduce-scatter.3.cloned.1.call-done = bf16[2048,256]{1,0:T(8,128)(2,1)} async-done(((bf16[16384,256]{1,0:T(8,128)(2,1)}), bf16[2048,256]{1,0:T(8,128)(2,1)}) %reduce-scatter.3.cloned.1.call-update) | async-done | bytes 1048592 | tf_op jit(solution)/shard_map/reduce_scatter | solution.py:399
  152.4 3.0 fusion.7
  183.6 3.5 collective-permute-done.16
  188.2 6.0 %collective-permute-start.18 = (f32[128,256]{1,0:T(8,128)S(1)}, f32[128,256]{1,0:T(8,128)S(1)}, u32[]{:S(2)}, u32[]{:S(2)}) collective-permute-start(f32[128,256]{1,0:T(8,128)S(1)} %bitcast.104), channel_id=1, source_target_pairs={{0,16},{16,0},{32,48},{48,32},{64,80},{80,64},{96,112},{112,96},{1... | collective-permute-start | bytes 393224 | tf_op jit(solution)/shard_map/ppermute | solution.py:227
  195.9 9.8 %all-gather.2.cloned.1.call-done.given = bf16[16384,256]{1,0:T(8,128)(2,1)} async-done(((bf16[2048,256]{1,0:T(8,128)(2,1)}), bf16[16384,256]{1,0:T(8,128)(2,1)}) %all-gather.2.cloned.1.call-update) | async-done | bytes 8388624 | tf_op jit(solution)/shard_map/all_gather | solution.py:404
  205.8 7.2 %product.3 = bf16[4096,256]{1,0:T(8,128)(2,1)} custom-call(s32[128]{0:T(128)S(1)} %bitcast.87, s32[128]{0:T(128)S(1)} %compare_select_fusion.4.dst_ids, s32[1]{0:T(128)} %bitcast.79.count, bf16[128,128,128]{2,1,0:T(8,128)(2,1)} %bitcast.92, bf16[16384,256]{1,0:T(8,128)(2,1)} %all-gather.2.cloned.1.call-done.given), custom_call_target="tpu_custom_call" | custom-call | flops 2147483648 | bytes 20971520 | tf_op jit(solution)/shard_map/product/pallas_call | solution.py:117
  213.0 7.2 %all-to-all-start.2 = ((bf16[16,256,256]{2,1,0:T(8,128)(2,1)}), bf16[16,256,256]{2,1,0:T(8,128)(2,1)}, u32[]{:S(2)}, u32[]{:S(2)}) async-start(bf16[16,256,256]{2,1,0:T(8,128)(2,1)} %bitcast.23), calls=%async_computation.3 | async-start | bytes 4194304 | tf_op jit(solution)/shard_map/all_to_all | solution.py:371
  220.2 12.3 %whitener.5.factor = f32[256,256]{1,0:T(8,128)} custom-call(f32[256,256]{1,0:T(8,128)} %fusion.1.g_ref), custom_call_target="tpu_custom_call" | custom-call | flops 1000000000 | bytes 40000000 | tf_op jit(solution)/shard_map/whitener/pallas_call | solution.py:355
  232.5 14.0 %all-to-all-done.2.parts = bf16[16,256,256]{2,1,0:T(8,128)(2,1)} async-done(((bf16[16,256,256]{2,1,0:T(8,128)(2,1)}), bf16[16,256,256]{2,1,0:T(8,128)(2,1)}, u32[]{:S(2)}, u32[]{:S(2)}) %all-to-all-start.2) | async-done | bytes 2097184 | tf_op jit(solution)/shard_map/all_to_all | solution.py:371
  250.3 29.9 %all_to_all.21 = bf16[16,256,256]{2,1,0:T(8,128)(2,1)S(1)} all-to-all(bf16[16,256,256]{2,1,0:T(8,128)(2,1)} %copy-done.3), channel_id=1, replica_groups=mesh['author'=8,'word'=16] {'word'}, dimensions={0} | all-to-all | bytes 4194304 | tf_op jit(solution)/shard_map/all_to_all | solution.py:371
  280.1 6.8 %product_t.3 = bf16[16384,256]{1,0:T(8,128)(2,1)} custom-call(s32[128]{0:T(128)S(1)} %bitcast.89, s32[128]{0:T(128)S(1)} %compare_select_fusion.3.dst_ids, s32[1]{0:T(128)} %bitcast.80.count, bf16[128,128,128]{2,1,0:T(8,128)(2,1)} %bitcast.93, bf16[4096,256]{1,0:T(8,128)(2,1)S(1)} %bitcast.83), custom_call_target="tpu_custom_call" | custom-call | flops 2147483648 | bytes 20971520 | tf_op jit(solution)/shard_map/product_t/pallas_call | solution.py:117
  287.0 3.0 gram_short.3
  290.9 4.9 %collective-permute-start.19 = (f32[128,256]{1,0:T(8,128)S(1)}, f32[128,256]{1,0:T(8,128)S(1)}, u32[]{:S(2)}, u32[]{:S(2)}) collective-permute-start(f32[128,256]{1,0:T(8,128)S(1)} %dynamic-slice_bitcast_fusion.1), channel_id=1, source_target_pairs={{0,16},{16,0},{32,48},{48,32},{64,80},{80,64},{96,112},{112,96},{1... | collective-permute-start | bytes 393224 | tf_op jit(solution)/shard_map/ppermute | solution.py:227
  297.8 4.0 collective-permute-start.21
  308.2 4.0 collective-permute-done.20
  315.2 12.3 %whitener.6 = f32[256,256]{1,0:T(8,128)} custom-call(f32[256,256]{1,0:T(8,128)} %fusion.2.g_ref), custom_call_target="tpu_custom_call" | custom-call | flops 1000000000 | bytes 40000000 | tf_op jit(solution)/shard_map/whitener/pallas_call | solution.py:355
  327.5 21.1 %reduce-scatter.5.cloned.1.call-done = bf16[2048,256]{1,0:T(8,128)(2,1)} async-done(((bf16[16384,256]{1,0:T(8,128)(2,1)}), bf16[2048,256]{1,0:T(8,128)(2,1)}) %reduce-scatter.5.cloned.1.call-update) | async-done | bytes 1048592 | tf_op jit(solution)/shard_map/reduce_scatter | solution.py:399
  364.5 3.3 collective-permute-done.28
  371.8 3.2 collective-permute-done.31
  378.3 3.3 collective-permute-done.35
  382.3 7.1 %collective-permute-start.37 = (f32[128,256]{1,0:T(8,128)S(1)}, f32[128,256]{1,0:T(8,128)S(1)}, u32[]{:S(2)}, u32[]{:S(2)}) collective-permute-start(f32[128,256]{1,0:T(8,128)S(1)} %bitcast.102), channel_id=1, source_target_pairs={{0,16},{16,0},{32,48},{48,32},{64,80},{80,64},{96,112},{112,96},{1... | collective-permute-start | bytes 393224 | tf_op jit(solution)/shard_map/ppermute | solution.py:227
  391.0 12.3 %whitener.7 = f32[256,256]{1,0:T(8,128)} custom-call(f32[256,256]{1,0:T(8,128)} %fusion.3.g_ref), custom_call_target="tpu_custom_call" | custom-call | flops 1000000000 | bytes 40000000 | tf_op jit(solution)/shard_map/whitener/pallas_call | solution.py:355
  (126 shorter events, 92.1 us)
Async XLA Ops:
  54.0 29.1 %all-to-all-start.1 = ((bf16[16,256,256]{2,1,0:T(8,128)(2,1)}), bf16[16,256,256]{2,1,0:T(8,128)(2,1)S(1)}, u32[]{:S(2)}, u32[]{:S(2)}) async-start(bf16[16,256,256]{2,1,0:T(8,128)(2,1)} %copy-done.2), calls=%async_computation.1 | async-start | bytes 4194304 | tf_op jit(solution)/shard_map/all_to_all | solution.py:371
  57.8 94.6 %reduce-scatter.3.cloned.1.call-start = ((), (), s32[]{:S(2)}) async-start(), calls=%async_computation.6 | async-start | bytes 9437184 | tf_op jit(solution)/shard_map/reduce_scatter | solution.py:399
  90.0 115.8 %all-gather.2.cloned.1.call-start = ((), (), s32[]{:S(2)}) async-start(), calls=%async_computation.7 | async-start | bytes 9437184 | tf_op jit(solution)/shard_map/all_gather | solution.py:404
  94.0 6.7 %collective-permute-start = (f32[128,256]{1,0:T(8,128)S(1)}, f32[128,256]{1,0:T(8,128)S(1)}, u32[]{:S(2)}, u32[]{:S(2)}) collective-permute-start(f32[128,256]{1,0:T(8,128)S(1)} %dynamic-slice_bitcast_fusion.3), channel_id=1, source_target_pairs={{0,16},{16,0},{32,48},{48,32},{64,80},{80,64},{96,112},{112,96},{1... | collective-permute-start | bytes 393224 | tf_op jit(solution)/shard_map/ppermute | solution.py:227
  101.7 9.5 %collective-permute-start.2 = (f32[128,256]{1,0:T(8,128)S(1)}, f32[128,256]{1,0:T(8,128)S(1)}, u32[]{:S(2)}, u32[]{:S(2)}) collective-permute-start(f32[128,256]{1,0:T(8,128)S(1)} %bitcast_add_fusion.3), channel_id=1, source_target_pairs={{0,32},{16,48},{32,64},{48,80},{64,96},{80,112},{96,0},{112,16},{1... | collective-permute-start | bytes 393224 | tf_op jit(solution)/shard_map/ppermute | solution.py:231
  104.2 7.0 %collective-permute-start.3 = (f32[128,256]{1,0:T(8,128)S(1)}, f32[128,256]{1,0:T(8,128)S(1)}, u32[]{:S(2)}, u32[]{:S(2)}) collective-permute-start(f32[128,256]{1,0:T(8,128)S(1)} %bitcast_add_fusion.3), channel_id=1, source_target_pairs={{0,96},{16,112},{32,0},{48,16},{64,32},{80,48},{96,64},{112,80},{1... | collective-permute-start | bytes 393224 | tf_op jit(solution)/shard_map/ppermute | solution.py:231
  105.8 10.2 %collective-permute-start.1 = (f32[128,256]{1,0:T(8,128)S(1)}, f32[128,256]{1,0:T(8,128)S(1)}, u32[]{:S(2)}, u32[]{:S(2)}) collective-permute-start(f32[128,256]{1,0:T(8,128)S(1)} %bitcast_add_fusion.3), channel_id=1, source_target_pairs={{0,64},{16,80},{32,96},{48,112},{64,0},{80,16},{96,32},{112,48},{1... | collective-permute-start | bytes 393224 | tf_op jit(solution)/shard_map/ppermute | solution.py:231
  159.6 4.3 %collective-permute-start.6 = (f32[32,256]{1,0:T(8,128)S(1)}, f32[32,256]{1,0:T(8,128)S(1)}, u32[]{:S(2)}, u32[]{:S(2)}) collective-permute-start(f32[32,256]{1,0:T(8,128)S(1)} %get-tuple-element.18), channel_id=1, source_target_pairs={{0,64},{16,80},{32,96},{48,112},{64,0},{80,16},{96,32},{112,48},{1... | collective-permute-start | bytes 98312 | tf_op jit(solution)/shard_map/ppermute | solution.py:231
  161.0 4.3 %collective-permute-start.7 = (f32[32,256]{1,0:T(8,128)S(1)}, f32[32,256]{1,0:T(8,128)S(1)}, u32[]{:S(2)}, u32[]{:S(2)}) collective-permute-start(f32[32,256]{1,0:T(8,128)S(1)} %get-tuple-element.17), channel_id=1, source_target_pairs={{0,32},{16,48},{32,64},{48,80},{64,96},{80,112},{96,0},{112,16},{1... | collective-permute-start | bytes 98312 | tf_op jit(solution)/shard_map/ppermute | solution.py:231
  161.0 4.3 %collective-permute-start.8 = (f32[32,256]{1,0:T(8,128)S(1)}, f32[32,256]{1,0:T(8,128)S(1)}, u32[]{:S(2)}, u32[]{:S(2)}) collective-permute-start(f32[32,256]{1,0:T(8,128)S(1)} %get-tuple-element.16), channel_id=1, source_target_pairs={{0,96},{16,112},{32,0},{48,16},{64,32},{80,48},{96,64},{112,80},{1... | collective-permute-start | bytes 98312 | tf_op jit(solution)/shard_map/ppermute | solution.py:231
  165.3 4.4 %collective-permute-start.10 = (f32[32,256]{1,0:T(8,128)S(1)}, f32[32,256]{1,0:T(8,128)S(1)}, u32[]{:S(2)}, u32[]{:S(2)}) collective-permute-start(f32[32,256]{1,0:T(8,128)S(1)} %fusion.5), channel_id=1, source_target_pairs={{0,4},{1,5},{2,6},{3,7},{4,8},{5,9},{6,10},{7,11},{8,12},{9,13},{1... | collective-permute-start | bytes 98312 | tf_op jit(solution)/shard_map/ppermute | solution.py:235
  165.4 4.4 %collective-permute-start.11 = (f32[32,256]{1,0:T(8,128)S(1)}, f32[32,256]{1,0:T(8,128)S(1)}, u32[]{:S(2)}, u32[]{:S(2)}) collective-permute-start(f32[32,256]{1,0:T(8,128)S(1)} %fusion.5), channel_id=1, source_target_pairs={{0,12},{1,13},{2,14},{3,15},{4,0},{5,1},{6,2},{7,3},{8,4},{9,5},{1... | collective-permute-start | bytes 98312 | tf_op jit(solution)/shard_map/ppermute | solution.py:235
  168.0 4.3 %collective-permute-start.9 = (f32[32,256]{1,0:T(8,128)S(1)}, f32[32,256]{1,0:T(8,128)S(1)}, u32[]{:S(2)}, u32[]{:S(2)}) collective-permute-start(f32[32,256]{1,0:T(8,128)S(1)} %fusion.5), channel_id=1, source_target_pairs={{0,8},{1,9},{2,10},{3,11},{4,12},{5,13},{6,14},{7,15},{8,0},{9,1},... | collective-permute-start | bytes 98312 | tf_op jit(solution)/shard_map/ppermute | solution.py:235
  172.3 4.4 %collective-permute-start.13 = (f32[32,256]{1,0:T(8,128)S(1)}, f32[32,256]{1,0:T(8,128)S(1)}, u32[]{:S(2)}, u32[]{:S(2)}) collective-permute-start(f32[32,256]{1,0:T(8,128)S(1)} %add_add_fusion.5), channel_id=1, source_target_pairs={{0,1},{1,2},{2,3},{3,0},{4,5},{5,6},{6,7},{7,4},{8,9},{9,10},{10,1... | collective-permute-start | bytes 98312 | tf_op jit(solution)/shard_map/ppermute | solution.py:239
  175.1 4.3 %collective-permute-start.12 = (f32[32,256]{1,0:T(8,128)S(1)}, f32[32,256]{1,0:T(8,128)S(1)}, u32[]{:S(2)}, u32[]{:S(2)}) collective-permute-start(f32[32,256]{1,0:T(8,128)S(1)} %add_add_fusion.5), channel_id=1, source_target_pairs={{0,2},{1,3},{2,0},{3,1},{4,6},{5,7},{6,4},{7,5},{8,10},{9,11},{10,... | collective-permute-start | bytes 98312 | tf_op jit(solution)/shard_map/ppermute | solution.py:239
  179.4 4.2 %collective-permute-start.17 = (f32[32,256]{1,0:T(8,128)S(1)}, f32[32,256]{1,0:T(8,128)S(1)}, u32[]{:S(2)}, u32[]{:S(2)}) collective-permute-start(f32[32,256]{1,0:T(8,128)S(1)} %add_add_fusion.4), channel_id=1, source_target_pairs={{0,96},{16,112},{32,0},{48,16},{64,32},{80,48},{96,64},{112,80},{1... | collective-permute-start | bytes 98312 | tf_op jit(solution)/shard_map/ppermute | solution.py:231
  182.1 5.0 %collective-permute-start.16 = (f32[32,256]{1,0:T(8,128)S(1)}, f32[32,256]{1,0:T(8,128)S(1)}, u32[]{:S(2)}, u32[]{:S(2)}) collective-permute-start(f32[32,256]{1,0:T(8,128)S(1)} %add_add_fusion.4), channel_id=1, source_target_pairs={{0,64},{16,80},{32,96},{48,112},{64,0},{80,16},{96,32},{112,48},{1... | collective-permute-start | bytes 98312 | tf_op jit(solution)/shard_map/ppermute | solution.py:231
  182.1 5.4 %collective-permute-start.15 = (f32[32,256]{1,0:T(8,128)S(1)}, f32[32,256]{1,0:T(8,128)S(1)}, u32[]{:S(2)}, u32[]{:S(2)}) collective-permute-start(f32[32,256]{1,0:T(8,128)S(1)} %add_add_fusion.4), channel_id=1, source_target_pairs={{0,32},{16,48},{32,64},{48,80},{64,96},{80,112},{96,0},{112,16},{1... | collective-permute-start | bytes 98312 | tf_op jit(solution)/shard_map/ppermute | solution.py:231
  188.2 7.0 %collective-permute-start.18 = (f32[128,256]{1,0:T(8,128)S(1)}, f32[128,256]{1,0:T(8,128)S(1)}, u32[]{:S(2)}, u32[]{:S(2)}) collective-permute-start(f32[128,256]{1,0:T(8,128)S(1)} %bitcast.104), channel_id=1, source_target_pairs={{0,16},{16,0},{32,48},{48,32},{64,80},{80,64},{96,112},{112,96},{1... | collective-permute-start | bytes 393224 | tf_op jit(solution)/shard_map/ppermute | solution.py:227
  213.0 33.5 %all-to-all-start.2 = ((bf16[16,256,256]{2,1,0:T(8,128)(2,1)}), bf16[16,256,256]{2,1,0:T(8,128)(2,1)}, u32[]{:S(2)}, u32[]{:S(2)}) async-start(bf16[16,256,256]{2,1,0:T(8,128)(2,1)} %bitcast.23), calls=%async_computation.3 | async-start | bytes 4194304 | tf_op jit(solution)/shard_map/all_to_all | solution.py:371
  220.2 128.4 %reduce-scatter.5.cloned.1.call-start = ((), (), s32[]{:S(2)}) async-start(), calls=%async_computation.8 | async-start | bytes 9437184 | tf_op jit(solution)/shard_map/reduce_scatter | solution.py:399
  290.9 5.9 %collective-permute-start.19 = (f32[128,256]{1,0:T(8,128)S(1)}, f32[128,256]{1,0:T(8,128)S(1)}, u32[]{:S(2)}, u32[]{:S(2)}) collective-permute-start(f32[128,256]{1,0:T(8,128)S(1)} %dynamic-slice_bitcast_fusion.1), channel_id=1, source_target_pairs={{0,16},{16,0},{32,48},{48,32},{64,80},{80,64},{96,112},{112,96},{1... | collective-permute-start | bytes 393224 | tf_op jit(solution)/shard_map/ppermute | solution.py:227
  297.8 8.3 %collective-permute-start.21 = (f32[128,256]{1,0:T(8,128)S(1)}, f32[128,256]{1,0:T(8,128)S(1)}, u32[]{:S(2)}, u32[]{:S(2)}) collective-permute-start(f32[128,256]{1,0:T(8,128)S(1)} %bitcast_add_fusion.1), channel_id=1, source_target_pairs={{0,32},{16,48},{32,64},{48,80},{64,96},{80,112},{96,0},{112,16},{1... | collective-permute-start | bytes 393224 | tf_op jit(solution)/shard_map/ppermute | solution.py:231
  301.8 6.5 %collective-permute-start.22 = (f32[128,256]{1,0:T(8,128)S(1)}, f32[128,256]{1,0:T(8,128)S(1)}, u32[]{:S(2)}, u32[]{:S(2)}) collective-permute-start(f32[128,256]{1,0:T(8,128)S(1)} %bitcast_add_fusion.1), channel_id=1, source_target_pairs={{0,96},{16,112},{32,0},{48,16},{64,32},{80,48},{96,64},{112,80},{1... | collective-permute-start | bytes 393224 | tf_op jit(solution)/shard_map/ppermute | solution.py:231
  301.8 10.5 %collective-permute-start.20 = (f32[128,256]{1,0:T(8,128)S(1)}, f32[128,256]{1,0:T(8,128)S(1)}, u32[]{:S(2)}, u32[]{:S(2)}) collective-permute-start(f32[128,256]{1,0:T(8,128)S(1)} %bitcast_add_fusion.1), channel_id=1, source_target_pairs={{0,64},{16,80},{32,96},{48,112},{64,0},{80,16},{96,32},{112,48},{1... | collective-permute-start | bytes 393224 | tf_op jit(solution)/shard_map/ppermute | solution.py:231
  354.0 5.2 %collective-permute-start.25 = (f32[32,256]{1,0:T(8,128)S(1)}, f32[32,256]{1,0:T(8,128)S(1)}, u32[]{:S(2)}, u32[]{:S(2)}) collective-permute-start(f32[32,256]{1,0:T(8,128)S(1)} %get-tuple-element.15), channel_id=1, source_target_pairs={{0,64},{16,80},{32,96},{48,112},{64,0},{80,16},{96,32},{112,48},{1... | collective-permute-start | bytes 98312 | tf_op jit(solution)/shard_map/ppermute | solution.py:231
  363.2 4.6 %collective-permute-start.28 = (f32[32,256]{1,0:T(8,128)S(1)}, f32[32,256]{1,0:T(8,128)S(1)}, u32[]{:S(2)}, u32[]{:S(2)}) collective-permute-start(f32[32,256]{1,0:T(8,128)S(1)} %fusion.4), channel_id=1, source_target_pairs={{0,8},{1,9},{2,10},{3,11},{4,12},{5,13},{6,14},{7,15},{8,0},{9,1},... | collective-permute-start | bytes 98312 | tf_op jit(solution)/shard_map/ppermute | solution.py:235
  367.8 4.0 collective-permute-start.32
  370.5 4.5 %collective-permute-start.31 = (f32[32,256]{1,0:T(8,128)S(1)}, f32[32,256]{1,0:T(8,128)S(1)}, u32[]{:S(2)}, u32[]{:S(2)}) collective-permute-start(f32[32,256]{1,0:T(8,128)S(1)} %add_add_fusion.3), channel_id=1, source_target_pairs={{0,2},{1,3},{2,0},{3,1},{4,6},{5,7},{6,4},{7,5},{8,10},{9,11},{10,... | collective-permute-start | bytes 98312 | tf_op jit(solution)/shard_map/ppermute | solution.py:239
  377.3 4.3 %collective-permute-start.35 = (f32[32,256]{1,0:T(8,128)S(1)}, f32[32,256]{1,0:T(8,128)S(1)}, u32[]{:S(2)}, u32[]{:S(2)}) collective-permute-start(f32[32,256]{1,0:T(8,128)S(1)} %add_add_fusion.2), channel_id=1, source_target_pairs={{0,64},{16,80},{32,96},{48,112},{64,0},{80,16},{96,32},{112,48},{1... | collective-permute-start | bytes 98312 | tf_op jit(solution)/shard_map/ppermute | solution.py:231
  377.3 4.3 %collective-permute-start.34 = (f32[32,256]{1,0:T(8,128)S(1)}, f32[32,256]{1,0:T(8,128)S(1)}, u32[]{:S(2)}, u32[]{:S(2)}) collective-permute-start(f32[32,256]{1,0:T(8,128)S(1)} %add_add_fusion.2), channel_id=1, source_target_pairs={{0,32},{16,48},{32,64},{48,80},{64,96},{80,112},{96,0},{112,16},{1... | collective-permute-start | bytes 98312 | tf_op jit(solution)/shard_map/ppermute | solution.py:231
  382.3 8.1 %collective-permute-start.37 = (f32[128,256]{1,0:T(8,128)S(1)}, f32[128,256]{1,0:T(8,128)S(1)}, u32[]{:S(2)}, u32[]{:S(2)}) collective-permute-start(f32[128,256]{1,0:T(8,128)S(1)} %bitcast.102), channel_id=1, source_target_pairs={{0,16},{16,0},{32,48},{48,32},{64,80},{80,64},{96,112},{112,96},{1... | collective-permute-start | bytes 393224 | tf_op jit(solution)/shard_map/ppermute | solution.py:227
  (19 other events, 120.4 us)
Sparse Core Ops, SparseCore 0:
  90.1 62.3 reduce-scatter.2
  155.6 50.1 all-gather.1
  287.1 61.4 reduce-scatter.4

commit v5 on v4

--- a/solution.py
+++ b/solution.py
@@ -274,6 +274,15 @@
     ring = jnp.stack([part] + [hop_x(part, k) for k in (1, 2, 3)])
     half = jnp.take(ring, (x - jnp.arange(4)) % 4, axis=0).reshape(half.shape)
     return join_core(half, core)
+
+
+def sum_all_swap(gram):
+    axes = ("author", "word")
+    devices = lax.axis_size(axes)
+    parts = lax.all_to_all(gram.reshape(devices, -1, gram.shape[1]), axes, 0, 0)
+    rows = jnp.sum(parts, axis=0)
+    rows = jnp.broadcast_to(rows[None], (devices,) + rows.shape)
+    return lax.all_to_all(rows, axes, 0, 0).reshape(gram.shape)
 
 
 def eliminate(strips):
@@ -342,9 +351,13 @@
         dot = lambda u, v, d: lax.dot_general(u, v, (((d,), (0,)), ((), ())), precision=HIGH, preferred_element_type=jnp.float32)
         left = dot(inverse, left, 1)
         right = dot(inverse, right, 1)
-        rest = jnp.where(lane >= (at + 1) * BLOCK, left, 0.0)
-        s_ref[...] -= dot(rest, left, 0)
-        y_ref[...] -= dot(rest, right, 0)
+
+        @pl.when(at + 1 < n // BLOCK)
+        def _():
+            rest = jnp.where(lane >= (at + 1) * BLOCK, left, 0.0)
+            s_ref[...] -= dot(rest, left, 0)
+            y_ref[...] -= dot(rest, right, 0)
+
         y_ref[rows, :] = right
         return carry
     lax.fori_loop(0, n // BLOCK, stage, 0)
@@ -399,7 +412,7 @@
         z = long(lax.psum_scatter(terms, "author", scatter_dimension=0, tiled=True))
         author_factor = whitener(sum_author(gram_short(y_rows)) / authors)
         z = apply_t(z, author_factor)
-        gram = sum_all(gram_of(z)) / words
+        gram = (sum_all if turn + 1 < ITERS else sum_all_swap)(gram_of(z)) / words
         if turn + 1 < ITERS:
             wide = lax.all_gather(short(z), "author", axis=0, tiled=True)
             wide, gram = lax.optimization_barrier((wide, gram))

time: 416 us -> 412 us (level)
  blocking collectives: 64.8 us -> 82.5 us
  starting transfers between devices: 79.9 us -> 67.5 us
  waiting for transfers between devices: 142 us -> 136 us
    all_to_all x0 -> x1, blocking collectives: none -> 17.3 us  [sum_all_swap(): parts = lax.all_to_all(gram.reshape(devices, -1, gram.shape[1]), axes, 0, 0)]
    all_to_all x0 -> x1, waiting for transfers between devices: none -> 10.3 us  [sum_all_swap(): return lax.all_to_all(rows, axes, 0, 0).reshape(gram.shape)]
    ppermute x8 -> x6, starting transfers between devices: 27.8 us -> 21.3 us  [hop_core(): return lax.ppermute(array, 'author', [(i, i ^ 1) for i in range(8)])]
    ppermute x18 -> x12, waiting for transfers between devices: 28 us -> 22 us  [hop_x(): lax.ppermute(array, 'author', [(i, (i + 2 * k) % 8) for i in range(8)])]
    all_to_all x0 -> x1, starting transfers between devices: none -> 4.2 us  [sum_all_swap(): return lax.all_to_all(rows, axes, 0, 0).reshape(gram.shape)]
    ppermute x18 -> x12, starting transfers between devices: 27.4 us -> 25.1 us  [hop_x(): lax.ppermute(array, 'author', [(i, (i + 2 * k) % 8) for i in range(8)])]
  transfers between devices with their start and end apart: 43 -> 30, of which waited for: 33 -> 26; matrix products, arithmetic and copies ran while one was open for 2% -> 2% of each run, Pallas kernels for 10% -> 10%
where the time goes in v5:
time: 412 us
  waiting for transfers between devices  136 us (33%)
  Pallas kernels  84.8 us (21%)
  blocking collectives  82.5 us (20%)
  starting transfers between devices  67.5 us (16%)
  between operations  14.7 us (4%)
  matrix products  12.6 us (3%)
  local copies, waits for them, and re-layouts  7.79 us (2%)
  other arithmetic  5.2 us (1%)
    all_to_all x2, blocking collectives, swap_word(): return lax.all_to_all(parts, 'word', 0, 0)  65.2 us
    pallas_call x4, Pallas kernels, whitener(): pl.pallas_call(whiten_kernel, out_shape=jax.ShapeDtypeStruct(gram.shape,...  46.9 us
    reduce_scatter x2, waiting for transfers between devices, shards(): z = long(lax.psum_scatter(terms, 'author', scatter_dimension=0, tiled=True))  41.1 us
    all_to_all x2, waiting for transfers between devices, swap_word(): return lax.all_to_all(parts, 'word', 0, 0)  38.9 us
    pallas_call x4, Pallas kernels, kernel_call(): pl.pallas_call(kernel, out_shape=out, in_specs=specs, out_specs=pl.BlockS...  26.8 us
    ppermute x12, starting transfers between devices, hop_x(): lax.ppermute(array, 'author', [(i, (i + 2 * k) % 8) for i in range(8)])  25.1 us
    ppermute x12, waiting for transfers between devices, hop_x(): lax.ppermute(array, 'author', [(i, (i + 2 * k) % 8) for i in range(8)])  22 us
    ppermute x6, starting transfers between devices, hop_core(): return lax.ppermute(array, 'author', [(i, i ^ 1) for i in range(8)])  21.3 us
  transfers between devices with their start and end apart: 30, of which 26 were waited for; matrix products, arithmetic and copies ran while one was open for 2% of the time, Pallas kernels for 10%

profile of v5, /device:TPU:1, one launch (start us, length us, event | category | flops | bytes accessed | tf_op | source)
XLA Modules:
  0.0 411.5 jit_solution(14105044556386111939)
XLA Ops:
  9.1 5.9 %product.2 = bf16[4096,256]{1,0:T(8,128)(2,1)S(1)} custom-call(s32[128]{0:T(128)S(1)} %bitcast.68, s32[128]{0:T(128)S(1)} %compare_select_fusion.7.dst_ids, s32[1]{0:T(128)} %bitcast.59.count, bf16[128,128,128]{2,1,0:T(8,128)(2,1)} %bitcast.72, bf16[16384,256]{1,0:T(8,128)(2,1)} %given.1), custom_call_target="tpu_custom_call" | custom-call | flops 2147483648 | bytes 20971520 | tf_op jit(solution)/shard_map/product/pallas_call | solution.py:117
  15.0 35.1 %all_to_all.30.p = bf16[16,256,256]{2,1,0:T(8,128)(2,1)} all-to-all(bf16[16,256,256]{2,1,0:T(8,128)(2,1)S(1)} %bitcast.67), channel_id=1, replica_groups=mesh['author'=8,'word'=16] {'word'}, dimensions={0} | all-to-all | bytes 4194304 | tf_op jit(solution)/shard_map/all_to_all | solution.py:384
  54.2 3.8 all-to-all-start.1
  58.1 25.1 %all-to-all-done.1 = bf16[16,256,256]{2,1,0:T(8,128)(2,1)S(1)} async-done(((bf16[16,256,256]{2,1,0:T(8,128)(2,1)}), bf16[16,256,256]{2,1,0:T(8,128)(2,1)S(1)}, u32[]{:S(2)}, u32[]{:S(2)}) %all-to-all-start.1) | async-done | bytes 2097184 | tf_op jit(solution)/shard_map/all_to_all | solution.py:384
  83.2 6.8 %product_t.2 = bf16[16384,256]{1,0:T(8,128)(2,1)} custom-call(s32[128]{0:T(128)S(1)} %bitcast.70, s32[128]{0:T(128)S(1)} %compare_select_fusion.6.dst_ids, s32[1]{0:T(128)} %bitcast.60.count, bf16[128,128,128]{2,1,0:T(8,128)(2,1)} %bitcast.73, bf16[4096,256]{1,0:T(8,128)(2,1)S(1)} %bitcast.63), custom_call_target="tpu_custom_call" | custom-call | flops 2147483648 | bytes 20971520 | tf_op jit(solution)/shard_map/product_t/pallas_call | solution.py:117
  90.2 3.0 gram_short.2
  94.1 6.4 %collective-permute-start = (f32[128,256]{1,0:T(8,128)S(1)}, f32[128,256]{1,0:T(8,128)S(1)}, u32[]{:S(2)}, u32[]{:S(2)}) collective-permute-start(f32[128,256]{1,0:T(8,128)S(1)} %dynamic-slice_bitcast_fusion.2), channel_id=1, source_target_pairs={{0,16},{16,0},{32,48},{48,32},{64,80},{80,64},{96,112},{112,96},{1... | collective-permute-start | bytes 393224 | tf_op jit(solution)/shard_map/ppermute | solution.py:227
  113.5 4.5 %collective-permute-done.1 = f32[128,256]{1,0:T(8,128)S(1)} collective-permute-done((f32[128,256]{1,0:T(8,128)S(1)}, f32[128,256]{1,0:T(8,128)S(1)}, u32[]{:S(2)}, u32[]{:S(2)}) %collective-permute-start.1) | collective-permute-done | bytes 131104 | tf_op jit(solution)/shard_map/ppermute | solution.py:231
  120.8 11.7 %whitener.4 = f32[256,256]{1,0:T(8,128)} custom-call(f32[256,256]{1,0:T(8,128)} %fusion.g_ref), custom_call_target="tpu_custom_call" | custom-call | flops 1000000000 | bytes 40000000 | tf_op jit(solution)/shard_map/whitener/pallas_call | solution.py:368
  132.6 20.7 %reduce-scatter.3.cloned.1.call-done = bf16[2048,256]{1,0:T(8,128)(2,1)} async-done(((bf16[16384,256]{1,0:T(8,128)(2,1)}), bf16[2048,256]{1,0:T(8,128)(2,1)}) %reduce-scatter.3.cloned.1.call-update) | async-done | bytes 1048592 | tf_op jit(solution)/shard_map/reduce_scatter | solution.py:412
  153.3 3.0 fusion.7
  184.5 3.4 collective-permute-done.16
  189.0 6.1 %collective-permute-start.18 = (f32[128,256]{1,0:T(8,128)S(1)}, f32[128,256]{1,0:T(8,128)S(1)}, u32[]{:S(2)}, u32[]{:S(2)}) collective-permute-start(f32[128,256]{1,0:T(8,128)S(1)} %bitcast_select_fusion), channel_id=1, source_target_pairs={{0,16},{16,0},{32,48},{48,32},{64,80},{80,64},{96,112},{112,96},{1... | collective-permute-start | bytes 393224 | tf_op jit(solution)/shard_map/ppermute | solution.py:227
  196.8 9.8 %all-gather.2.cloned.1.call-done.given = bf16[16384,256]{1,0:T(8,128)(2,1)} async-done(((bf16[2048,256]{1,0:T(8,128)(2,1)}), bf16[16384,256]{1,0:T(8,128)(2,1)}) %all-gather.2.cloned.1.call-update) | async-done | bytes 8388624 | tf_op jit(solution)/shard_map/all_gather | solution.py:417
  206.6 7.3 %product.3 = bf16[4096,256]{1,0:T(8,128)(2,1)} custom-call(s32[128]{0:T(128)S(1)} %bitcast.69, s32[128]{0:T(128)S(1)} %compare_select_fusion.7.dst_ids, s32[1]{0:T(128)} %bitcast.61.count, bf16[128,128,128]{2,1,0:T(8,128)(2,1)} %bitcast.74, bf16[16384,256]{1,0:T(8,128)(2,1)} %all-gather.2.cloned.1.call-done.given), custom_call_target="tpu_custom_call" | custom-call | flops 2147483648 | bytes 20971520 | tf_op jit(solution)/shard_map/product/pallas_call | solution.py:117
  213.9 7.4 %all-to-all-start.2 = ((bf16[16,256,256]{2,1,0:T(8,128)(2,1)}), bf16[16,256,256]{2,1,0:T(8,128)(2,1)}, u32[]{:S(2)}, u32[]{:S(2)}) async-start(bf16[16,256,256]{2,1,0:T(8,128)(2,1)} %bitcast.24), calls=%async_computation.3 | async-start | bytes 4194304 | tf_op jit(solution)/shard_map/all_to_all | solution.py:384
  221.3 11.7 %whitener.5.factor = f32[256,256]{1,0:T(8,128)} custom-call(f32[256,256]{1,0:T(8,128)} %fusion.1.g_ref), custom_call_target="tpu_custom_call" | custom-call | flops 1000000000 | bytes 40000000 | tf_op jit(solution)/shard_map/whitener/pallas_call | solution.py:368
  233.0 13.8 %all-to-all-done.2.parts = bf16[16,256,256]{2,1,0:T(8,128)(2,1)} async-done(((bf16[16,256,256]{2,1,0:T(8,128)(2,1)}), bf16[16,256,256]{2,1,0:T(8,128)(2,1)}, u32[]{:S(2)}, u32[]{:S(2)}) %all-to-all-start.2) | async-done | bytes 2097184 | tf_op jit(solution)/shard_map/all_to_all | solution.py:384
  250.6 30.1 %all_to_all.31 = bf16[16,256,256]{2,1,0:T(8,128)(2,1)S(1)} all-to-all(bf16[16,256,256]{2,1,0:T(8,128)(2,1)} %copy-done.3), channel_id=1, replica_groups=mesh['author'=8,'word'=16] {'word'}, dimensions={0} | all-to-all | bytes 4194304 | tf_op jit(solution)/shard_map/all_to_all | solution.py:384
  280.7 6.8 %product_t.3 = bf16[16384,256]{1,0:T(8,128)(2,1)} custom-call(s32[128]{0:T(128)S(1)} %bitcast.71, s32[128]{0:T(128)S(1)} %compare_select_fusion.6.dst_ids, s32[1]{0:T(128)} %bitcast.62.count, bf16[128,128,128]{2,1,0:T(8,128)(2,1)} %bitcast.75, bf16[4096,256]{1,0:T(8,128)(2,1)S(1)} %bitcast.65), custom_call_target="tpu_custom_call" | custom-call | flops 2147483648 | bytes 20971520 | tf_op jit(solution)/shard_map/product_t/pallas_call | solution.py:117
  287.6 3.0 gram_short.3
  291.5 5.3 %collective-permute-start.19 = (f32[128,256]{1,0:T(8,128)S(1)}, f32[128,256]{1,0:T(8,128)S(1)}, u32[]{:S(2)}, u32[]{:S(2)}) collective-permute-start(f32[128,256]{1,0:T(8,128)S(1)} %dynamic-slice_bitcast_fusion), channel_id=1, source_target_pairs={{0,16},{16,0},{32,48},{48,32},{64,80},{80,64},{96,112},{112,96},{1... | collective-permute-start | bytes 393224 | tf_op jit(solution)/shard_map/ppermute | solution.py:227
  298.7 4.0 collective-permute-start.21
  304.2 4.5 %collective-permute-start.20 = (f32[128,256]{1,0:T(8,128)S(1)}, f32[128,256]{1,0:T(8,128)S(1)}, u32[]{:S(2)}, u32[]{:S(2)}) collective-permute-start(f32[128,256]{1,0:T(8,128)S(1)} %bitcast_add_fusion), channel_id=1, source_target_pairs={{0,64},{16,80},{32,96},{48,112},{64,0},{80,16},{96,32},{112,48},{1... | collective-permute-start | bytes 393224 | tf_op jit(solution)/shard_map/ppermute | solution.py:231
  308.7 3.4 collective-permute-done.22
  312.0 4.5 %collective-permute-done.20 = f32[128,256]{1,0:T(8,128)S(1)} collective-permute-done((f32[128,256]{1,0:T(8,128)S(1)}, f32[128,256]{1,0:T(8,128)S(1)}, u32[]{:S(2)}, u32[]{:S(2)}) %collective-permute-start.20) | collective-permute-done | bytes 131104 | tf_op jit(solution)/shard_map/ppermute | solution.py:231
  319.6 11.7 %whitener.6 = f32[256,256]{1,0:T(8,128)} custom-call(f32[256,256]{1,0:T(8,128)} %fusion.2.g_ref), custom_call_target="tpu_custom_call" | custom-call | flops 1000000000 | bytes 40000000 | tf_op jit(solution)/shard_map/whitener/pallas_call | solution.py:368
  331.3 20.3 %reduce-scatter.5.cloned.1.call-done = bf16[2048,256]{1,0:T(8,128)(2,1)} async-done(((bf16[16384,256]{1,0:T(8,128)(2,1)}), bf16[2048,256]{1,0:T(8,128)(2,1)}) %reduce-scatter.5.cloned.1.call-update) | async-done | bytes 1048592 | tf_op jit(solution)/shard_map/reduce_scatter | solution.py:412
  355.7 17.3 %all_to_all.32 = f32[128,2,256]{2,1,0:T(2,128)S(1)} all-to-all(f32[128,2,256]{2,1,0:T(2,128)S(1)} %reshape.100), channel_id=1, replica_groups=mesh['author'=8,'word'=16] {'author','word'}, dimensions={0} | all-to-all | bytes 524288 | tf_op jit(solution)/shard_map/all_to_all | solution.py:282
  373.9 4.2 %all-to-all-start.5 = ((f32[128,2,256]{2,1,0:T(2,128)}), f32[128,2,256]{2,1,0:T(2,128)S(1)}, u32[]{:S(2)}, u32[]{:S(2)}) async-start(f32[128,2,256]{2,1,0:T(2,128)} %broadcast_in_dim.35), calls=%async_computation.7 | async-start | bytes 524288 | tf_op jit(solution)/shard_map/all_to_all | solution.py:285
  379.1 10.3 %all-to-all-done.5 = f32[128,2,256]{2,1,0:T(2,128)S(1)} async-done(((f32[128,2,256]{2,1,0:T(2,128)}), f32[128,2,256]{2,1,0:T(2,128)S(1)}, u32[]{:S(2)}, u32[]{:S(2)}) %all-to-all-start.5) | async-done | bytes 262176 | tf_op jit(solution)/shard_map/all_to_all | solution.py:285
  390.4 11.7 %whitener.7 = f32[256,256]{1,0:T(8,128)} custom-call(f32[256,256]{1,0:T(8,128)} %div.29.g_ref), custom_call_target="tpu_custom_call" | custom-call | flops 1000000000 | bytes 40000000 | tf_op jit(solution)/shard_map/whitener/pallas_call | solution.py:368
  (98 shorter events, 74.0 us)
Async XLA Ops:
  54.2 29.0 %copy-start.6 = (s32[1,1,128]{2,1,0:T(1,128)S(1)}, s32[1,1,128]{2,1,0:T(1,128)}, u32[]{:S(2)}) copy-start(s32[1,1,128]{2,1,0:T(1,128)} %param.6) | copy-start | bytes 1540
  54.2 29.0 %all-to-all-start.1 = ((bf16[16,256,256]{2,1,0:T(8,128)(2,1)}), bf16[16,256,256]{2,1,0:T(8,128)(2,1)S(1)}, u32[]{:S(2)}, u32[]{:S(2)}) async-start(bf16[16,256,256]{2,1,0:T(8,128)(2,1)} %copy-done.2), calls=%async_computation.1 | async-start | bytes 4194304 | tf_op jit(solution)/shard_map/all_to_all | solution.py:384
  58.0 95.3 %reduce-scatter.3.cloned.1.call-start = ((), (), s32[]{:S(2)}) async-start(), calls=%async_computation.8 | async-start | bytes 9437184 | tf_op jit(solution)/shard_map/reduce_scatter | solution.py:412
  90.1 116.5 %all-gather.2.cloned.1.call-start = ((), (), s32[]{:S(2)}) async-start(), calls=%async_computation.9 | async-start | bytes 9437184 | tf_op jit(solution)/shard_map/all_gather | solution.py:417
  94.1 7.3 %collective-permute-start = (f32[128,256]{1,0:T(8,128)S(1)}, f32[128,256]{1,0:T(8,128)S(1)}, u32[]{:S(2)}, u32[]{:S(2)}) collective-permute-start(f32[128,256]{1,0:T(8,128)S(1)} %dynamic-slice_bitcast_fusion.2), channel_id=1, source_target_pairs={{0,16},{16,0},{32,48},{48,32},{64,80},{80,64},{96,112},{112,96},{1... | collective-permute-start | bytes 393224 | tf_op jit(solution)/shard_map/ppermute | solution.py:227
  102.4 10.0 %collective-permute-start.2 = (f32[128,256]{1,0:T(8,128)S(1)}, f32[128,256]{1,0:T(8,128)S(1)}, u32[]{:S(2)}, u32[]{:S(2)}) collective-permute-start(f32[128,256]{1,0:T(8,128)S(1)} %bitcast_add_fusion.2), channel_id=1, source_target_pairs={{0,32},{16,48},{32,64},{48,80},{64,96},{80,112},{96,0},{112,16},{1... | collective-permute-start | bytes 393224 | tf_op jit(solution)/shard_map/ppermute | solution.py:231
  104.4 9.1 %collective-permute-start.3 = (f32[128,256]{1,0:T(8,128)S(1)}, f32[128,256]{1,0:T(8,128)S(1)}, u32[]{:S(2)}, u32[]{:S(2)}) collective-permute-start(f32[128,256]{1,0:T(8,128)S(1)} %bitcast_add_fusion.2), channel_id=1, source_target_pairs={{0,96},{16,112},{32,0},{48,16},{64,32},{80,48},{96,64},{112,80},{1... | collective-permute-start | bytes 393224 | tf_op jit(solution)/shard_map/ppermute | solution.py:231
  107.3 10.8 %collective-permute-start.1 = (f32[128,256]{1,0:T(8,128)S(1)}, f32[128,256]{1,0:T(8,128)S(1)}, u32[]{:S(2)}, u32[]{:S(2)}) collective-permute-start(f32[128,256]{1,0:T(8,128)S(1)} %bitcast_add_fusion.2), channel_id=1, source_target_pairs={{0,64},{16,80},{32,96},{48,112},{64,0},{80,16},{96,32},{112,48},{1... | collective-permute-start | bytes 393224 | tf_op jit(solution)/shard_map/ppermute | solution.py:231
  118.1 2.0 collective-permute-start.4
  158.2 2.3 collective-permute-start.5
  160.5 4.3 %collective-permute-start.6 = (f32[32,256]{1,0:T(8,128)S(1)}, f32[32,256]{1,0:T(8,128)S(1)}, u32[]{:S(2)}, u32[]{:S(2)}) collective-permute-start(f32[32,256]{1,0:T(8,128)S(1)} %get-tuple-element.14), channel_id=1, source_target_pairs={{0,64},{16,80},{32,96},{48,112},{64,0},{80,16},{96,32},{112,48},{1... | collective-permute-start | bytes 98312 | tf_op jit(solution)/shard_map/ppermute | solution.py:231
  161.8 4.3 %collective-permute-start.7 = (f32[32,256]{1,0:T(8,128)S(1)}, f32[32,256]{1,0:T(8,128)S(1)}, u32[]{:S(2)}, u32[]{:S(2)}) collective-permute-start(f32[32,256]{1,0:T(8,128)S(1)} %get-tuple-element.13), channel_id=1, source_target_pairs={{0,32},{16,48},{32,64},{48,80},{64,96},{80,112},{96,0},{112,16},{1... | collective-permute-start | bytes 98312 | tf_op jit(solution)/shard_map/ppermute | solution.py:231
  161.8 4.3 %collective-permute-start.8 = (f32[32,256]{1,0:T(8,128)S(1)}, f32[32,256]{1,0:T(8,128)S(1)}, u32[]{:S(2)}, u32[]{:S(2)}) collective-permute-start(f32[32,256]{1,0:T(8,128)S(1)} %get-tuple-element.12), channel_id=1, source_target_pairs={{0,96},{16,112},{32,0},{48,16},{64,32},{80,48},{96,64},{112,80},{1... | collective-permute-start | bytes 98312 | tf_op jit(solution)/shard_map/ppermute | solution.py:231
  166.1 4.4 %collective-permute-start.10 = (f32[32,256]{1,0:T(8,128)S(1)}, f32[32,256]{1,0:T(8,128)S(1)}, u32[]{:S(2)}, u32[]{:S(2)}) collective-permute-start(f32[32,256]{1,0:T(8,128)S(1)} %fusion.3), channel_id=1, source_target_pairs={{0,4},{1,5},{2,6},{3,7},{4,8},{5,9},{6,10},{7,11},{8,12},{9,13},{1... | collective-permute-start | bytes 98312 | tf_op jit(solution)/shard_map/ppermute | solution.py:235
  166.3 4.3 %collective-permute-start.11 = (f32[32,256]{1,0:T(8,128)S(1)}, f32[32,256]{1,0:T(8,128)S(1)}, u32[]{:S(2)}, u32[]{:S(2)}) collective-permute-start(f32[32,256]{1,0:T(8,128)S(1)} %fusion.3), channel_id=1, source_target_pairs={{0,12},{1,13},{2,14},{3,15},{4,0},{5,1},{6,2},{7,3},{8,4},{9,5},{1... | collective-permute-start | bytes 98312 | tf_op jit(solution)/shard_map/ppermute | solution.py:235
  168.9 4.3 %collective-permute-start.9 = (f32[32,256]{1,0:T(8,128)S(1)}, f32[32,256]{1,0:T(8,128)S(1)}, u32[]{:S(2)}, u32[]{:S(2)}) collective-permute-start(f32[32,256]{1,0:T(8,128)S(1)} %fusion.3), channel_id=1, source_target_pairs={{0,8},{1,9},{2,10},{3,11},{4,12},{5,13},{6,14},{7,15},{8,0},{9,1},... | collective-permute-start | bytes 98312 | tf_op jit(solution)/shard_map/ppermute | solution.py:235
  173.2 4.4 %collective-permute-start.13 = (f32[32,256]{1,0:T(8,128)S(1)}, f32[32,256]{1,0:T(8,128)S(1)}, u32[]{:S(2)}, u32[]{:S(2)}) collective-permute-start(f32[32,256]{1,0:T(8,128)S(1)} %add_add_fusion.3), channel_id=1, source_target_pairs={{0,1},{1,2},{2,3},{3,0},{4,5},{5,6},{6,7},{7,4},{8,9},{9,10},{10,1... | collective-permute-start | bytes 98312 | tf_op jit(solution)/shard_map/ppermute | solution.py:239
  173.5 4.2 %collective-permute-start.14 = (f32[32,256]{1,0:T(8,128)S(1)}, f32[32,256]{1,0:T(8,128)S(1)}, u32[]{:S(2)}, u32[]{:S(2)}) collective-permute-start(f32[32,256]{1,0:T(8,128)S(1)} %add_add_fusion.3), channel_id=1, source_target_pairs={{0,3},{1,0},{2,1},{3,2},{4,7},{5,4},{6,5},{7,6},{8,11},{9,8},{10,9... | collective-permute-start | bytes 98312 | tf_op jit(solution)/shard_map/ppermute | solution.py:239
  175.9 4.3 %collective-permute-start.12 = (f32[32,256]{1,0:T(8,128)S(1)}, f32[32,256]{1,0:T(8,128)S(1)}, u32[]{:S(2)}, u32[]{:S(2)}) collective-permute-start(f32[32,256]{1,0:T(8,128)S(1)} %add_add_fusion.3), channel_id=1, source_target_pairs={{0,2},{1,3},{2,0},{3,1},{4,6},{5,7},{6,4},{7,5},{8,10},{9,11},{10,... | collective-permute-start | bytes 98312 | tf_op jit(solution)/shard_map/ppermute | solution.py:239
  180.3 4.2 %collective-permute-start.17 = (f32[32,256]{1,0:T(8,128)S(1)}, f32[32,256]{1,0:T(8,128)S(1)}, u32[]{:S(2)}, u32[]{:S(2)}) collective-permute-start(f32[32,256]{1,0:T(8,128)S(1)} %add_add_fusion.2), channel_id=1, source_target_pairs={{0,96},{16,112},{32,0},{48,16},{64,32},{80,48},{96,64},{112,80},{1... | collective-permute-start | bytes 98312 | tf_op jit(solution)/shard_map/ppermute | solution.py:231
  182.9 5.0 %collective-permute-start.16 = (f32[32,256]{1,0:T(8,128)S(1)}, f32[32,256]{1,0:T(8,128)S(1)}, u32[]{:S(2)}, u32[]{:S(2)}) collective-permute-start(f32[32,256]{1,0:T(8,128)S(1)} %add_add_fusion.2), channel_id=1, source_target_pairs={{0,64},{16,80},{32,96},{48,112},{64,0},{80,16},{96,32},{112,48},{1... | collective-permute-start | bytes 98312 | tf_op jit(solution)/shard_map/ppermute | solution.py:231
  182.9 5.4 %collective-permute-start.15 = (f32[32,256]{1,0:T(8,128)S(1)}, f32[32,256]{1,0:T(8,128)S(1)}, u32[]{:S(2)}, u32[]{:S(2)}) collective-permute-start(f32[32,256]{1,0:T(8,128)S(1)} %add_add_fusion.2), channel_id=1, source_target_pairs={{0,32},{16,48},{32,64},{48,80},{64,96},{80,112},{96,0},{112,16},{1... | collective-permute-start | bytes 98312 | tf_op jit(solution)/shard_map/ppermute | solution.py:231
  189.0 7.1 %collective-permute-start.18 = (f32[128,256]{1,0:T(8,128)S(1)}, f32[128,256]{1,0:T(8,128)S(1)}, u32[]{:S(2)}, u32[]{:S(2)}) collective-permute-start(f32[128,256]{1,0:T(8,128)S(1)} %bitcast_select_fusion), channel_id=1, source_target_pairs={{0,16},{16,0},{32,48},{48,32},{64,80},{80,64},{96,112},{112,96},{1... | collective-permute-start | bytes 393224 | tf_op jit(solution)/shard_map/ppermute | solution.py:227
  213.9 33.0 %all-to-all-start.2 = ((bf16[16,256,256]{2,1,0:T(8,128)(2,1)}), bf16[16,256,256]{2,1,0:T(8,128)(2,1)}, u32[]{:S(2)}, u32[]{:S(2)}) async-start(bf16[16,256,256]{2,1,0:T(8,128)(2,1)} %bitcast.24), calls=%async_computation.3 | async-start | bytes 4194304 | tf_op jit(solution)/shard_map/all_to_all | solution.py:384
  221.3 130.4 %reduce-scatter.5.cloned.1.call-start = ((), (), s32[]{:S(2)}) async-start(), calls=%async_computation.10 | async-start | bytes 9437184 | tf_op jit(solution)/shard_map/reduce_scatter | solution.py:412
  291.5 6.3 %collective-permute-start.19 = (f32[128,256]{1,0:T(8,128)S(1)}, f32[128,256]{1,0:T(8,128)S(1)}, u32[]{:S(2)}, u32[]{:S(2)}) collective-permute-start(f32[128,256]{1,0:T(8,128)S(1)} %dynamic-slice_bitcast_fusion), channel_id=1, source_target_pairs={{0,16},{16,0},{32,48},{48,32},{64,80},{80,64},{96,112},{112,96},{1... | collective-permute-start | bytes 393224 | tf_op jit(solution)/shard_map/ppermute | solution.py:227
  298.7 9.9 %collective-permute-start.21 = (f32[128,256]{1,0:T(8,128)S(1)}, f32[128,256]{1,0:T(8,128)S(1)}, u32[]{:S(2)}, u32[]{:S(2)}) collective-permute-start(f32[128,256]{1,0:T(8,128)S(1)} %bitcast_add_fusion), channel_id=1, source_target_pairs={{0,32},{16,48},{32,64},{48,80},{64,96},{80,112},{96,0},{112,16},{1... | collective-permute-start | bytes 393224 | tf_op jit(solution)/shard_map/ppermute | solution.py:231
  302.8 9.3 %collective-permute-start.22 = (f32[128,256]{1,0:T(8,128)S(1)}, f32[128,256]{1,0:T(8,128)S(1)}, u32[]{:S(2)}, u32[]{:S(2)}) collective-permute-start(f32[128,256]{1,0:T(8,128)S(1)} %bitcast_add_fusion), channel_id=1, source_target_pairs={{0,96},{16,112},{32,0},{48,16},{64,32},{80,48},{96,64},{112,80},{1... | collective-permute-start | bytes 393224 | tf_op jit(solution)/shard_map/ppermute | solution.py:231
  304.2 12.4 %collective-permute-start.20 = (f32[128,256]{1,0:T(8,128)S(1)}, f32[128,256]{1,0:T(8,128)S(1)}, u32[]{:S(2)}, u32[]{:S(2)}) collective-permute-start(f32[128,256]{1,0:T(8,128)S(1)} %bitcast_add_fusion), channel_id=1, source_target_pairs={{0,64},{16,80},{32,96},{48,112},{64,0},{80,16},{96,32},{112,48},{1... | collective-permute-start | bytes 393224 | tf_op jit(solution)/shard_map/ppermute | solution.py:231
  316.6 2.2 collective-permute-start.23
  355.5 22.6 %copy-start.7 = (f32[256,256]{1,0:T(8,128)S(1)}, f32[256,256]{1,0:T(8,128)}, u32[]{:S(2)}) copy-start(f32[256,256]{1,0:T(8,128)} %whitener.6) | copy-start | bytes 786436
  373.9 15.5 %all-to-all-start.5 = ((f32[128,2,256]{2,1,0:T(2,128)}), f32[128,2,256]{2,1,0:T(2,128)S(1)}, u32[]{:S(2)}, u32[]{:S(2)}) async-start(f32[128,2,256]{2,1,0:T(2,128)} %broadcast_in_dim.35), calls=%async_computation.7 | async-start | bytes 524288 | tf_op jit(solution)/shard_map/all_to_all | solution.py:285
  (6 other events, 21.0 us)
Sparse Core Ops, SparseCore 0:
  90.2 63.0 reduce-scatter.2
  156.4 50.1 all-gather.1
  287.7 63.9 reduce-scatter.4
